TPU v7x, 128 devices: a whole 4x4x4 slice. The times are simulated.
128 devices in a mesh: grp: 4 (over x_lo, core), dp: 32 (over y, x_hi, z).
Axes of the slice: x: 4 (x_hi: 2, x_lo: 2; x = x_hi * 2 + x_lo), y: 4, z: 4, core: 2. Of those that a mesh axis runs over, the one named last changes fastest.
Arguments:
- photo_vectors_raw: bfloat16 [131072, 768], P(('grp', 'dp')), may hold values from -0.21875 to 0.21875
- sentence_vectors_raw: bfloat16 [131072, 768], P(('grp', 'dp')), may hold values from -0.21875 to 0.21875
- companion_index: int32 [128, 1024], P(('grp', 'dp')), may hold values from 0 to 1023, each once within a row
- exponent_of_sharpness: float32 [1], replicated, may hold values from 1 to 2.3
- affinity_offset: float32 [1], replicated, may hold values from -4 to -1
Outputs:
- image_grad: float32 [131072, 768], P(('grp', 'dp'))
- text_grad: float32 [131072, 768], P(('grp', 'dp'))
Inputs may be any that keep to these rules, and one draw needn't show every extreme that they name: Each row of companion_index is a permutation of 0 to 1023.
All inputs are finite; a program needn't handle non-finite values.
Results may differ from a plain program's by a relative error of at most 0.0055.
Values may be sent and summed in bfloat16 or wider, within the bound.
No kernel may reach another device: no remote copies, remote signals or barrier semaphores. Data moves between devices by JAX's collectives and lax.ppermute only.
A program may use at most 128 MiB of HBM per device.

v0:
```python
import jax
import jax.numpy as jnp
from jax import lax
from jax.sharding import PartitionSpec as P


def passed_along(x, axis, by):
    devices = lax.axis_size(axis)
    return lax.ppermute(x, axis, [(i, (i + by) % devices) for i in range(devices)])


def unit_rows(raw):
    values = raw.astype(jnp.float32)
    inverse_norm = lax.rsqrt(jnp.sum(values * values, -1, keepdims=True) + 1e-06)
    return (values * inverse_norm, inverse_norm)


def gradient_panel(picture_rows, caption_rows, matching_pairs, sharpness_factor, block_distance):
    score_matrix = (
        sharpness_factor * jnp.dot(picture_rows, caption_rows.T, preferred_element_type=jnp.float32)
        + block_distance
    )
    if matching_pairs is None:
        target_labels = -1.0
    else:
        target_labels = jnp.where(matching_pairs, 1.0, -1.0)
    return (
        sharpness_factor * -target_labels * jax.nn.sigmoid(-target_labels * score_matrix)
    ).astype(jnp.bfloat16)


def unit_backward(grad, unit, inverse_norm):
    return inverse_norm * (grad - unit * jnp.sum(unit * grad, -1, keepdims=True))


def similarity_entries(left, right):
    return jnp.dot(left, right, preferred_element_type=jnp.float32)


def local(
    photo_vectors_raw, sentence_vectors_raw, companion_index, exponent_of_sharpness, affinity_offset
):
    sharpness_factor = jnp.exp(exponent_of_sharpness[0])
    block_distance = affinity_offset[0]
    image_unit, image_norm = unit_rows(photo_vectors_raw)
    text_unit, text_norm = unit_rows(sentence_vectors_raw)
    picture_rows = image_unit.astype(jnp.bfloat16)
    caption_rows = text_unit.astype(jnp.bfloat16)
    row_count = picture_rows.shape[0]
    matching_pairs = companion_index[0][:, None] == jnp.arange(row_count, dtype=jnp.int32)[None, :]
    local_panel = gradient_panel(
        picture_rows, caption_rows, matching_pairs, sharpness_factor, block_distance
    )
    preceding_block = passed_along(caption_rows, ("grp", "dp"), 1)
    following_block = passed_along(caption_rows, ("grp", "dp"), -1)
    leftward_panel = gradient_panel(
        picture_rows, preceding_block, None, sharpness_factor, block_distance
    )
    rightward_panel = gradient_panel(
        picture_rows, following_block, None, sharpness_factor, block_distance
    )
    image_part = (
        similarity_entries(local_panel, caption_rows)
        + similarity_entries(leftward_panel, preceding_block)
        + similarity_entries(rightward_panel, following_block)
    )
    text_left = similarity_entries(leftward_panel.T, picture_rows)
    text_right = similarity_entries(rightward_panel.T, picture_rows)
    from_after = passed_along(text_left.astype(jnp.bfloat16), ("grp", "dp"), -1).astype(
        text_left.dtype
    )
    from_before = passed_along(text_right.astype(jnp.bfloat16), ("grp", "dp"), 1).astype(
        text_right.dtype
    )
    text_part = similarity_entries(local_panel.T, picture_rows) + from_after + from_before
    image_grad = unit_backward(image_part, image_unit, image_norm)
    text_grad = unit_backward(text_part, text_unit, text_norm)
    return (image_grad, text_grad)


def solution(mesh):
    placed = (P(("grp", "dp"), None), P(("grp", "dp"), None), P(("grp", "dp"), None), P(), P())
    return jax.shard_map(
        local,
        mesh=mesh,
        in_specs=placed,
        out_specs=(P(("grp", "dp"), None), P(("grp", "dp"), None)),
        check_vma=False,
    )
```

profile of v0, /device:TPU:102, one launch (start us, length us, event | category | flops | bytes accessed | tf_op | source)
XLA Modules:
  0.0 112.0 jit_solution(16418463847990067407)
XLA Ops:
  0.6 1.7 %copy.8 = bf16[1024,768]{0,1:T(8,128)(2,1)S(1)} copy(bf16[1024,768]{1,0:T(8,128)(2,1)} %param.6) | data formatting | bytes 3145728 | tf_op args[1]
  2.4 0.4 fusion.13
  2.7 1.6 %fusion.2 = bf16[1024,768]{0,1:T(8,128)(2,1)} fusion(bf16[1024,768]{0,1:T(8,128)(2,1)S(1)} %copy.8, f32[1024]{0:T(1024)S(1)} %add_rsqrt_fusion), kind=kLoop, calls=%fused_computation.8 | loop fusion | flops 2359296 | bytes 3149824 | tf_op jit(solution)/shard_map/convert_element_type | solution.py:48
  4.3 0.4 collective-permute-start.1
  4.7 6.1 %collective-permute-start = (bf16[1024,768]{0,1:T(8,128)(2,1)}, bf16[1024,768]{0,1:T(8,128)(2,1)}, u32[]{:S(2)}, u32[]{:S(2)}) collective-permute-start(bf16[1024,768]{0,1:T(8,128)(2,1)} %fusion.2), channel_id=1, source_target_pairs={{0,1},{1,2},{2,3},{3,4},{4,5},{5,6},{6,7},{7,8},{8,9},{9,10},{10,1... | collective-permute-start | bytes 4718600 | tf_op jit(solution)/shard_map/ppermute | solution.py:9
  10.8 1.7 %copy.7 = bf16[1024,768]{0,1:T(8,128)(2,1)S(1)} copy(bf16[1024,768]{1,0:T(8,128)(2,1)} %param.5) | data formatting | bytes 3145728 | tf_op args[0]
  12.5 0.4 fusion.9
  14.3 4.9 %multiply_convert_fusion.2 = bf16[1024,1024]{1,0:T(8,128)(2,1)S(1)} fusion(bf16[1024,768]{0,1:T(8,128)(2,1)} %fusion.2, f32[]{:T(128)} %bitcast.15, s32[1024]{0:T(1024)S(1)} %bitcast.18, f32[]{:T(128)} %bitcast, bf16[1024,768]{0,1:T(8,128)(2,1)S(1)} %copy.7, f32[1024]{0:T(1024)S(1)} %add_rsqrt_fusion.1), kind=kOutput, calls=%fused_computation.2 | convolution fusion | flops 1625554944 | bytes 5251080 | tf_op jit(solution)/shard_map/dot_general | solution.py:20
  19.2 4.0 %fusion.21 = f32[1024,768]{0,1:T(8,128)S(1)} fusion(bf16[1024,1024]{1,0:T(8,128)(2,1)S(1)} %multiply_convert_fusion.2, bf16[1024,768]{0,1:T(8,128)(2,1)} %fusion.2), kind=kOutput, calls=%fused_computation.29 | convolution fusion | flops 1610612736 | bytes 6815744 | tf_op jit(solution)/shard_map/dot_general | solution.py:37
  23.2 22.1 %collective-permute-done.1 = bf16[1024,768]{0,1:T(8,128)(2,1)} collective-permute-done((bf16[1024,768]{0,1:T(8,128)(2,1)}, bf16[1024,768]{0,1:T(8,128)(2,1)}, u32[]{:S(2)}, u32[]{:S(2)}) %collective-permute-start.1) | collective-permute-done | bytes 1572896 | tf_op jit(solution)/shard_map/ppermute | solution.py:9
  45.2 4.0 %multiply_convert_fusion = bf16[1024,1024]{1,0:T(8,128)(2,1)S(1)} fusion(bf16[1024,768]{0,1:T(8,128)(2,1)} %collective-permute-done.1, f32[]{:T(128)} %bitcast.16, f32[]{:T(128)} %bitcast, bf16[1024,768]{0,1:T(8,128)(2,1)S(1)} %copy.7, f32[1024]{0:T(1024)S(1)} %add_rsqrt_fusion.1), kind=kOutput, calls=%fused_computation | convolution fusion | flops 1620312064 | bytes 5246984 | tf_op jit(solution)/shard_map/dot_general | solution.py:20
  49.2 3.0 %convolution_convert_fusion = bf16[1024,768]{0,1:T(8,128)(2,1)} fusion(bf16[1024,1024]{1,0:T(8,128)(2,1)S(1)} %multiply_convert_fusion, bf16[1024,768]{0,1:T(8,128)(2,1)S(1)} %copy.7, f32[1024]{0:T(1024)S(1)} %add_rsqrt_fusion.1), kind=kOutput, calls=%fused_computation.24 | convolution fusion | flops 1613758464 | bytes 5246976 | tf_op jit(solution)/shard_map/dot_general | solution.py:37
  52.3 4.0 %multiply_convert_fusion.1 = bf16[1024,1024]{1,0:T(8,128)(2,1)S(1)} fusion(bf16[1024,768]{0,1:T(8,128)(2,1)} %collective-permute-done, f32[]{:T(128)} %bitcast.17, f32[]{:T(128)} %bitcast, bf16[1024,768]{0,1:T(8,128)(2,1)S(1)} %copy.7, f32[1024]{0:T(1024)S(1)} %add_rsqrt_fusion.1), kind=kOutput, calls=%fused_computation.1 | convolution fusion | flops 1620312064 | bytes 5246984 | tf_op jit(solution)/shard_map/dot_general | solution.py:20
  56.3 3.0 %convolution_convert_fusion.1 = bf16[1024,768]{0,1:T(8,128)(2,1)} fusion(bf16[1024,1024]{1,0:T(8,128)(2,1)S(1)} %multiply_convert_fusion.1, bf16[1024,768]{0,1:T(8,128)(2,1)S(1)} %copy.7, f32[1024]{0:T(1024)S(1)} %add_rsqrt_fusion.1), kind=kOutput, calls=%fused_computation.25 | convolution fusion | flops 1613758464 | bytes 5246976 | tf_op jit(solution)/shard_map/dot_general | solution.py:37
  59.2 2.0 %collective-permute-start.2 = (bf16[1024,768]{0,1:T(8,128)(2,1)}, bf16[1024,768]{0,1:T(8,128)(2,1)}, u32[]{:S(2)}, u32[]{:S(2)}) collective-permute-start(bf16[1024,768]{0,1:T(8,128)(2,1)} %convolution_convert_fusion.1), channel_id=1, source_target_pairs={{0,127},{1,0},{2,1},{3,2},{4,3},{5,4},{6,5},{7,6},{8,7},{9,8},{10,... | collective-permute-start | bytes 4718600 | tf_op jit(solution)/shard_map/ppermute | solution.py:9
  61.2 3.2 %fusion.22 = f32[1024,768]{0,1:T(8,128)S(1)} fusion(bf16[1024,1024]{1,0:T(8,128)(2,1)S(1)} %multiply_convert_fusion.1, bf16[1024,768]{0,1:T(8,128)(2,1)} %collective-permute-done), kind=kOutput, calls=%fused_computation.30 | convolution fusion | flops 1610612736 | bytes 6815744 | tf_op jit(solution)/shard_map/dot_general | solution.py:37
  64.5 3.6 %fusion.6 = (f32[1024]{0:T(1024)S(1)}, f32[1024,768]{0,1:T(8,128)S(1)}) fusion(bf16[1024,768]{0,1:T(8,128)(2,1)S(1)} %copy.7, f32[1024]{0:T(1024)S(1)} %add_rsqrt_fusion.1, bf16[1024,1024]{1,0:T(8,128)(2,1)S(1)} %multiply_convert_fusion, bf16[1024,768]{0,1:T(8,128)(2,1)} %collective-permute-done.1, f32[1024,768]{0,1:T(8,128)S(1)} %fusion.21, ...), kind=kOutput, calls=%fused_computation.14 | convolution fusion | flops 1615330304 | bytes 14688256 | tf_op jit(solution)/shard_map/dot_general | solution.py:37
  68.1 2.3 %fusion.8 = f32[1024,768]{0,1:T(8,128)} fusion(f32[1024,768]{0,1:T(8,128)S(1)} %get-tuple-element.5, bf16[1024,768]{0,1:T(8,128)(2,1)S(1)} %copy.7, f32[1024]{0:T(1024)S(1)} %get-tuple-element.4, f32[1024]{0:T(1024)S(1)} %add_rsqrt_fusion.1), kind=kLoop, calls=%fused_computation.16 | loop fusion | flops 3932160 | bytes 7872512 | tf_op jit(solution)/shard_map/mul | solution.py:33
  70.4 3.5 %copy.11 = f32[1024,768]{1,0:T(8,128)} copy(f32[1024,768]{0,1:T(8,128)} %fusion.8) | data formatting | bytes 6291456
  73.9 13.9 %collective-permute-done.3 = bf16[1024,768]{0,1:T(8,128)(2,1)} collective-permute-done((bf16[1024,768]{0,1:T(8,128)(2,1)}, bf16[1024,768]{0,1:T(8,128)(2,1)}, u32[]{:S(2)}, u32[]{:S(2)}) %collective-permute-start.3) | collective-permute-done | bytes 1572896 | tf_op jit(solution)/shard_map/ppermute | solution.py:9
  87.8 11.5 %collective-permute-done.2 = bf16[1024,768]{0,1:T(8,128)(2,1)} collective-permute-done((bf16[1024,768]{0,1:T(8,128)(2,1)}, bf16[1024,768]{0,1:T(8,128)(2,1)}, u32[]{:S(2)}, u32[]{:S(2)}) %collective-permute-start.2) | collective-permute-done | bytes 1572896 | tf_op jit(solution)/shard_map/ppermute | solution.py:9
  99.3 4.7 %fusion.10 = (f32[1024]{0:T(1024)S(1)}, f32[1024,768]{0,1:T(8,128)S(1)}) fusion(bf16[1024,768]{0,1:T(8,128)(2,1)S(1)} %copy.8, f32[1024]{0:T(1024)S(1)} %add_rsqrt_fusion, bf16[1024,768]{0,1:T(8,128)(2,1)} %collective-permute-done.3, bf16[1024,768]{0,1:T(8,128)(2,1)} %collective-permute-done.2, bf16[1024,1024]{1,0:T(8,128)(2,1)} %copy-done.1, ...), kind=kOutput, calls=%fused_computation.18 | convolution fusion | flops 1619262464 | bytes 11546624 | tf_op jit(solution)/shard_map/dot_general | solution.py:37
  104.0 4.5 %fusion.12 = f32[1024,768]{0,1:T(8,128)} fusion(bf16[1024,768]{0,1:T(8,128)(2,1)S(1)} %copy.8, f32[1024]{0:T(1024)S(1)} %get-tuple-element.6, f32[1024]{0:T(1024)S(1)} %add_rsqrt_fusion, bf16[1024,768]{0,1:T(8,128)(2,1)} %collective-permute-done.3, f32[1024,768]{0,1:T(8,128)S(1)} %get-tuple-element.7, bf16[1024,768]{0,1:T(8,128)(2,1)} %collective-permute-done.2), kind=kLoop, calls=%fused_computation.20 | loop fusion | flops 7077888 | bytes 11018240 | tf_op jit(solution)/shard_map/mul | solution.py:33
  108.5 3.5 %copy.12 = f32[1024,768]{1,0:T(8,128)} copy(f32[1024,768]{0,1:T(8,128)} %fusion.12) | data formatting | bytes 6291456
  (8 shorter events, 0.0 us)
Async XLA Ops:
  4.3 10.0 %copy-start = (s32[1,1024]{1,0:T(1,128)S(1)}, s32[1,1024]{1,0:T(1,128)}, u32[]{:S(2)}) copy-start(s32[1,1024]{1,0:T(1,128)} %param.7) | copy-start | bytes 12292
  4.3 41.0 %collective-permute-start.1 = (bf16[1024,768]{0,1:T(8,128)(2,1)}, bf16[1024,768]{0,1:T(8,128)(2,1)}, u32[]{:S(2)}, u32[]{:S(2)}) collective-permute-start(bf16[1024,768]{0,1:T(8,128)(2,1)} %fusion.2), channel_id=1, source_target_pairs={{0,127},{1,0},{2,1},{3,2},{4,3},{5,4},{6,5},{7,6},{8,7},{9,8},{10,... | collective-permute-start | bytes 4718600 | tf_op jit(solution)/shard_map/ppermute | solution.py:9
  4.7 47.6 %collective-permute-start = (bf16[1024,768]{0,1:T(8,128)(2,1)}, bf16[1024,768]{0,1:T(8,128)(2,1)}, u32[]{:S(2)}, u32[]{:S(2)}) collective-permute-start(bf16[1024,768]{0,1:T(8,128)(2,1)} %fusion.2), channel_id=1, source_target_pairs={{0,1},{1,2},{2,3},{3,4},{4,5},{5,6},{6,7},{7,8},{8,9},{9,10},{10,1... | collective-permute-start | bytes 4718600 | tf_op jit(solution)/shard_map/ppermute | solution.py:9
  19.2 4.0 %copy-start.1 = (bf16[1024,1024]{1,0:T(8,128)(2,1)}, bf16[1024,1024]{1,0:T(8,128)(2,1)S(1)}, u32[]{:S(2)}) copy-start(bf16[1024,1024]{1,0:T(8,128)(2,1)S(1)} %multiply_convert_fusion.2) | copy-start | bytes 6291460
  52.3 35.6 %collective-permute-start.3 = (bf16[1024,768]{0,1:T(8,128)(2,1)}, bf16[1024,768]{0,1:T(8,128)(2,1)}, u32[]{:S(2)}, u32[]{:S(2)}) collective-permute-start(bf16[1024,768]{0,1:T(8,128)(2,1)} %convolution_convert_fusion), channel_id=1, source_target_pairs={{0,1},{1,2},{2,3},{3,4},{4,5},{5,6},{6,7},{7,8},{8,9},{9,10},{10,1... | collective-permute-start | bytes 4718600 | tf_op jit(solution)/shard_map/ppermute | solution.py:9
  59.2 40.1 %collective-permute-start.2 = (bf16[1024,768]{0,1:T(8,128)(2,1)}, bf16[1024,768]{0,1:T(8,128)(2,1)}, u32[]{:S(2)}, u32[]{:S(2)}) collective-permute-start(bf16[1024,768]{0,1:T(8,128)(2,1)} %convolution_convert_fusion.1), channel_id=1, source_target_pairs={{0,127},{1,0},{2,1},{3,2},{4,3},{5,4},{6,5},{7,6},{8,7},{9,8},{10,... | collective-permute-start | bytes 4718600 | tf_op jit(solution)/shard_map/ppermute | solution.py:9
where the time goes:
time: 112 us
  waiting for transfers between devices  47.5 us (42%)
  matrix products  34.3 us (31%)
  local copies, waits for them, and re-layouts  10.5 us (9%)
  other arithmetic  9.07 us (8%)
  starting transfers between devices  8.57 us (8%)
  between operations  2.08 us (2%)
    ppermute x4, waiting for transfers between devices, passed_along(): lax.ppermute(x, axis, [(i, (i + by) % devices) for i in range(devices)])  47.5 us
    dot_general x6, matrix products, similarity_entries(): return jnp.dot(left, right, preferred_element_type=jnp.float32)  21.5 us
    dot_general x3, matrix products, gradient_panel(): jnp.dot(picture_rows, caption_rows.T, preferred_element_type=jnp.float32)  12.8 us
    unnamed x8, local copies, waits for them, and re-layouts  10.5 us
    ppermute x4, starting transfers between devices, passed_along(): lax.ppermute(x, axis, [(i, (i + by) % devices) for i in range(devices)])  8.57 us
    mul x2, other arithmetic, unit_backward(): inverse_norm * (grad - unit * jnp.sum(unit * grad, -1, keepdims=True))  6.78 us
  transfers between devices with their start and end apart: 4, of which 3 were waited for; matrix products, arithmetic and copies ran while one was open for 34% of the time, Pallas kernels for 0%

commit v1 on v0

v1 whole, which is shorter than its diff:
```python
import functools

import jax
import jax.numpy as jnp
from jax import lax
from jax.experimental import pallas as pl
from jax.experimental.pallas import tpu as pltpu
from jax.sharding import PartitionSpec as P

AXES = ("grp", "dp")
LOG2E = 1.4426950408889634
VMEM_LIMIT = 32 * 2**20


def swapped(x, parity):
    devices = lax.axis_size(AXES)
    pairs = []
    for k in range(parity, devices, 2):
        after = (k + 1) % devices
        pairs += [(k, after), (after, k)]
    return lax.ppermute(x, AXES, pairs)


def prepare_kernel(image_ref, text_ref, image_out, image_norm_out, text_out, text_norm_out):
    for raw_ref, out_ref, norm_ref in (
        (image_ref, image_out, image_norm_out),
        (text_ref, text_out, text_norm_out),
    ):
        values = raw_ref[...].astype(jnp.float32)
        norm = lax.rsqrt(jnp.sum(values * values, -1, keepdims=True) + 1e-06)
        out_ref[...] = (values * norm).astype(jnp.bfloat16)
        norm_ref[...] = norm


def prepare(image, text, step=256):
    rows, width = image.shape
    block = pl.BlockSpec((step, width), lambda i: (i, 0))
    column = pl.BlockSpec((step, 1), lambda i: (i, 0))
    unit = jax.ShapeDtypeStruct((rows, width), jnp.bfloat16)
    norm = jax.ShapeDtypeStruct((rows, 1), jnp.float32)
    return pl.pallas_call(
        prepare_kernel,
        grid=(rows // step,),
        in_specs=[block, block],
        out_specs=[block, column, block, column],
        out_shape=[unit, norm, unit, norm],
        compiler_params=pltpu.CompilerParams(vmem_limit_bytes=VMEM_LIMIT),
        cost_estimate=pl.CostEstimate(
            flops=8 * rows * width, bytes_accessed=8 * rows * width, transcendentals=2 * rows
        ),
        name="prepare",
    )(image, text)


def side_kernel(*refs, label, raw_other, has_sum, final, chunk):
    refs = list(refs)
    scalars, own_ref, other_ref = refs[:3]
    refs = refs[3:]
    pair_ref = refs.pop(0) if label else None
    sum_ref = refs.pop(0) if has_sum else None
    raw_ref, norm_ref = (refs.pop(0), refs.pop(0)) if final else (None, None)
    out_ref = refs.pop(0)
    count = other_ref.shape[0]
    if raw_other:
        unit_ref = refs.pop(0)

        @pl.when(pl.program_id(0) == 0)
        def _():
            for r in range(0, count, 256):
                values = other_ref[r : r + 256, :].astype(jnp.float32)
                norm = lax.rsqrt(jnp.sum(values * values, -1, keepdims=True) + 1e-06)
                unit_ref[r : r + 256, :] = (values * norm).astype(jnp.bfloat16)
    else:
        unit_ref = other_ref
    slope, shift, floor = scalars[0], scalars[1], scalars[2]
    own = own_ref[...]
    rows = own.shape[0]
    if label == "row":
        row_id = pl.program_id(0) * rows + lax.broadcasted_iota(jnp.int32, (rows, chunk), 0)
    grads = []
    for c in range(0, count, chunk):
        other = unit_ref[c : c + chunk, :]
        scores = lax.dot_general(
            own, other, (((1,), (1,)), ((), ())), preferred_element_type=jnp.float32
        )
        power = slope * scores + shift
        if label:
            if label == "row":
                match = row_id == pair_ref[:, c : c + chunk]
            else:
                match = pair_ref[...] == c + lax.broadcasted_iota(jnp.int32, (rows, chunk), 1)
            sign = jnp.where(match, -1.0, 1.0)
            tile = sign * pltpu.reciprocal(
                floor + floor * jnp.exp2(sign * power), approx=True
            )
        else:
            tile = pltpu.reciprocal(floor + floor * jnp.exp2(power), approx=True)
        grads.append(tile.astype(jnp.bfloat16))
    grad = grads[0] if len(grads) == 1 else jnp.concatenate(grads, 1)
    total = jnp.dot(grad, unit_ref[...], preferred_element_type=jnp.float32)
    if has_sum:
        total = total + sum_ref[...]
    if final:
        norm = norm_ref[...]
        unit = raw_ref[...].astype(jnp.float32) * norm
        total = norm * (total - unit * jnp.sum(unit * total, -1, keepdims=True))
    out_ref[...] = total


def one_side(
    scalars, own, other, pair=None, label=None, raw_other=False, so_far=None, final=None, step=512,
    chunk=256, name="side",
):
    rows, width = own.shape
    count = other.shape[0]
    block = pl.BlockSpec((step, width), lambda i: (i, 0))
    column = pl.BlockSpec((step, 1), lambda i: (i, 0))
    whole = pl.BlockSpec((count, width), lambda i: (0, 0))
    args = [scalars, own, other]
    specs = [pl.BlockSpec(memory_space=pltpu.SMEM), block, whole]
    if label:
        args.append(pair)
        specs.append(column if label == "column" else pl.BlockSpec((1, count), lambda i: (0, 0)))
    if so_far is not None:
        args.append(so_far)
        specs.append(block)
    if final is not None:
        args += list(final)
        specs += [block, column]
    kernel = functools.partial(
        side_kernel, label=label, raw_other=raw_other, has_sum=so_far is not None,
        final=final is not None, chunk=chunk,
    )
    return pl.pallas_call(
        kernel,
        grid=(rows // step,),
        in_specs=specs,
        out_specs=block,
        out_shape=jax.ShapeDtypeStruct((rows, width), jnp.float32),
        scratch_shapes=[pltpu.VMEM((count, width), jnp.bfloat16)] if raw_other else [],
        compiler_params=pltpu.CompilerParams(vmem_limit_bytes=VMEM_LIMIT),
        cost_estimate=pl.CostEstimate(
            flops=rows * width, bytes_accessed=rows * width, transcendentals=0
        ),
        name=name,
    )(*args)


def local(
    photo_vectors_raw, sentence_vectors_raw, companion_index, exponent_of_sharpness, affinity_offset
):
    sharpness = jnp.exp(exponent_of_sharpness[0])
    scalars = jnp.stack([-LOG2E * sharpness, -LOG2E * affinity_offset[0], 1.0 / sharpness])
    rows = photo_vectors_raw.shape[0]

    text_near = swapped(sentence_vectors_raw, 0)
    text_far = swapped(sentence_vectors_raw, 1)
    image_unit, image_norm, text_unit, text_norm = prepare(photo_vectors_raw, sentence_vectors_raw)
    image_near = swapped(image_unit, 0)
    image_far = swapped(image_unit, 1)

    image_sum = one_side(
        scalars, image_unit, text_unit, companion_index.reshape(rows, 1), "column", name="image_own"
    )
    text_sum = one_side(scalars, text_unit, image_unit, companion_index, "row", name="text_own")
    image_sum = one_side(
        scalars, image_unit, text_near, raw_other=True, so_far=image_sum, name="image_near"
    )
    image_grad = one_side(
        scalars, image_unit, text_far, raw_other=True, so_far=image_sum,
        final=(photo_vectors_raw, image_norm), name="image_far",
    )
    image_grad, text_sum = lax.optimization_barrier((image_grad, text_sum))
    text_sum = one_side(scalars, text_unit, image_near, so_far=text_sum, name="text_near")
    text_grad = one_side(
        scalars, text_unit, image_far, so_far=text_sum, final=(sentence_vectors_raw, text_norm),
        name="text_far",
    )
    return (image_grad, text_grad)


def solution(mesh):
    placed = (P(AXES, None), P(AXES, None), P(AXES, None), P(), P())
    return jax.shard_map(
        local, mesh=mesh, in_specs=placed, out_specs=(P(AXES, None), P(AXES, None)), check_vma=False
    )
```

time: 112 us -> 94 us (0.84)
  the two profiles are of different devices: /device:TPU:102 before, /device:TPU:0 now
where the time goes in v1:
time: 94 us; the launch traced here: 92.7 us
  waiting for transfers between devices  38.5 us (41%)
  Pallas kernels  36.3 us (39%)
  starting transfers between devices  10.3 us (11%)
  local copies, waits for them, and re-layouts  5.45 us (6%)
  between operations  2.12 us (2%)
    ppermute x4, waiting for transfers between devices, swapped(): return lax.ppermute(x, AXES, pairs)  38.5 us
    pallas_call x6, Pallas kernels, one_side(): pl.pallas_call(kernel, grid=(rows // step,), in_specs=specs, out_specs=bl...  35.3 us
    ppermute x4, starting transfers between devices, swapped(): return lax.ppermute(x, AXES, pairs)  10.3 us
    unnamed x20, local copies, waits for them, and re-layouts  4.43 us
  transfers between devices with their start and end apart: 4, of which 3 were waited for; matrix products, arithmetic and copies ran while one was open for 1% of the time, Pallas kernels for 31%

profile of v1, /device:TPU:0, one launch (start us, length us, event | category | flops | bytes accessed | tf_op | source)
XLA Modules:
  0.0 92.7 jit_solution(2017600378425151908)
XLA Ops:
  0.6 8.3 %collective-permute-start = (bf16[1024,768]{1,0:T(8,128)(2,1)}, bf16[1024,768]{1,0:T(8,128)(2,1)}, u32[]{:S(2)}, u32[]{:S(2)}) collective-permute-start(bf16[1024,768]{1,0:T(8,128)(2,1)} %refs_4_.3), channel_id=1, source_target_pairs={{1,2},{2,1},{3,4},{4,3},{5,6},{6,5},{7,8},{8,7},{9,10},{10,9},{11,... | collective-permute-start | bytes 4718600 | tf_op jit(solution)/shard_map/ppermute | solution.py:21
  8.9 0.0 collective-permute-start.1
  8.9 1.4 %copy-done = bf16[1024,768]{1,0:T(8,128)(2,1)S(1)} copy-done((bf16[1024,768]{1,0:T(8,128)(2,1)S(1)}, bf16[1024,768]{1,0:T(8,128)(2,1)}, u32[]{:S(2)}) %copy-start) | copy-done | bytes 1572888
  10.3 1.4 %copy-done.2 = bf16[1024,768]{1,0:T(8,128)(2,1)S(1)} copy-done((bf16[1024,768]{1,0:T(8,128)(2,1)S(1)}, bf16[1024,768]{1,0:T(8,128)(2,1)}, u32[]{:S(2)}) %copy-start.2) | copy-done | bytes 1572888
  11.7 1.0 %prepare.1 = (bf16[1024,768]{1,0:T(8,128)(2,1)S(1)}, f32[1024,1]{1,0:T(8,128)S(1)}, bf16[1024,768]{1,0:T(8,128)(2,1)S(1)}, f32[1024,1]{1,0:T(8,128)S(1)}) custom-call(bf16[1024,768]{1,0:T(8,128)(2,1)S(1)} %copy-done, bf16[1024,768]{1,0:T(8,128)(2,1)S(1)} %copy-done.2), custom_call_target="tpu_custom_call" | custom-call | flops 6291456 | bytes 6291456 | tf_op jit(solution)/shard_map/prepare/pallas_call | solution.py:41
  12.8 0.8 copy-done.5
  13.6 0.8 copy-done.7
  14.4 2.0 %collective-permute-start.3 = (bf16[1024,768]{1,0:T(8,128)(2,1)S(1)}, bf16[1024,768]{1,0:T(8,128)(2,1)}, u32[]{:S(2)}, u32[]{:S(2)}) collective-permute-start(bf16[1024,768]{1,0:T(8,128)(2,1)S(1)} %get-tuple-element.8.refs_1_.refs_2_), channel_id=1, source_target_pairs={{0,1},{1,0},{2,3},{3,2},{4,5},{5,4},{6,7},{7,6},{8,9},{9,8},{10,11... | collective-permute-start | bytes 4718600 | tf_op jit(solution)/shard_map/ppermute | solution.py:21
  16.4 0.0 collective-permute-start.2
  17.8 0.0 copy-done.9
  17.8 1.0 %copy.7.refs_3_ = s32[1024,1]{1,0:T(8,128)} copy(s32[1024,1]{0,1:T(1,128)S(1)} %bitcast.1) | data formatting | bytes 8192 | tf_op jit(solution)/shard_map/reshape | solution.py:163
  18.8 0.1 pad_maximum_fusion.refs_0_
  18.9 4.6 %text_own.1.refs_3_ = f32[1024,768]{1,0:T(8,128)S(1)} custom-call(f32[3]{0:T(128)S(1)} %pad_maximum_fusion.refs_0_, bf16[1024,768]{1,0:T(8,128)(2,1)S(1)} %get-tuple-element.9.refs_2_.refs_1_, bf16[1024,768]{1,0:T(8,128)(2,1)S(1)} %get-tuple-element.8.refs_1_.refs_2_, s32[1,1024]{1,0:T(1,128)S(1)} %copy-done.9), custom_call_target="tpu_custom_call" | custom-call | flops 786432 | bytes 786432 | tf_op jit(solution)/shard_map/text_own/pallas_call | solution.py:134
  23.5 4.6 %image_own.1.refs_3_ = f32[1024,768]{1,0:T(8,128)S(1)} custom-call(f32[3]{0:T(128)S(1)} %pad_maximum_fusion.refs_0_, bf16[1024,768]{1,0:T(8,128)(2,1)S(1)} %get-tuple-element.8.refs_1_.refs_2_, bf16[1024,768]{1,0:T(8,128)(2,1)S(1)} %get-tuple-element.9.refs_2_.refs_1_, s32[1024,1]{1,0:T(8,128)S(1)} %copy-done.4), custom_call_target="tpu_custom_call" | custom-call | flops 786432 | bytes 786432 | tf_op jit(solution)/shard_map/image_own/pallas_call | solution.py:134
  28.1 0.0 copy-start.1
  28.1 0.0 copy-start.8
  28.1 18.4 %collective-permute-done.1.refs_2_ = bf16[1024,768]{1,0:T(8,128)(2,1)} collective-permute-done((bf16[1024,768]{1,0:T(8,128)(2,1)}, bf16[1024,768]{1,0:T(8,128)(2,1)}, u32[]{:S(2)}, u32[]{:S(2)}) %collective-permute-start.1) | collective-permute-done | bytes 1572896 | tf_op jit(solution)/shard_map/ppermute | solution.py:21
  46.5 5.9 %image_near.1.refs_3_ = f32[1024,768]{1,0:T(8,128)S(1)} custom-call(f32[3]{0:T(128)S(1)} %pad_maximum_fusion.refs_0_, bf16[1024,768]{1,0:T(8,128)(2,1)S(1)} %get-tuple-element.8.refs_1_.refs_2_, bf16[1024,768]{1,0:T(8,128)(2,1)} %collective-permute-done.1.refs_2_, f32[1024,768]{1,0:T(8,128)S(1)} %image_own.1.refs_3_), custom_call_target="tpu_custom_call" | custom-call | flops 786432 | bytes 786432 | tf_op jit(solution)/shard_map/image_near/pallas_call | solution.py:134
  52.4 8.6 %collective-permute-done.refs_2_ = bf16[1024,768]{1,0:T(8,128)(2,1)} collective-permute-done((bf16[1024,768]{1,0:T(8,128)(2,1)}, bf16[1024,768]{1,0:T(8,128)(2,1)}, u32[]{:S(2)}, u32[]{:S(2)}) %collective-permute-start) | collective-permute-done | bytes 1572896 | tf_op jit(solution)/shard_map/ppermute | solution.py:21
  61.0 7.6 %image_far.1 = f32[1024,768]{1,0:T(8,128)} custom-call(f32[3]{0:T(128)S(1)} %pad_maximum_fusion.refs_0_, bf16[1024,768]{1,0:T(8,128)(2,1)S(1)} %get-tuple-element.8.refs_1_.refs_2_, bf16[1024,768]{1,0:T(8,128)(2,1)} %collective-permute-done.refs_2_, f32[1024,768]{1,0:T(8,128)S(1)} %image_near.1.refs_3_, bf16[1024,768]{1,0:T(8,128)(2,1)S(1)} %copy-done.1, ...), custom_call_target="tpu_custom_call" | custom-call | flops 786432 | bytes 786432 | tf_op jit(solution)/shard_map/image_far/pallas_call | solution.py:134
  68.7 11.5 %collective-permute-done.3.refs_2_ = bf16[1024,768]{1,0:T(8,128)(2,1)} collective-permute-done((bf16[1024,768]{1,0:T(8,128)(2,1)S(1)}, bf16[1024,768]{1,0:T(8,128)(2,1)}, u32[]{:S(2)}, u32[]{:S(2)}) %collective-permute-start.3) | collective-permute-done | bytes 1572896 | tf_op jit(solution)/shard_map/ppermute | solution.py:21
  80.2 5.4 %text_near.1.refs_3_ = f32[1024,768]{1,0:T(8,128)S(1)} custom-call(f32[3]{0:T(128)S(1)} %pad_maximum_fusion.refs_0_, bf16[1024,768]{1,0:T(8,128)(2,1)S(1)} %get-tuple-element.9.refs_2_.refs_1_, bf16[1024,768]{1,0:T(8,128)(2,1)} %collective-permute-done.3.refs_2_, f32[1024,768]{1,0:T(8,128)S(1)} %text_own.1.refs_3_), custom_call_target="tpu_custom_call" | custom-call | flops 786432 | bytes 786432 | tf_op jit(solution)/shard_map/text_near/pallas_call | solution.py:134
  85.6 0.0 collective-permute-done.2.refs_2_
  85.6 7.1 %text_far.1 = f32[1024,768]{1,0:T(8,128)} custom-call(f32[3]{0:T(128)S(1)} %pad_maximum_fusion.refs_0_, bf16[1024,768]{1,0:T(8,128)(2,1)S(1)} %get-tuple-element.9.refs_2_.refs_1_, bf16[1024,768]{1,0:T(8,128)(2,1)} %collective-permute-done.2.refs_2_, f32[1024,768]{1,0:T(8,128)S(1)} %text_near.1.refs_3_, bf16[1024,768]{1,0:T(8,128)(2,1)S(1)} %copy-done.3, ...), custom_call_target="tpu_custom_call" | custom-call | flops 786432 | bytes 786432 | tf_op jit(solution)/shard_map/text_far/pallas_call | solution.py:134
  (13 shorter events, 0.0 us)
Async XLA Ops:
  0.6 60.4 %collective-permute-start = (bf16[1024,768]{1,0:T(8,128)(2,1)}, bf16[1024,768]{1,0:T(8,128)(2,1)}, u32[]{:S(2)}, u32[]{:S(2)}) collective-permute-start(bf16[1024,768]{1,0:T(8,128)(2,1)} %refs_4_.3), channel_id=1, source_target_pairs={{1,2},{2,1},{3,4},{4,3},{5,6},{6,5},{7,8},{8,7},{9,10},{10,9},{11,... | collective-permute-start | bytes 4718600 | tf_op jit(solution)/shard_map/ppermute | solution.py:21
  8.9 37.6 %collective-permute-start.1 = (bf16[1024,768]{1,0:T(8,128)(2,1)}, bf16[1024,768]{1,0:T(8,128)(2,1)}, u32[]{:S(2)}, u32[]{:S(2)}) collective-permute-start(bf16[1024,768]{1,0:T(8,128)(2,1)} %refs_4_.3), channel_id=1, source_target_pairs={{0,1},{1,0},{2,3},{3,2},{4,5},{5,4},{6,7},{7,6},{8,9},{9,8},{10,11... | collective-permute-start | bytes 4718600 | tf_op jit(solution)/shard_map/ppermute | solution.py:21
  8.9 1.4 %copy-start = (bf16[1024,768]{1,0:T(8,128)(2,1)S(1)}, bf16[1024,768]{1,0:T(8,128)(2,1)}, u32[]{:S(2)}) copy-start(bf16[1024,768]{1,0:T(8,128)(2,1)} %refs_4_.2) | copy-start | bytes 4718596
  10.3 1.4 %copy-start.2 = (bf16[1024,768]{1,0:T(8,128)(2,1)S(1)}, bf16[1024,768]{1,0:T(8,128)(2,1)}, u32[]{:S(2)}) copy-start(bf16[1024,768]{1,0:T(8,128)(2,1)} %refs_4_.3) | copy-start | bytes 4718596
  11.7 6.0 %copy-start.9 = (s32[1,1024]{1,0:T(1,128)S(1)}, s32[1,1024]{1,0:T(1,128)}, u32[]{:S(2)}) copy-start(s32[1,1024]{1,0:T(1,128)} %refs_3_.1) | copy-start | bytes 12292
  12.8 0.8 copy-start.5
  13.6 0.8 copy-start.7
  14.4 65.8 %collective-permute-start.3 = (bf16[1024,768]{1,0:T(8,128)(2,1)S(1)}, bf16[1024,768]{1,0:T(8,128)(2,1)}, u32[]{:S(2)}, u32[]{:S(2)}) collective-permute-start(bf16[1024,768]{1,0:T(8,128)(2,1)S(1)} %get-tuple-element.8.refs_1_.refs_2_), channel_id=1, source_target_pairs={{0,1},{1,0},{2,3},{3,2},{4,5},{5,4},{6,7},{7,6},{8,9},{9,8},{10,11... | collective-permute-start | bytes 4718600 | tf_op jit(solution)/shard_map/ppermute | solution.py:21
  16.4 69.2 %collective-permute-start.2 = (bf16[1024,768]{1,0:T(8,128)(2,1)S(1)}, bf16[1024,768]{1,0:T(8,128)(2,1)}, u32[]{:S(2)}, u32[]{:S(2)}) collective-permute-start(bf16[1024,768]{1,0:T(8,128)(2,1)S(1)} %get-tuple-element.8.refs_1_.refs_2_), channel_id=1, source_target_pairs={{1,2},{2,1},{3,4},{4,3},{5,6},{6,5},{7,8},{8,7},{9,10},{10,9},{11,... | collective-permute-start | bytes 4718600 | tf_op jit(solution)/shard_map/ppermute | solution.py:21
  18.9 4.6 %copy-start.4 = (s32[1024,1]{1,0:T(8,128)S(1)}, s32[1024,1]{1,0:T(8,128)}, u32[]{:S(2)}) copy-start(s32[1024,1]{1,0:T(8,128)} %copy.7.refs_3_) | copy-start | bytes 12292
  28.1 32.9 %copy-start.1 = (bf16[1024,768]{1,0:T(8,128)(2,1)S(1)}, bf16[1024,768]{1,0:T(8,128)(2,1)}, u32[]{:S(2)}) copy-start(bf16[1024,768]{1,0:T(8,128)(2,1)} %refs_4_.2) | copy-start | bytes 4718596
  28.1 32.9 %copy-start.8 = (f32[1024,1]{1,0:T(8,128)S(1)}, f32[1024,1]{1,0:T(8,128)}, u32[]{:S(2)}) copy-start(f32[1024,1]{1,0:T(8,128)} %copy-done.7) | copy-start | bytes 12292
  68.7 16.9 %copy-start.3 = (bf16[1024,768]{1,0:T(8,128)(2,1)S(1)}, bf16[1024,768]{1,0:T(8,128)(2,1)}, u32[]{:S(2)}) copy-start(bf16[1024,768]{1,0:T(8,128)(2,1)} %refs_4_.3) | copy-start | bytes 4718596
  68.7 16.9 %copy-start.6 = (f32[1024,1]{1,0:T(8,128)S(1)}, f32[1024,1]{1,0:T(8,128)}, u32[]{:S(2)}) copy-start(f32[1024,1]{1,0:T(8,128)} %copy-done.5) | copy-start | bytes 12292

commit v2 on v1

v2 whole, which is shorter than its diff:
```python
import functools

import jax
import jax.numpy as jnp
from jax import lax
from jax.experimental import pallas as pl
from jax.experimental.pallas import tpu as pltpu
from jax.sharding import PartitionSpec as P

AXES = ("grp", "dp")
LOG2E = 1.4426950408889634
VMEM_LIMIT = 24 * 2**20
LAST = 4
IN_VMEM = pl.BlockSpec(memory_space=pltpu.VMEM)
IN_SMEM = pl.BlockSpec(memory_space=pltpu.SMEM)


def swapped(x, parity):
    devices = lax.axis_size(AXES)
    pairs = []
    for k in range(parity, devices, 2):
        after = (k + 1) % devices
        pairs += [(k, after), (after, k)]
    return lax.ppermute(x, AXES, pairs)


def unit_rows(raw):
    values = raw.astype(jnp.float32)
    norm = lax.rsqrt(jnp.sum(values * values, -1, keepdims=True) + 1e-06)
    return values * norm, norm


def prepare_kernel(image, text, image_out, head_out, tail_out, image_norm, text_out, text_norm):
    rows, step = image.shape[0], 256
    head = head_out.shape[0]
    for r in range(0, rows, step):
        at = slice(r, r + step)
        unit, image_norm[at, :] = unit_rows(image[at, :])
        unit = unit.astype(jnp.bfloat16)
        image_out[at, :] = unit
        if r < head:
            head_out[at, :] = unit
        else:
            tail_out[r - head : r - head + step, :] = unit
        unit, text_norm[at, :] = unit_rows(text[at, :])
        text_out[at, :] = unit.astype(jnp.bfloat16)


def prepare(image, text):
    rows, width = image.shape
    last = rows // LAST
    unit = jax.ShapeDtypeStruct((rows, width), jnp.bfloat16)
    head = jax.ShapeDtypeStruct((rows - last, width), jnp.bfloat16)
    tail = jax.ShapeDtypeStruct((last, width), jnp.bfloat16)
    norm = jax.ShapeDtypeStruct((rows, 1), jnp.float32)
    return pl.pallas_call(
        prepare_kernel,
        in_specs=[IN_VMEM, IN_VMEM],
        out_specs=[IN_VMEM] * 6,
        out_shape=[unit, head, tail, norm, unit, norm],
        compiler_params=pltpu.CompilerParams(vmem_limit_bytes=VMEM_LIMIT),
        cost_estimate=pl.CostEstimate(
            flops=8 * rows * width, bytes_accessed=8 * rows * width, transcendentals=2 * rows
        ),
        name="prepare",
    )(image, text)


def side_kernel(*refs, label, raw_other, has_sum, final, step, chunk):
    refs = list(refs)
    scalars, own_ref, other_ref = refs[:3]
    refs = refs[3:]
    pair_ref = refs.pop(0) if label else None
    sum_ref = refs.pop(0) if has_sum else None
    raw_ref, norm_ref = (refs.pop(0), refs.pop(0)) if final else (None, None)
    out_ref = refs.pop(0)
    rows, count = own_ref.shape[0], other_ref.shape[0]
    if raw_other:
        unit_ref = refs.pop(0)
        for r in range(0, count, 256):
            unit, _ = unit_rows(other_ref[r : r + 256, :])
            unit_ref[r : r + 256, :] = unit.astype(jnp.bfloat16)
    else:
        unit_ref = other_ref
    if final:
        grad_ref, sem = refs
    slope, shift, floor = scalars[0], scalars[1], scalars[2]
    for r in range(0, rows, step):
        at = slice(r, r + step)
        own = own_ref[at, :]
        tiles = []
        for c in range(0, count, chunk):
            scores = lax.dot_general(
                own,
                unit_ref[c : c + chunk, :],
                (((1,), (1,)), ((), ())),
                preferred_element_type=jnp.float32,
            )
            power = slope * scores + shift
            if label:
                if label == "row":
                    row_id = r + lax.broadcasted_iota(jnp.int32, (step, chunk), 0)
                    match = row_id == pair_ref[:, c : c + chunk]
                else:
                    column_id = c + lax.broadcasted_iota(jnp.int32, (step, chunk), 1)
                    match = pair_ref[at, :] == column_id
                sign = jnp.where(match, -1.0, 1.0)
                tile = sign * pltpu.reciprocal(
                    floor + floor * jnp.exp2(sign * power), approx=True
                )
            else:
                tile = pltpu.reciprocal(floor + floor * jnp.exp2(power), approx=True)
            tiles.append(tile.astype(jnp.bfloat16))
        tile = tiles[0] if len(tiles) == 1 else jnp.concatenate(tiles, 1)
        total = jnp.dot(tile, unit_ref[...], preferred_element_type=jnp.float32)
        if has_sum:
            total = total + sum_ref[at, :]
        if final:
            norm = norm_ref[at, :]
            unit = raw_ref[at, :].astype(jnp.float32) * norm
            total = norm * (total - unit * jnp.sum(unit * total, -1, keepdims=True))
            grad_ref[at, :] = total
            pltpu.make_async_copy(grad_ref.at[at], out_ref.at[at], sem.at[r // step]).start()
        else:
            out_ref[at, :] = total
    if final:
        for r in range(0, rows, step):
            at = slice(r, r + step)
            pltpu.make_async_copy(grad_ref.at[at], out_ref.at[at], sem.at[r // step]).wait()


def one_side(
    scalars, own, other, pair=None, label=None, raw_other=False, so_far=None, final=None, step=256,
    chunk=256, name="side",
):
    rows, width = own.shape
    count = other.shape[0]
    args = [scalars, own, other]
    if label:
        args.append(pair)
    if so_far is not None:
        args.append(so_far)
    scratch = []
    if raw_other:
        scratch.append(pltpu.VMEM((count, width), jnp.bfloat16))
    if final is not None:
        args += list(final)
        scratch.append(pltpu.VMEM((rows, width), jnp.float32))
        scratch.append(pltpu.SemaphoreType.DMA((rows // step,)))
    kernel = functools.partial(
        side_kernel, label=label, raw_other=raw_other, has_sum=so_far is not None,
        final=final is not None, step=step, chunk=min(chunk, count),
    )
    return pl.pallas_call(
        kernel,
        in_specs=[IN_SMEM] + [IN_VMEM] * (len(args) - 1),
        out_specs=IN_VMEM if final is None else pl.BlockSpec(memory_space=pl.ANY),
        out_shape=jax.ShapeDtypeStruct((rows, width), jnp.float32),
        scratch_shapes=scratch,
        compiler_params=pltpu.CompilerParams(vmem_limit_bytes=VMEM_LIMIT),
        cost_estimate=pl.CostEstimate(
            flops=rows * width, bytes_accessed=rows * width, transcendentals=0
        ),
        name=name,
    )(*args)


def local(
    photo_vectors_raw, sentence_vectors_raw, companion_index, exponent_of_sharpness, affinity_offset
):
    sharpness = jnp.exp(exponent_of_sharpness[0])
    scalars = jnp.stack([-LOG2E * sharpness, -LOG2E * affinity_offset[0], 1.0 / sharpness])
    rows = photo_vectors_raw.shape[0]

    text_far = swapped(sentence_vectors_raw, 1)
    text_near = swapped(sentence_vectors_raw, 0)
    image_unit, image_head, image_tail, image_norm, text_unit, text_norm = prepare(
        photo_vectors_raw, sentence_vectors_raw
    )
    image_near = swapped(image_unit, 0)
    head_far = swapped(image_head, 1)
    tail_far = swapped(image_tail, 1)

    image_sum = one_side(
        scalars, image_unit, text_unit, companion_index.reshape(rows, 1), "column", name="image_own"
    )
    text_sum = one_side(scalars, text_unit, image_unit, companion_index, "row", name="text_own")
    image_sum = one_side(
        scalars, image_unit, text_near, raw_other=True, so_far=image_sum, name="image_near"
    )
    image_grad = one_side(
        scalars, image_unit, text_far, raw_other=True, so_far=image_sum,
        final=(photo_vectors_raw, image_norm), name="image_far",
    )
    image_grad, text_sum = lax.optimization_barrier((image_grad, text_sum))
    text_sum = one_side(scalars, text_unit, image_near, so_far=text_sum, name="text_near")
    text_sum = one_side(scalars, text_unit, head_far, so_far=text_sum, name="text_far_head")
    text_grad = one_side(
        scalars, text_unit, tail_far, so_far=text_sum, final=(sentence_vectors_raw, text_norm),
        name="text_far_tail",
    )
    return (image_grad, text_grad)


def solution(mesh):
    placed = (P(AXES, None), P(AXES, None), P(AXES, None), P(), P())
    return jax.shard_map(
        local, mesh=mesh, in_specs=placed, out_specs=(P(AXES, None), P(AXES, None)), check_vma=False
    )
```

time: 94 us -> 84.7 us (0.901)
  waiting for transfers between devices: 38.5 us -> 25.3 us
  starting transfers between devices: 10.3 us -> 15.6 us
    ppermute x4 -> x5, waiting for transfers between devices: 38.5 us -> 25.3 us  [swapped(): return lax.ppermute(x, AXES, pairs)]
    ppermute x4 -> x5, starting transfers between devices: 10.3 us -> 15.6 us  [swapped(): return lax.ppermute(x, AXES, pairs)]
    pallas_call x7 -> x8, Pallas kernels: 36.3 us -> 35.6 us  [the longest x7 33.6 us: one_side(): pl.pallas_call(kernel, in_specs=[IN_SMEM] + [IN_VMEM] * (len(args) - 1),...]
  transfers between devices with their start and end apart: 4 -> 5, of which waited for: 3 -> 3; matrix products, arithmetic and copies ran while one was open for 1% -> 1% of each run, Pallas kernels for 31% -> 38%
where the time goes in v2:
time: 84.7 us; the launch traced here: 84.3 us
  Pallas kernels  35.6 us (42%)
  waiting for transfers between devices  25.3 us (30%)
  starting transfers between devices  15.6 us (18%)
  local copies, waits for them, and re-layouts  5.48 us (6%)
  between operations  2.33 us (3%)
    pallas_call x7, Pallas kernels, one_side(): pl.pallas_call(kernel, in_specs=[IN_SMEM] + [IN_VMEM] * (len(args) - 1),...  33.6 us
    ppermute x5, waiting for transfers between devices, swapped(): return lax.ppermute(x, AXES, pairs)  25.3 us
    ppermute x5, starting transfers between devices, swapped(): return lax.ppermute(x, AXES, pairs)  15.6 us
    unnamed x20, local copies, waits for them, and re-layouts  4.46 us
    pallas_call x1, Pallas kernels, prepare(): pl.pallas_call(prepare_kernel, in_specs=[IN_VMEM, IN_VMEM], out_specs=[IN...  1.92 us
  transfers between devices with their start and end apart: 5, of which 3 were waited for; matrix products, arithmetic and copies ran while one was open for 1% of the time, Pallas kernels for 38%

profile of v2, /device:TPU:0, one launch (start us, length us, event | category | flops | bytes accessed | tf_op | source)
XLA Modules:
  0.0 84.3 jit_solution(282445758841112320)
XLA Ops:
  0.6 2.1 %collective-permute-start.1 = (bf16[1024,768]{1,0:T(8,128)(2,1)}, bf16[1024,768]{1,0:T(8,128)(2,1)}, u32[]{:S(2)}, u32[]{:S(2)}) collective-permute-start(bf16[1024,768]{1,0:T(8,128)(2,1)} %refs_4_.3), channel_id=1, source_target_pairs={{0,1},{1,0},{2,3},{3,2},{4,5},{5,4},{6,7},{7,6},{8,9},{9,8},{10,11... | collective-permute-start | bytes 4718600 | tf_op jit(solution)/shard_map/ppermute | solution.py:24
  2.7 6.3 %collective-permute-start = (bf16[1024,768]{1,0:T(8,128)(2,1)}, bf16[1024,768]{1,0:T(8,128)(2,1)}, u32[]{:S(2)}, u32[]{:S(2)}) collective-permute-start(bf16[1024,768]{1,0:T(8,128)(2,1)} %refs_4_.3), channel_id=1, source_target_pairs={{1,2},{2,1},{3,4},{4,3},{5,6},{6,5},{7,8},{8,7},{9,10},{10,9},{11,... | collective-permute-start | bytes 4718600 | tf_op jit(solution)/shard_map/ppermute | solution.py:24
  9.0 1.4 %copy-done = bf16[1024,768]{1,0:T(8,128)(2,1)S(1)} copy-done((bf16[1024,768]{1,0:T(8,128)(2,1)S(1)}, bf16[1024,768]{1,0:T(8,128)(2,1)}, u32[]{:S(2)}) %copy-start) | copy-done | bytes 1572888
  10.4 1.4 %copy-done.2 = bf16[1024,768]{1,0:T(8,128)(2,1)S(1)} copy-done((bf16[1024,768]{1,0:T(8,128)(2,1)S(1)}, bf16[1024,768]{1,0:T(8,128)(2,1)}, u32[]{:S(2)}) %copy-start.2) | copy-done | bytes 1572888
  11.9 1.9 %prepare.1 = (bf16[1024,768]{1,0:T(8,128)(2,1)S(1)}, bf16[768,768]{1,0:T(8,128)(2,1)}, bf16[256,768]{1,0:T(8,128)(2,1)}, f32[1024,1]{1,0:T(8,128)S(1)}, bf16[102...) custom-call(bf16[1024,768]{1,0:T(8,128)(2,1)S(1)} %copy-done, bf16[1024,768]{1,0:T(8,128)(2,1)S(1)} %copy-done.2), custom_call_target="tpu_custom_call" | custom-call | flops 6291456 | bytes 6291456 | tf_op jit(solution)/shard_map/prepare/pallas_call | solution.py:56
  13.8 0.8 copy-done.5
  14.6 0.8 copy-done.7
  15.4 0.0 collective-permute-start.4
  15.4 1.3 %collective-permute-start.3 = (bf16[768,768]{1,0:T(8,128)(2,1)}, bf16[768,768]{1,0:T(8,128)(2,1)}, u32[]{:S(2)}, u32[]{:S(2)}) collective-permute-start(bf16[768,768]{1,0:T(8,128)(2,1)} %get-tuple-element.15), channel_id=1, source_target_pairs={{1,2},{2,1},{3,4},{4,3},{5,6},{6,5},{7,8},{8,7},{9,10},{10,9},{11,... | collective-permute-start | bytes 3538952 | tf_op jit(solution)/shard_map/ppermute | solution.py:24
  16.7 5.8 %collective-permute-start.2 = (bf16[256,768]{1,0:T(8,128)(2,1)}, bf16[256,768]{1,0:T(8,128)(2,1)S(1)}, u32[]{:S(2)}, u32[]{:S(2)}) collective-permute-start(bf16[256,768]{1,0:T(8,128)(2,1)} %get-tuple-element.14), channel_id=1, source_target_pairs={{1,2},{2,1},{3,4},{4,3},{5,6},{6,5},{7,8},{8,7},{9,10},{10,9},{11,... | collective-permute-start | bytes 1179656 | tf_op jit(solution)/shard_map/ppermute | solution.py:24
  24.0 1.0 %copy.7.refs_3_ = s32[1024,1]{1,0:T(8,128)} copy(s32[1024,1]{0,1:T(1,128)S(1)} %bitcast.1) | data formatting | bytes 8192 | tf_op jit(solution)/shard_map/reshape | solution.py:185
  25.0 0.1 pad_maximum_fusion.refs_0_
  25.1 4.2 %text_own.1.refs_3_ = f32[1024,768]{1,0:T(8,128)S(1)} custom-call(f32[3]{0:T(128)S(1)} %pad_maximum_fusion.refs_0_, bf16[1024,768]{1,0:T(8,128)(2,1)S(1)} %get-tuple-element.11.refs_2_.refs_1_, bf16[1024,768]{1,0:T(8,128)(2,1)S(1)} %get-tuple-element.10.refs_1_.refs_2_, s32[1,1024]{1,0:T(1,128)S(1)} %copy-done.9), custom_call_target="tpu_custom_call" | custom-call | flops 786432 | bytes 786432 | tf_op jit(solution)/shard_map/text_own/pallas_call | solution.py:154
  29.3 4.2 %image_own.1.refs_3_ = f32[1024,768]{1,0:T(8,128)S(1)} custom-call(f32[3]{0:T(128)S(1)} %pad_maximum_fusion.refs_0_, bf16[1024,768]{1,0:T(8,128)(2,1)S(1)} %get-tuple-element.10.refs_1_.refs_2_, bf16[1024,768]{1,0:T(8,128)(2,1)S(1)} %get-tuple-element.11.refs_2_.refs_1_, s32[1024,1]{1,0:T(8,128)S(1)} %copy-done.4), custom_call_target="tpu_custom_call" | custom-call | flops 786432 | bytes 786432 | tf_op jit(solution)/shard_map/image_own/pallas_call | solution.py:154
  33.6 0.0 copy-start.1
  33.6 4.7 %collective-permute-done.1.refs_2_ = bf16[1024,768]{1,0:T(8,128)(2,1)} collective-permute-done((bf16[1024,768]{1,0:T(8,128)(2,1)}, bf16[1024,768]{1,0:T(8,128)(2,1)}, u32[]{:S(2)}, u32[]{:S(2)}) %collective-permute-start.1) | collective-permute-done | bytes 1572896 | tf_op jit(solution)/shard_map/ppermute | solution.py:24
  38.3 5.3 %image_near.1.refs_3_ = f32[1024,768]{1,0:T(8,128)S(1)} custom-call(f32[3]{0:T(128)S(1)} %pad_maximum_fusion.refs_0_, bf16[1024,768]{1,0:T(8,128)(2,1)S(1)} %get-tuple-element.10.refs_1_.refs_2_, bf16[1024,768]{1,0:T(8,128)(2,1)} %collective-permute-done.1.refs_2_, f32[1024,768]{1,0:T(8,128)S(1)} %image_own.1.refs_3_), custom_call_target="tpu_custom_call" | custom-call | flops 786432 | bytes 786432 | tf_op jit(solution)/shard_map/image_near/pallas_call | solution.py:154
  43.6 18.4 %collective-permute-done.refs_2_ = bf16[1024,768]{1,0:T(8,128)(2,1)} collective-permute-done((bf16[1024,768]{1,0:T(8,128)(2,1)}, bf16[1024,768]{1,0:T(8,128)(2,1)}, u32[]{:S(2)}, u32[]{:S(2)}) %collective-permute-start) | collective-permute-done | bytes 1572896 | tf_op jit(solution)/shard_map/ppermute | solution.py:24
  62.0 6.9 %image_far.1 = f32[1024,768]{1,0:T(8,128)} custom-call(f32[3]{0:T(128)S(1)} %pad_maximum_fusion.refs_0_, bf16[1024,768]{1,0:T(8,128)(2,1)S(1)} %get-tuple-element.10.refs_1_.refs_2_, bf16[1024,768]{1,0:T(8,128)(2,1)} %collective-permute-done.refs_2_, f32[1024,768]{1,0:T(8,128)S(1)} %image_near.1.refs_3_, bf16[1024,768]{1,0:T(8,128)(2,1)S(1)} %copy-done.1, ...), custom_call_target="tpu_custom_call" | custom-call | flops 786432 | bytes 786432 | tf_op jit(solution)/shard_map/image_far/pallas_call | solution.py:154
  68.9 2.2 %collective-permute-done.4.refs_2_ = bf16[1024,768]{1,0:T(8,128)(2,1)} collective-permute-done((bf16[1024,768]{1,0:T(8,128)(2,1)S(1)}, bf16[1024,768]{1,0:T(8,128)(2,1)}, u32[]{:S(2)}, u32[]{:S(2)}) %collective-permute-start.4) | collective-permute-done | bytes 1572896 | tf_op jit(solution)/shard_map/ppermute | solution.py:24
  71.1 5.1 %text_near.1.refs_3_ = f32[1024,768]{1,0:T(8,128)S(1)} custom-call(f32[3]{0:T(128)S(1)} %pad_maximum_fusion.refs_0_, bf16[1024,768]{1,0:T(8,128)(2,1)S(1)} %get-tuple-element.11.refs_2_.refs_1_, bf16[1024,768]{1,0:T(8,128)(2,1)} %collective-permute-done.4.refs_2_, f32[1024,768]{1,0:T(8,128)S(1)} %text_own.1.refs_3_), custom_call_target="tpu_custom_call" | custom-call | flops 786432 | bytes 786432 | tf_op jit(solution)/shard_map/text_near/pallas_call | solution.py:154
  76.2 0.0 copy-start.3
  76.3 4.3 %text_far_head.1.refs_3_ = f32[1024,768]{1,0:T(8,128)S(1)} custom-call(f32[3]{0:T(128)S(1)} %pad_maximum_fusion.refs_0_, bf16[1024,768]{1,0:T(8,128)(2,1)S(1)} %get-tuple-element.11.refs_2_.refs_1_, bf16[768,768]{1,0:T(8,128)(2,1)} %collective-permute-done.3.refs_2_, f32[1024,768]{1,0:T(8,128)S(1)} %text_near.1.refs_3_), custom_call_target="tpu_custom_call" | custom-call | flops 786432 | bytes 786432 | tf_op jit(solution)/shard_map/text_far_head/pallas_call | solution.py:154
  80.6 3.5 %text_far_tail.1 = f32[1024,768]{1,0:T(8,128)} custom-call(f32[3]{0:T(128)S(1)} %pad_maximum_fusion.refs_0_, bf16[1024,768]{1,0:T(8,128)(2,1)S(1)} %get-tuple-element.11.refs_2_.refs_1_, bf16[256,768]{1,0:T(8,128)(2,1)S(1)} %collective-permute-done.2.refs_2_, f32[1024,768]{1,0:T(8,128)S(1)} %text_far_head.1.refs_3_, bf16[1024,768]{1,0:T(8,128)(2,1)S(1)} %copy-done.3, ...), custom_call_target="tpu_custom_call" | custom-call | flops 786432 | bytes 786432 | tf_op jit(solution)/shard_map/text_far_tail/pallas_call | solution.py:154
  (16 shorter events, 0.0 us)
Async XLA Ops:
  0.6 37.6 %collective-permute-start.1 = (bf16[1024,768]{1,0:T(8,128)(2,1)}, bf16[1024,768]{1,0:T(8,128)(2,1)}, u32[]{:S(2)}, u32[]{:S(2)}) collective-permute-start(bf16[1024,768]{1,0:T(8,128)(2,1)} %refs_4_.3), channel_id=1, source_target_pairs={{0,1},{1,0},{2,3},{3,2},{4,5},{5,4},{6,7},{7,6},{8,9},{9,8},{10,11... | collective-permute-start | bytes 4718600 | tf_op jit(solution)/shard_map/ppermute | solution.py:24
  2.7 59.3 %collective-permute-start = (bf16[1024,768]{1,0:T(8,128)(2,1)}, bf16[1024,768]{1,0:T(8,128)(2,1)}, u32[]{:S(2)}, u32[]{:S(2)}) collective-permute-start(bf16[1024,768]{1,0:T(8,128)(2,1)} %refs_4_.3), channel_id=1, source_target_pairs={{1,2},{2,1},{3,4},{4,3},{5,6},{6,5},{7,8},{8,7},{9,10},{10,9},{11,... | collective-permute-start | bytes 4718600 | tf_op jit(solution)/shard_map/ppermute | solution.py:24
  9.0 1.4 %copy-start = (bf16[1024,768]{1,0:T(8,128)(2,1)S(1)}, bf16[1024,768]{1,0:T(8,128)(2,1)}, u32[]{:S(2)}) copy-start(bf16[1024,768]{1,0:T(8,128)(2,1)} %refs_4_.2) | copy-start | bytes 4718596
  10.4 1.4 %copy-start.2 = (bf16[1024,768]{1,0:T(8,128)(2,1)S(1)}, bf16[1024,768]{1,0:T(8,128)(2,1)}, u32[]{:S(2)}) copy-start(bf16[1024,768]{1,0:T(8,128)(2,1)} %refs_4_.3) | copy-start | bytes 4718596
  11.9 12.1 %copy-start.9 = (s32[1,1024]{1,0:T(1,128)S(1)}, s32[1,1024]{1,0:T(1,128)}, u32[]{:S(2)}) copy-start(s32[1,1024]{1,0:T(1,128)} %refs_3_.1) | copy-start | bytes 12292
  13.8 0.8 copy-start.5
  14.6 0.8 copy-start.7
  15.4 55.7 %collective-permute-start.4 = (bf16[1024,768]{1,0:T(8,128)(2,1)S(1)}, bf16[1024,768]{1,0:T(8,128)(2,1)}, u32[]{:S(2)}, u32[]{:S(2)}) collective-permute-start(bf16[1024,768]{1,0:T(8,128)(2,1)S(1)} %get-tuple-element.10.refs_1_.refs_2_), channel_id=1, source_target_pairs={{0,1},{1,0},{2,3},{3,2},{4,5},{5,4},{6,7},{7,6},{8,9},{9,8},{10,11... | collective-permute-start | bytes 4718600 | tf_op jit(solution)/shard_map/ppermute | solution.py:24
  15.4 60.8 %collective-permute-start.3 = (bf16[768,768]{1,0:T(8,128)(2,1)}, bf16[768,768]{1,0:T(8,128)(2,1)}, u32[]{:S(2)}, u32[]{:S(2)}) collective-permute-start(bf16[768,768]{1,0:T(8,128)(2,1)} %get-tuple-element.15), channel_id=1, source_target_pairs={{1,2},{2,1},{3,4},{4,3},{5,6},{6,5},{7,8},{8,7},{9,10},{10,9},{11,... | collective-permute-start | bytes 3538952 | tf_op jit(solution)/shard_map/ppermute | solution.py:24
  16.7 63.8 %collective-permute-start.2 = (bf16[256,768]{1,0:T(8,128)(2,1)}, bf16[256,768]{1,0:T(8,128)(2,1)S(1)}, u32[]{:S(2)}, u32[]{:S(2)}) collective-permute-start(bf16[256,768]{1,0:T(8,128)(2,1)} %get-tuple-element.14), channel_id=1, source_target_pairs={{1,2},{2,1},{3,4},{4,3},{5,6},{6,5},{7,8},{8,7},{9,10},{10,9},{11,... | collective-permute-start | bytes 1179656 | tf_op jit(solution)/shard_map/ppermute | solution.py:24
  25.1 4.2 %copy-start.4 = (s32[1024,1]{1,0:T(8,128)S(1)}, s32[1024,1]{1,0:T(8,128)}, u32[]{:S(2)}) copy-start(s32[1024,1]{1,0:T(8,128)} %copy.7.refs_3_) | copy-start | bytes 12292
  33.6 28.5 %copy-start.1 = (bf16[1024,768]{1,0:T(8,128)(2,1)S(1)}, bf16[1024,768]{1,0:T(8,128)(2,1)}, u32[]{:S(2)}) copy-start(bf16[1024,768]{1,0:T(8,128)(2,1)} %refs_4_.2) | copy-start | bytes 4718596
  33.6 28.4 %copy-start.6 = (f32[1024,1]{1,0:T(8,128)S(1)}, f32[1024,1]{1,0:T(8,128)}, u32[]{:S(2)}) copy-start(f32[1024,1]{1,0:T(8,128)} %copy-done.5) | copy-start | bytes 12292
  76.2 4.3 %copy-start.3 = (bf16[1024,768]{1,0:T(8,128)(2,1)S(1)}, bf16[1024,768]{1,0:T(8,128)(2,1)}, u32[]{:S(2)}) copy-start(bf16[1024,768]{1,0:T(8,128)(2,1)} %refs_4_.3) | copy-start | bytes 4718596
  76.2 4.3 %copy-start.8 = (f32[1024,1]{1,0:T(8,128)S(1)}, f32[1024,1]{1,0:T(8,128)}, u32[]{:S(2)}) copy-start(f32[1024,1]{1,0:T(8,128)} %copy-done.7) | copy-start | bytes 12292

commit v3 on v2

--- a/solution.py
+++ b/solution.py
@@ -10,7 +10,7 @@
 AXES = ("grp", "dp")
 LOG2E = 1.4426950408889634
 VMEM_LIMIT = 24 * 2**20
-LAST = 4
+NEAR_LAST, FAR_LAST = 2, 4
 IN_VMEM = pl.BlockSpec(memory_space=pltpu.VMEM)
 IN_SMEM = pl.BlockSpec(memory_space=pltpu.SMEM)
 
@@ -30,34 +30,37 @@
     return values * norm, norm
 
 
-def prepare_kernel(image, text, image_out, head_out, tail_out, image_norm, text_out, text_norm):
+def prepare_kernel(image, text, *outs):
+    image_out, image_norm, text_out, text_norm, *parts = outs
     rows, step = image.shape[0], 256
-    head = head_out.shape[0]
     for r in range(0, rows, step):
         at = slice(r, r + step)
         unit, image_norm[at, :] = unit_rows(image[at, :])
         unit = unit.astype(jnp.bfloat16)
         image_out[at, :] = unit
-        if r < head:
-            head_out[at, :] = unit
-        else:
-            tail_out[r - head : r - head + step, :] = unit
+        for head, tail in (parts[:2], parts[2:]):
+            count = head.shape[0]
+            if r < count:
+                head[at, :] = unit
+            else:
+                tail[r - count : r - count + step, :] = unit
         unit, text_norm[at, :] = unit_rows(text[at, :])
         text_out[at, :] = unit.astype(jnp.bfloat16)
 
 
 def prepare(image, text):
     rows, width = image.shape
-    last = rows // LAST
     unit = jax.ShapeDtypeStruct((rows, width), jnp.bfloat16)
-    head = jax.ShapeDtypeStruct((rows - last, width), jnp.bfloat16)
-    tail = jax.ShapeDtypeStruct((last, width), jnp.bfloat16)
     norm = jax.ShapeDtypeStruct((rows, 1), jnp.float32)
+    parts = []
+    for last in (rows // NEAR_LAST, rows // FAR_LAST):
+        parts.append(jax.ShapeDtypeStruct((rows - last, width), jnp.bfloat16))
+        parts.append(jax.ShapeDtypeStruct((last, width), jnp.bfloat16))
     return pl.pallas_call(
         prepare_kernel,
         in_specs=[IN_VMEM, IN_VMEM],
-        out_specs=[IN_VMEM] * 6,
-        out_shape=[unit, head, tail, norm, unit, norm],
+        out_specs=[IN_VMEM] * 8,
+        out_shape=[unit, norm, unit, norm] + parts,
         compiler_params=pltpu.CompilerParams(vmem_limit_bytes=VMEM_LIMIT),
         cost_estimate=pl.CostEstimate(
             flops=8 * rows * width, bytes_accessed=8 * rows * width, transcendentals=2 * rows
@@ -84,33 +87,42 @@
         unit_ref = other_ref
     if final:
         grad_ref, sem = refs
-    slope, shift, floor = scalars[0], scalars[1], scalars[2]
-    for r in range(0, rows, step):
-        at = slice(r, r + step)
-        own = own_ref[at, :]
-        tiles = []
-        for c in range(0, count, chunk):
-            scores = lax.dot_general(
+    slope, shift, floor, log_floor = (scalars[i] for i in range(4))
+
+    def scores(r):
+        own = own_ref[r : r + step, :]
+        return [
+            lax.dot_general(
                 own,
                 unit_ref[c : c + chunk, :],
                 (((1,), (1,)), ((), ())),
                 preferred_element_type=jnp.float32,
             )
-            power = slope * scores + shift
-            if label:
-                if label == "row":
-                    row_id = r + lax.broadcasted_iota(jnp.int32, (step, chunk), 0)
-                    match = row_id == pair_ref[:, c : c + chunk]
-                else:
-                    column_id = c + lax.broadcasted_iota(jnp.int32, (step, chunk), 1)
-                    match = pair_ref[at, :] == column_id
-                sign = jnp.where(match, -1.0, 1.0)
-                tile = sign * pltpu.reciprocal(
-                    floor + floor * jnp.exp2(sign * power), approx=True
-                )
+            for c in range(0, count, chunk)
+        ]
+
+    def grad_tile(r, c, scores):
+        power = slope * scores + shift
+        if not label:
+            tile = pltpu.reciprocal(floor + jnp.exp2(power + log_floor), approx=True)
+        else:
+            if label == "row":
+                row_id = r + lax.broadcasted_iota(jnp.int32, (step, chunk), 0)
+                match = row_id == pair_ref[:, c : c + chunk]
             else:
-                tile = pltpu.reciprocal(floor + floor * jnp.exp2(power), approx=True)
-            tiles.append(tile.astype(jnp.bfloat16))
+                column_id = c + lax.broadcasted_iota(jnp.int32, (step, chunk), 1)
+                match = pair_ref[r : r + step, :] == column_id
+            sign = jnp.where(match, -1.0, 1.0)
+            tile = sign * pltpu.reciprocal(
+                floor + jnp.exp2(sign * power + log_floor), approx=True
+            )
+        return tile.astype(jnp.bfloat16)
+
+    coming = scores(0)
+    for r in range(0, rows, step):
+        at = slice(r, r + step)
+        now, coming = coming, scores(r + step) if r + step < rows else None
+        tiles = [grad_tile(r, i * chunk, part) for i, part in enumerate(now)]
         tile = tiles[0] if len(tiles) == 1 else jnp.concatenate(tiles, 1)
         total = jnp.dot(tile, unit_ref[...], preferred_element_type=jnp.float32)
         if has_sum:
@@ -168,35 +180,41 @@
 def local(
     photo_vectors_raw, sentence_vectors_raw, companion_index, exponent_of_sharpness, affinity_offset
 ):
-    sharpness = jnp.exp(exponent_of_sharpness[0])
-    scalars = jnp.stack([-LOG2E * sharpness, -LOG2E * affinity_offset[0], 1.0 / sharpness])
+    exponent, offset = exponent_of_sharpness[0], affinity_offset[0]
+    scalars = jnp.stack(
+        [-LOG2E * jnp.exp(exponent), -LOG2E * offset, jnp.exp(-exponent), -LOG2E * exponent]
+    )
     rows = photo_vectors_raw.shape[0]
 
     text_far = swapped(sentence_vectors_raw, 1)
     text_near = swapped(sentence_vectors_raw, 0)
-    image_unit, image_head, image_tail, image_norm, text_unit, text_norm = prepare(
+    image_unit, image_norm, text_unit, text_norm, *parts = prepare(
         photo_vectors_raw, sentence_vectors_raw
     )
-    image_near = swapped(image_unit, 0)
-    head_far = swapped(image_head, 1)
-    tail_far = swapped(image_tail, 1)
-
+    near_head, near_tail = (swapped(part, 0) for part in parts[:2])
+    far_head = swapped(parts[2], 1)
+
+    text_sum = one_side(scalars, text_unit, image_unit, companion_index, "row", name="text_own")
     image_sum = one_side(
         scalars, image_unit, text_unit, companion_index.reshape(rows, 1), "column", name="image_own"
     )
-    text_sum = one_side(scalars, text_unit, image_unit, companion_index, "row", name="text_own")
+    image_sum, text_sum, far_part = lax.optimization_barrier((image_sum, text_sum, parts[3]))
+    far_tail = swapped(far_part, 1)
     image_sum = one_side(
         scalars, image_unit, text_near, raw_other=True, so_far=image_sum, name="image_near"
     )
+    image_sum, text_sum = lax.optimization_barrier((image_sum, text_sum))
+    text_sum = one_side(scalars, text_unit, near_head, so_far=text_sum, name="text_near_head")
+    image_sum, text_sum = lax.optimization_barrier((image_sum, text_sum))
     image_grad = one_side(
         scalars, image_unit, text_far, raw_other=True, so_far=image_sum,
         final=(photo_vectors_raw, image_norm), name="image_far",
     )
     image_grad, text_sum = lax.optimization_barrier((image_grad, text_sum))
-    text_sum = one_side(scalars, text_unit, image_near, so_far=text_sum, name="text_near")
-    text_sum = one_side(scalars, text_unit, head_far, so_far=text_sum, name="text_far_head")
+    text_sum = one_side(scalars, text_unit, near_tail, so_far=text_sum, name="text_near_tail")
+    text_sum = one_side(scalars, text_unit, far_head, so_far=text_sum, name="text_far_head")
     text_grad = one_side(
-        scalars, text_unit, tail_far, so_far=text_sum, final=(sentence_vectors_raw, text_norm),
+        scalars, text_unit, far_tail, so_far=text_sum, final=(sentence_vectors_raw, text_norm),
         name="text_far_tail",
     )
     return (image_grad, text_grad)

time: 84.7 us -> 83.1 us (0.981)
  waiting for transfers between devices: 25.3 us -> 21.3 us
  starting transfers between devices: 15.6 us -> 17.5 us
    ppermute x5 -> x6, waiting for transfers between devices: 25.3 us -> 21.3 us  [swapped(): return lax.ppermute(x, AXES, pairs)]
    ppermute x5 -> x6, starting transfers between devices: 15.6 us -> 17.5 us  [swapped(): return lax.ppermute(x, AXES, pairs)]
    pallas_call x7 -> x8, Pallas kernels: 33.6 us -> 33.7 us  [one_side(): pl.pallas_call(kernel, in_specs=[IN_SMEM] + [IN_VMEM] * (len(args) - 1),...]
  transfers between devices with their start and end apart: 5 -> 6, of which waited for: 3 -> 5; matrix products, arithmetic and copies ran while one was open for 1% -> 1% of each run, Pallas kernels for 38% -> 39%
where the time goes in v3:
time: 83.1 us; the launch traced here: 82.7 us
  Pallas kernels  36 us (43%)
  waiting for transfers between devices  21.3 us (26%)
  starting transfers between devices  17.5 us (21%)
  local copies, waits for them, and re-layouts  5.51 us (7%)
  between operations  2.33 us (3%)
    pallas_call x8, Pallas kernels, one_side(): pl.pallas_call(kernel, in_specs=[IN_SMEM] + [IN_VMEM] * (len(args) - 1),...  33.7 us
    ppermute x6, waiting for transfers between devices, swapped(): return lax.ppermute(x, AXES, pairs)  21.3 us
    ppermute x6, starting transfers between devices, swapped(): return lax.ppermute(x, AXES, pairs)  17.5 us
    unnamed x20, local copies, waits for them, and re-layouts  4.43 us
    pallas_call x1, Pallas kernels, prepare(): pl.pallas_call(prepare_kernel, in_specs=[IN_VMEM, IN_VMEM], out_specs=[IN...  2.3 us
  transfers between devices with their start and end apart: 6, of which 5 were waited for; matrix products, arithmetic and copies ran while one was open for 1% of the time, Pallas kernels for 39%

profile of v3, /device:TPU:0, one launch (start us, length us, event | category | flops | bytes accessed | tf_op | source)
XLA Modules:
  0.0 82.7 jit_solution(1617939607915245225)
XLA Ops:
  0.6 2.1 %collective-permute-start.1 = (bf16[1024,768]{1,0:T(8,128)(2,1)}, bf16[1024,768]{1,0:T(8,128)(2,1)}, u32[]{:S(2)}, u32[]{:S(2)}) collective-permute-start(bf16[1024,768]{1,0:T(8,128)(2,1)} %refs_4_.3), channel_id=1, source_target_pairs={{0,1},{1,0},{2,3},{3,2},{4,5},{5,4},{6,7},{7,6},{8,9},{9,8},{10,11... | collective-permute-start | bytes 4718600 | tf_op jit(solution)/shard_map/ppermute | solution.py:24
  2.7 6.3 %collective-permute-start = (bf16[1024,768]{1,0:T(8,128)(2,1)}, bf16[1024,768]{1,0:T(8,128)(2,1)}, u32[]{:S(2)}, u32[]{:S(2)}) collective-permute-start(bf16[1024,768]{1,0:T(8,128)(2,1)} %refs_4_.3), channel_id=1, source_target_pairs={{1,2},{2,1},{3,4},{4,3},{5,6},{6,5},{7,8},{8,7},{9,10},{10,9},{11,... | collective-permute-start | bytes 4718600 | tf_op jit(solution)/shard_map/ppermute | solution.py:24
  9.0 1.4 %copy-done = bf16[1024,768]{1,0:T(8,128)(2,1)S(1)} copy-done((bf16[1024,768]{1,0:T(8,128)(2,1)S(1)}, bf16[1024,768]{1,0:T(8,128)(2,1)}, u32[]{:S(2)}) %copy-start) | copy-done | bytes 1572888
  10.4 1.4 %copy-done.2 = bf16[1024,768]{1,0:T(8,128)(2,1)S(1)} copy-done((bf16[1024,768]{1,0:T(8,128)(2,1)S(1)}, bf16[1024,768]{1,0:T(8,128)(2,1)}, u32[]{:S(2)}) %copy-start.2) | copy-done | bytes 1572888
  11.9 2.3 %prepare.1 = (bf16[1024,768]{1,0:T(8,128)(2,1)S(1)}, f32[1024,1]{1,0:T(8,128)S(1)}, bf16[1024,768]{1,0:T(8,128)(2,1)S(1)}, f32[1024,1]{1,0:T(8,128)S(1)}, bf16[5...) custom-call(bf16[1024,768]{1,0:T(8,128)(2,1)S(1)} %copy-done, ...), custom_call_target="tpu_custom_call" | custom-call | flops 6291456 | bytes 6291456 | tf_op jit(solution)/shard_map/prepare/pallas_call | solution.py:59
  14.2 0.8 copy-done.5
  14.9 0.8 copy-done.7
  15.7 0.8 %collective-permute-start.4 = (bf16[768,768]{1,0:T(8,128)(2,1)}, bf16[768,768]{1,0:T(8,128)(2,1)}, u32[]{:S(2)}, u32[]{:S(2)}) collective-permute-start(bf16[768,768]{1,0:T(8,128)(2,1)} %get-tuple-element.32), channel_id=1, source_target_pairs={{1,2},{2,1},{3,4},{4,3},{5,6},{6,5},{7,8},{8,7},{9,10},{10,9},{11,... | collective-permute-start | bytes 3538952 | tf_op jit(solution)/shard_map/ppermute | solution.py:24
  16.6 2.1 %collective-permute-start.5 = (bf16[512,768]{1,0:T(8,128)(2,1)}, bf16[512,768]{1,0:T(8,128)(2,1)}, u32[]{:S(2)}, u32[]{:S(2)}) collective-permute-start(bf16[512,768]{1,0:T(8,128)(2,1)} %get-tuple-element.33), channel_id=1, source_target_pairs={{0,1},{1,0},{2,3},{3,2},{4,5},{5,4},{6,7},{7,6},{8,9},{9,8},{10,11... | collective-permute-start | bytes 2359304 | tf_op jit(solution)/shard_map/ppermute | solution.py:24
  20.0 1.1 %copy.7.refs_3_ = s32[1024,1]{1,0:T(8,128)} copy(s32[1024,1]{0,1:T(1,128)S(1)} %bitcast.1) | data formatting | bytes 8192 | tf_op jit(solution)/shard_map/reshape | solution.py:199
  21.2 4.0 %text_own.1.refs_3_ = f32[1024,768]{1,0:T(8,128)S(1)} custom-call(f32[4]{0:T(128)S(1)} %pad_maximum_fusion.refs_0_, bf16[1024,768]{1,0:T(8,128)(2,1)S(1)} %get-tuple-element.20.refs_2_.refs_1_, bf16[1024,768]{1,0:T(8,128)(2,1)S(1)} %get-tuple-element.19.refs_1_.refs_2_, s32[1,1024]{1,0:T(1,128)S(1)} %copy-done.9), custom_call_target="tpu_custom_call" | custom-call | flops 786432 | bytes 786432 | tf_op jit(solution)/shard_map/text_own/pallas_call | solution.py:166
  25.3 4.1 %image_own.1.refs_3_ = f32[1024,768]{1,0:T(8,128)S(1)} custom-call(f32[4]{0:T(128)S(1)} %pad_maximum_fusion.refs_0_, bf16[1024,768]{1,0:T(8,128)(2,1)S(1)} %get-tuple-element.19.refs_1_.refs_2_, bf16[1024,768]{1,0:T(8,128)(2,1)S(1)} %get-tuple-element.20.refs_2_.refs_1_, s32[1024,1]{1,0:T(8,128)S(1)} %copy-done.4), custom_call_target="tpu_custom_call" | custom-call | flops 786432 | bytes 786432 | tf_op jit(solution)/shard_map/image_own/pallas_call | solution.py:166
  29.3 8.9 %collective-permute-done.1.refs_2_ = bf16[1024,768]{1,0:T(8,128)(2,1)} collective-permute-done((bf16[1024,768]{1,0:T(8,128)(2,1)}, bf16[1024,768]{1,0:T(8,128)(2,1)}, u32[]{:S(2)}, u32[]{:S(2)}) %collective-permute-start.1) | collective-permute-done | bytes 1572896 | tf_op jit(solution)/shard_map/ppermute | solution.py:24
  38.3 6.2 %collective-permute-start.3 = (bf16[256,768]{1,0:T(8,128)(2,1)S(1)}, bf16[256,768]{1,0:T(8,128)(2,1)S(1)}, u32[]{:S(2)}, u32[]{:S(2)}) collective-permute-start(bf16[256,768]{1,0:T(8,128)(2,1)S(1)} %get-tuple-element.31), channel_id=1, source_target_pairs={{1,2},{2,1},{3,4},{4,3},{5,6},{6,5},{7,8},{8,7},{9,10},{10,9},{11,... | collective-permute-start | bytes 1179656 | tf_op jit(solution)/shard_map/ppermute | solution.py:24
  44.5 5.2 %image_near.1.refs_3_ = f32[1024,768]{1,0:T(8,128)S(1)} custom-call(f32[4]{0:T(128)S(1)} %pad_maximum_fusion.refs_0_, bf16[1024,768]{1,0:T(8,128)(2,1)S(1)} %get-tuple-element.19.refs_1_.refs_2_, bf16[1024,768]{1,0:T(8,128)(2,1)} %collective-permute-done.1.refs_2_, f32[1024,768]{1,0:T(8,128)S(1)} %image_own.1.refs_3_), custom_call_target="tpu_custom_call" | custom-call | flops 786432 | bytes 786432 | tf_op jit(solution)/shard_map/image_near/pallas_call | solution.py:166
  49.7 5.4 %collective-permute-done.2.refs_2_ = bf16[512,768]{1,0:T(8,128)(2,1)} collective-permute-done((bf16[512,768]{1,0:T(8,128)(2,1)}, bf16[512,768]{1,0:T(8,128)(2,1)}, u32[]{:S(2)}, u32[]{:S(2)}) %collective-permute-start.2) | collective-permute-done | bytes 786464 | tf_op jit(solution)/shard_map/ppermute | solution.py:24
  55.1 3.0 %text_near_head.1.refs_3_ = f32[1024,768]{1,0:T(8,128)S(1)} custom-call(f32[4]{0:T(128)S(1)} %pad_maximum_fusion.refs_0_, bf16[1024,768]{1,0:T(8,128)(2,1)S(1)} %get-tuple-element.20.refs_2_.refs_1_, bf16[512,768]{1,0:T(8,128)(2,1)} %collective-permute-done.2.refs_2_, f32[1024,768]{1,0:T(8,128)S(1)} %text_own.1.refs_3_), custom_call_target="tpu_custom_call" | custom-call | flops 786432 | bytes 786432 | tf_op jit(solution)/shard_map/text_near_head/pallas_call | solution.py:166
  58.2 3.8 %collective-permute-done.refs_2_ = bf16[1024,768]{1,0:T(8,128)(2,1)} collective-permute-done((bf16[1024,768]{1,0:T(8,128)(2,1)}, bf16[1024,768]{1,0:T(8,128)(2,1)}, u32[]{:S(2)}, u32[]{:S(2)}) %collective-permute-start) | collective-permute-done | bytes 1572896 | tf_op jit(solution)/shard_map/ppermute | solution.py:24
  62.0 6.5 %image_far.1 = f32[1024,768]{1,0:T(8,128)} custom-call(f32[4]{0:T(128)S(1)} %pad_maximum_fusion.refs_0_, bf16[1024,768]{1,0:T(8,128)(2,1)S(1)} %get-tuple-element.19.refs_1_.refs_2_, bf16[1024,768]{1,0:T(8,128)(2,1)} %collective-permute-done.refs_2_, f32[1024,768]{1,0:T(8,128)S(1)} %image_near.1.refs_3_, bf16[1024,768]{1,0:T(8,128)(2,1)S(1)} %copy-done.1, ...), custom_call_target="tpu_custom_call" | custom-call | flops 786432 | bytes 786432 | tf_op jit(solution)/shard_map/image_far/pallas_call | solution.py:166
  68.5 2.6 %collective-permute-done.5.refs_2_ = bf16[512,768]{1,0:T(8,128)(2,1)} collective-permute-done((bf16[512,768]{1,0:T(8,128)(2,1)}, bf16[512,768]{1,0:T(8,128)(2,1)}, u32[]{:S(2)}, u32[]{:S(2)}) %collective-permute-start.5) | collective-permute-done | bytes 786464 | tf_op jit(solution)/shard_map/ppermute | solution.py:24
  71.1 3.0 %text_near_tail.1.refs_3_ = f32[1024,768]{1,0:T(8,128)S(1)} custom-call(f32[4]{0:T(128)S(1)} %pad_maximum_fusion.refs_0_, bf16[1024,768]{1,0:T(8,128)(2,1)S(1)} %get-tuple-element.20.refs_2_.refs_1_, bf16[512,768]{1,0:T(8,128)(2,1)} %collective-permute-done.5.refs_2_, f32[1024,768]{1,0:T(8,128)S(1)} %text_near_head.1.refs_3_), custom_call_target="tpu_custom_call" | custom-call | flops 786432 | bytes 786432 | tf_op jit(solution)/shard_map/text_near_tail/pallas_call | solution.py:166
  74.2 0.4 collective-permute-done.4.refs_2_
  74.6 4.4 %text_far_head.1.refs_3_ = f32[1024,768]{1,0:T(8,128)S(1)} custom-call(f32[4]{0:T(128)S(1)} %pad_maximum_fusion.refs_0_, bf16[1024,768]{1,0:T(8,128)(2,1)S(1)} %get-tuple-element.20.refs_2_.refs_1_, bf16[768,768]{1,0:T(8,128)(2,1)} %collective-permute-done.4.refs_2_, f32[1024,768]{1,0:T(8,128)S(1)} %text_near_tail.1.refs_3_), custom_call_target="tpu_custom_call" | custom-call | flops 786432 | bytes 786432 | tf_op jit(solution)/shard_map/text_far_head/pallas_call | solution.py:166
  79.1 3.5 %text_far_tail.1 = f32[1024,768]{1,0:T(8,128)} custom-call(f32[4]{0:T(128)S(1)} %pad_maximum_fusion.refs_0_, bf16[1024,768]{1,0:T(8,128)(2,1)S(1)} %get-tuple-element.20.refs_2_.refs_1_, bf16[256,768]{1,0:T(8,128)(2,1)S(1)} %collective-permute-done.3.refs_2_, f32[1024,768]{1,0:T(8,128)S(1)} %text_far_head.1.refs_3_, bf16[1024,768]{1,0:T(8,128)(2,1)S(1)} %copy-done.3, ...), custom_call_target="tpu_custom_call" | custom-call | flops 786432 | bytes 786432 | tf_op jit(solution)/shard_map/text_far_tail/pallas_call | solution.py:166
  (19 shorter events, 0.1 us)
Async XLA Ops:
  0.6 37.6 %collective-permute-start.1 = (bf16[1024,768]{1,0:T(8,128)(2,1)}, bf16[1024,768]{1,0:T(8,128)(2,1)}, u32[]{:S(2)}, u32[]{:S(2)}) collective-permute-start(bf16[1024,768]{1,0:T(8,128)(2,1)} %refs_4_.3), channel_id=1, source_target_pairs={{0,1},{1,0},{2,3},{3,2},{4,5},{5,4},{6,7},{7,6},{8,9},{9,8},{10,11... | collective-permute-start | bytes 4718600 | tf_op jit(solution)/shard_map/ppermute | solution.py:24
  2.7 59.3 %collective-permute-start = (bf16[1024,768]{1,0:T(8,128)(2,1)}, bf16[1024,768]{1,0:T(8,128)(2,1)}, u32[]{:S(2)}, u32[]{:S(2)}) collective-permute-start(bf16[1024,768]{1,0:T(8,128)(2,1)} %refs_4_.3), channel_id=1, source_target_pairs={{1,2},{2,1},{3,4},{4,3},{5,6},{6,5},{7,8},{8,7},{9,10},{10,9},{11,... | collective-permute-start | bytes 4718600 | tf_op jit(solution)/shard_map/ppermute | solution.py:24
  9.0 1.4 %copy-start = (bf16[1024,768]{1,0:T(8,128)(2,1)S(1)}, bf16[1024,768]{1,0:T(8,128)(2,1)}, u32[]{:S(2)}) copy-start(bf16[1024,768]{1,0:T(8,128)(2,1)} %refs_4_.2) | copy-start | bytes 4718596
  10.4 1.4 %copy-start.2 = (bf16[1024,768]{1,0:T(8,128)(2,1)S(1)}, bf16[1024,768]{1,0:T(8,128)(2,1)}, u32[]{:S(2)}) copy-start(bf16[1024,768]{1,0:T(8,128)(2,1)} %refs_4_.3) | copy-start | bytes 4718596
  11.9 8.2 %copy-start.9 = (s32[1,1024]{1,0:T(1,128)S(1)}, s32[1,1024]{1,0:T(1,128)}, u32[]{:S(2)}) copy-start(s32[1,1024]{1,0:T(1,128)} %refs_3_.1) | copy-start | bytes 12292
  14.2 0.8 copy-start.5
  14.9 0.8 copy-start.7
  15.7 58.9 %collective-permute-start.4 = (bf16[768,768]{1,0:T(8,128)(2,1)}, bf16[768,768]{1,0:T(8,128)(2,1)}, u32[]{:S(2)}, u32[]{:S(2)}) collective-permute-start(bf16[768,768]{1,0:T(8,128)(2,1)} %get-tuple-element.32), channel_id=1, source_target_pairs={{1,2},{2,1},{3,4},{4,3},{5,6},{6,5},{7,8},{8,7},{9,10},{10,9},{11,... | collective-permute-start | bytes 3538952 | tf_op jit(solution)/shard_map/ppermute | solution.py:24
  16.6 38.5 %collective-permute-start.2 = (bf16[512,768]{1,0:T(8,128)(2,1)}, bf16[512,768]{1,0:T(8,128)(2,1)}, u32[]{:S(2)}, u32[]{:S(2)}) collective-permute-start(bf16[512,768]{1,0:T(8,128)(2,1)} %get-tuple-element.25), channel_id=1, source_target_pairs={{0,1},{1,0},{2,3},{3,2},{4,5},{5,4},{6,7},{7,6},{8,9},{9,8},{10,11... | collective-permute-start | bytes 2359304 | tf_op jit(solution)/shard_map/ppermute | solution.py:24
  16.6 54.5 %collective-permute-start.5 = (bf16[512,768]{1,0:T(8,128)(2,1)}, bf16[512,768]{1,0:T(8,128)(2,1)}, u32[]{:S(2)}, u32[]{:S(2)}) collective-permute-start(bf16[512,768]{1,0:T(8,128)(2,1)} %get-tuple-element.33), channel_id=1, source_target_pairs={{0,1},{1,0},{2,3},{3,2},{4,5},{5,4},{6,7},{7,6},{8,9},{9,8},{10,11... | collective-permute-start | bytes 2359304 | tf_op jit(solution)/shard_map/ppermute | solution.py:24
  21.2 4.1 %copy-start.4 = (s32[1024,1]{1,0:T(8,128)S(1)}, s32[1024,1]{1,0:T(8,128)}, u32[]{:S(2)}) copy-start(s32[1024,1]{1,0:T(8,128)} %copy.7.refs_3_) | copy-start | bytes 12292
  38.3 40.8 %collective-permute-start.3 = (bf16[256,768]{1,0:T(8,128)(2,1)S(1)}, bf16[256,768]{1,0:T(8,128)(2,1)S(1)}, u32[]{:S(2)}, u32[]{:S(2)}) collective-permute-start(bf16[256,768]{1,0:T(8,128)(2,1)S(1)} %get-tuple-element.31), channel_id=1, source_target_pairs={{1,2},{2,1},{3,4},{4,3},{5,6},{6,5},{7,8},{8,7},{9,10},{10,9},{11,... | collective-permute-start | bytes 1179656 | tf_op jit(solution)/shard_map/ppermute | solution.py:24
  49.7 12.3 %copy-start.1 = (bf16[1024,768]{1,0:T(8,128)(2,1)S(1)}, bf16[1024,768]{1,0:T(8,128)(2,1)}, u32[]{:S(2)}) copy-start(bf16[1024,768]{1,0:T(8,128)(2,1)} %refs_4_.2) | copy-start | bytes 4718596
  49.7 12.3 %copy-start.6 = (f32[1024,1]{1,0:T(8,128)S(1)}, f32[1024,1]{1,0:T(8,128)}, u32[]{:S(2)}) copy-start(f32[1024,1]{1,0:T(8,128)} %copy-done.5) | copy-start | bytes 12292
  74.2 4.9 %copy-start.3 = (bf16[1024,768]{1,0:T(8,128)(2,1)S(1)}, bf16[1024,768]{1,0:T(8,128)(2,1)}, u32[]{:S(2)}) copy-start(bf16[1024,768]{1,0:T(8,128)(2,1)} %refs_4_.3) | copy-start | bytes 4718596
  74.2 4.9 %copy-start.8 = (f32[1024,1]{1,0:T(8,128)S(1)}, f32[1024,1]{1,0:T(8,128)}, u32[]{:S(2)}) copy-start(f32[1024,1]{1,0:T(8,128)} %copy-done.7) | copy-start | bytes 12292

commit v4 on v3

--- a/solution.py
+++ b/solution.py
@@ -12,6 +12,7 @@
 VMEM_LIMIT = 24 * 2**20
 NEAR_LAST, FAR_LAST = 2, 4
 IN_VMEM = pl.BlockSpec(memory_space=pltpu.VMEM)
+ANYWHERE = pl.BlockSpec(memory_space=pl.ANY)
 IN_SMEM = pl.BlockSpec(memory_space=pltpu.SMEM)
 
 
@@ -69,7 +70,7 @@
     )(image, text)
 
 
-def side_kernel(*refs, label, raw_other, has_sum, final, step, chunk):
+def side_kernel(*refs, label, raw_other, has_sum, final, late, step, chunk):
     refs = list(refs)
     scalars, own_ref, other_ref = refs[:3]
     refs = refs[3:]
@@ -86,7 +87,12 @@
     else:
         unit_ref = other_ref
     if final:
-        grad_ref, sem = refs
+        grad_ref, sem = refs[:2]
+    if late:
+        late_ref, late_sem = refs[2:]
+        fetch = pltpu.make_async_copy(raw_ref, late_ref, late_sem)
+        fetch.start()
+        raw_ref = late_ref
     slope, shift, floor, log_floor = (scalars[i] for i in range(4))
 
     def scores(r):
@@ -127,6 +133,8 @@
         total = jnp.dot(tile, unit_ref[...], preferred_element_type=jnp.float32)
         if has_sum:
             total = total + sum_ref[at, :]
+        if late and r == 0:
+            fetch.wait()
         if final:
             norm = norm_ref[at, :]
             unit = raw_ref[at, :].astype(jnp.float32) * norm
@@ -142,8 +150,8 @@
 
 
 def one_side(
-    scalars, own, other, pair=None, label=None, raw_other=False, so_far=None, final=None, step=256,
-    chunk=256, name="side",
+    scalars, own, other, pair=None, label=None, raw_other=False, so_far=None, final=None, late=False,
+    step=256, chunk=256, name="side",
 ):
     rows, width = own.shape
     count = other.shape[0]
@@ -155,20 +163,25 @@
     scratch = []
     if raw_other:
         scratch.append(pltpu.VMEM((count, width), jnp.bfloat16))
+    specs = [IN_SMEM] + [IN_VMEM] * (len(args) - 1)
     if final is not None:
         args += list(final)
+        specs += [ANYWHERE if late else IN_VMEM, IN_VMEM]
         scratch.append(pltpu.VMEM((rows, width), jnp.float32))
         scratch.append(pltpu.SemaphoreType.DMA((rows // step,)))
+    if late:
+        scratch += [pltpu.VMEM((rows, width), jnp.bfloat16), pltpu.SemaphoreType.DMA]
     kernel = functools.partial(
         side_kernel, label=label, raw_other=raw_other, has_sum=so_far is not None,
-        final=final is not None, step=step, chunk=min(chunk, count),
+        final=final is not None, late=late, step=step, chunk=min(chunk, count),
     )
     return pl.pallas_call(
         kernel,
-        in_specs=[IN_SMEM] + [IN_VMEM] * (len(args) - 1),
-        out_specs=IN_VMEM if final is None else pl.BlockSpec(memory_space=pl.ANY),
+        in_specs=specs,
+        out_specs=IN_VMEM if final is None else ANYWHERE,
         out_shape=jax.ShapeDtypeStruct((rows, width), jnp.float32),
         scratch_shapes=scratch,
+        input_output_aliases={len(args) - 1: 0} if so_far is not None and final is None else {},
         compiler_params=pltpu.CompilerParams(vmem_limit_bytes=VMEM_LIMIT),
         cost_estimate=pl.CostEstimate(
             flops=rows * width, bytes_accessed=rows * width, transcendentals=0
@@ -191,24 +204,27 @@
     image_unit, image_norm, text_unit, text_norm, *parts = prepare(
         photo_vectors_raw, sentence_vectors_raw
     )
-    near_head, near_tail = (swapped(part, 0) for part in parts[:2])
-    far_head = swapped(parts[2], 1)
-
     text_sum = one_side(scalars, text_unit, image_unit, companion_index, "row", name="text_own")
+    text_sum, near_part, image_unit = lax.optimization_barrier((text_sum, parts[0], image_unit))
+    near_head = swapped(near_part, 0)
     image_sum = one_side(
         scalars, image_unit, text_unit, companion_index.reshape(rows, 1), "column", name="image_own"
     )
-    image_sum, text_sum, far_part = lax.optimization_barrier((image_sum, text_sum, parts[3]))
-    far_tail = swapped(far_part, 1)
+    image_sum, far_part = lax.optimization_barrier((image_sum, parts[2]))
+    far_head = swapped(far_part, 1)
     image_sum = one_side(
         scalars, image_unit, text_near, raw_other=True, so_far=image_sum, name="image_near"
     )
-    image_sum, text_sum = lax.optimization_barrier((image_sum, text_sum))
+    image_sum, text_sum, near_part, far_part = lax.optimization_barrier(
+        (image_sum, text_sum, parts[1], parts[3])
+    )
+    near_tail = swapped(near_part, 0)
+    far_tail = swapped(far_part, 1)
     text_sum = one_side(scalars, text_unit, near_head, so_far=text_sum, name="text_near_head")
     image_sum, text_sum = lax.optimization_barrier((image_sum, text_sum))
     image_grad = one_side(
         scalars, image_unit, text_far, raw_other=True, so_far=image_sum,
-        final=(photo_vectors_raw, image_norm), name="image_far",
+        final=(photo_vectors_raw, image_norm), late=True, name="image_far",
     )
     image_grad, text_sum = lax.optimization_barrier((image_grad, text_sum))
     text_sum = one_side(scalars, text_unit, near_tail, so_far=text_sum, name="text_near_tail")

time: 83.1 us -> 82.7 us (level)
  local copies, waits for them, and re-layouts: 5.51 us -> 9.45 us
  starting transfers between devices: 17.5 us -> 15.8 us
  waiting for transfers between devices: 21.3 us -> 19.9 us
  Pallas kernels: 36 us -> 34.8 us
    unnamed x20 -> x44, local copies, waits for them, and re-layouts: 4.43 us -> 8.44 us
    ppermute x6, starting transfers between devices: 17.5 us -> 15.8 us  [swapped(): return lax.ppermute(x, AXES, pairs)]
    ppermute x6, waiting for transfers between devices: 21.3 us -> 19.9 us  [swapped(): return lax.ppermute(x, AXES, pairs)]
    pallas_call x1, Pallas kernels: 2.3 us -> 1.06 us  [prepare(): pl.pallas_call(prepare_kernel, in_specs=[IN_VMEM, IN_VMEM], out_specs=[IN...]
  transfers between devices with their start and end apart: 6 -> 6, of which waited for: 5 -> 6; matrix products, arithmetic and copies ran while one was open for 1% -> 1% of each run, Pallas kernels for 39% -> 38%
where the time goes in v4:
time: 82.7 us; the launch traced here: 82.3 us
  Pallas kernels  34.8 us (42%)
  waiting for transfers between devices  19.9 us (24%)
  starting transfers between devices  15.8 us (19%)
  local copies, waits for them, and re-layouts  9.45 us (11%)
  between operations  2.42 us (3%)
    pallas_call x8, Pallas kernels, one_side(): pl.pallas_call(kernel, in_specs=specs, out_specs=IN_VMEM if final is None...  33.7 us
    ppermute x6, waiting for transfers between devices, swapped(): return lax.ppermute(x, AXES, pairs)  19.9 us
    ppermute x6, starting transfers between devices, swapped(): return lax.ppermute(x, AXES, pairs)  15.8 us
    unnamed x44, local copies, waits for them, and re-layouts  8.44 us
  transfers between devices with their start and end apart: 6, of which 6 were waited for; matrix products, arithmetic and copies ran while one was open for 1% of the time, Pallas kernels for 38%

profile of v4, /device:TPU:0, one launch (start us, length us, event | category | flops | bytes accessed | tf_op | source)
XLA Modules:
  0.0 82.3 jit_solution(1063806978580005832)
XLA Ops:
  0.6 2.1 %collective-permute-start.1 = (bf16[1024,768]{1,0:T(8,128)(2,1)}, bf16[1024,768]{1,0:T(8,128)(2,1)}, u32[]{:S(2)}, u32[]{:S(2)}) collective-permute-start(bf16[1024,768]{1,0:T(8,128)(2,1)} %refs_4_.3), channel_id=1, source_target_pairs={{0,1},{1,0},{2,3},{3,2},{4,5},{5,4},{6,7},{7,6},{8,9},{9,8},{10,11... | collective-permute-start | bytes 4718600 | tf_op jit(solution)/shard_map/ppermute | solution.py:25
  2.7 6.3 %collective-permute-start = (bf16[1024,768]{1,0:T(8,128)(2,1)}, bf16[1024,768]{1,0:T(8,128)(2,1)}, u32[]{:S(2)}, u32[]{:S(2)}) collective-permute-start(bf16[1024,768]{1,0:T(8,128)(2,1)} %refs_4_.3), channel_id=1, source_target_pairs={{1,2},{2,1},{3,4},{4,3},{5,6},{6,5},{7,8},{8,7},{9,10},{10,9},{11,... | collective-permute-start | bytes 4718600 | tf_op jit(solution)/shard_map/ppermute | solution.py:25
  10.4 1.4 %copy-done.6 = bf16[1024,768]{1,0:T(8,128)(2,1)S(1)} copy-done((bf16[1024,768]{1,0:T(8,128)(2,1)S(1)}, bf16[1024,768]{1,0:T(8,128)(2,1)}, u32[]{:S(2)}) %copy-start.6) | copy-done | bytes 1572888
  11.8 1.4 %copy-done.8 = bf16[1024,768]{1,0:T(8,128)(2,1)S(1)} copy-done((bf16[1024,768]{1,0:T(8,128)(2,1)S(1)}, bf16[1024,768]{1,0:T(8,128)(2,1)}, u32[]{:S(2)}) %copy-start.8) | copy-done | bytes 1572888
  13.2 1.1 %prepare.1 = (bf16[1024,768]{1,0:T(8,128)(2,1)S(1)}, f32[1024,1]{1,0:T(8,128)S(1)}, bf16[1024,768]{1,0:T(8,128)(2,1)S(1)}, f32[1024,1]{1,0:T(8,128)S(1)}, bf16[5...) custom-call(bf16[1024,768]{1,0:T(8,128)(2,1)S(1)} %copy-done.6, ...), custom_call_target="tpu_custom_call" | custom-call | flops 6291456 | bytes 6291456 | tf_op jit(solution)/shard_map/prepare/pallas_call | solution.py:60
  16.1 4.0 %text_own.1.refs_3_ = f32[1024,768]{1,0:T(8,128)S(1)} custom-call(f32[4]{0:T(128)S(1)} %pad_maximum_fusion.refs_0_, bf16[1024,768]{1,0:T(8,128)(2,1)S(1)} %get-tuple-element.23.refs_1_.refs_2_, bf16[1024,768]{1,0:T(8,128)(2,1)S(1)} %get-tuple-element.26.refs_2_.refs_1_, s32[1,1024]{1,0:T(1,128)S(1)} %copy-done.15), custom_call_target="tpu_custom_call" | custom-call | flops 786432 | bytes 786432 | tf_op jit(solution)/shard_map/text_own/pallas_call | solution.py:178
  20.2 1.0 %copy.11.refs_3_ = s32[1024,1]{1,0:T(8,128)} copy(s32[1024,1]{0,1:T(1,128)S(1)} %bitcast.1) | data formatting | bytes 8192 | tf_op jit(solution)/shard_map/reshape | solution.py:211
  21.3 1.4 %copy-done.1 = bf16[1024,768]{1,0:T(8,128)(2,1)S(1)} copy-done((bf16[1024,768]{1,0:T(8,128)(2,1)S(1)}, bf16[1024,768]{1,0:T(8,128)(2,1)}, u32[]{:S(2)}) %copy-start.1) | copy-done | bytes 1572888
  22.7 1.4 %copy-done.4 = bf16[1024,768]{1,0:T(8,128)(2,1)S(1)} copy-done((bf16[1024,768]{1,0:T(8,128)(2,1)S(1)}, bf16[1024,768]{1,0:T(8,128)(2,1)}, u32[]{:S(2)}) %copy-start.4) | copy-done | bytes 1572888
  24.1 1.0 %copy-done.10 = s32[1024,1]{1,0:T(8,128)S(1)} copy-done((s32[1024,1]{1,0:T(8,128)S(1)}, s32[1024,1]{1,0:T(8,128)}, u32[]{:S(2)}) %copy-start.10) | copy-done | bytes 4120
  25.1 4.1 %image_own.1.refs_3_ = f32[1024,768]{1,0:T(8,128)S(1)} custom-call(f32[4]{0:T(128)S(1)} %pad_maximum_fusion.refs_0_, bf16[1024,768]{1,0:T(8,128)(2,1)S(1)} %copy-done.4, bf16[1024,768]{1,0:T(8,128)(2,1)S(1)} %copy-done.1, s32[1024,1]{1,0:T(8,128)S(1)} %copy-done.10), custom_call_target="tpu_custom_call" | custom-call | flops 786432 | bytes 786432 | tf_op jit(solution)/shard_map/image_own/pallas_call | solution.py:178
  29.2 0.9 %collective-permute-start.4 = (bf16[768,768]{1,0:T(8,128)(2,1)S(1)}, bf16[768,768]{1,0:T(8,128)(2,1)S(1)}, u32[]{:S(2)}, u32[]{:S(2)}) collective-permute-start(bf16[768,768]{1,0:T(8,128)(2,1)S(1)} %copy-done.17), channel_id=1, source_target_pairs={{1,2},{2,1},{3,4},{4,3},{5,6},{6,5},{7,8},{8,7},{9,10},{10,9},{11,... | collective-permute-start | bytes 3538952 | tf_op jit(solution)/shard_map/ppermute | solution.py:25
  30.2 8.1 %collective-permute-done.1.refs_2_ = bf16[1024,768]{1,0:T(8,128)(2,1)} collective-permute-done((bf16[1024,768]{1,0:T(8,128)(2,1)}, bf16[1024,768]{1,0:T(8,128)(2,1)}, u32[]{:S(2)}, u32[]{:S(2)}) %collective-permute-start.1) | collective-permute-done | bytes 1572896 | tf_op jit(solution)/shard_map/ppermute | solution.py:25
  38.3 5.4 %image_near.1.refs_3_ = f32[1024,768]{1,0:T(8,128)S(1)} custom-call(f32[4]{0:T(128)S(1)} %pad_maximum_fusion.refs_0_, bf16[1024,768]{1,0:T(8,128)(2,1)S(1)} %copy-done.4, bf16[1024,768]{1,0:T(8,128)(2,1)} %collective-permute-done.1.refs_2_, f32[1024,768]{1,0:T(8,128)S(1)} %image_own.1.refs_3_), custom_call_target="tpu_custom_call", output_to_operand_aliasing={{}: (3, {})} | custom-call | flops 786432 | bytes 786432 | tf_op jit(solution)/shard_map/image_near/pallas_call | solution.py:178
  43.8 2.1 %collective-permute-start.5 = (bf16[512,768]{1,0:T(8,128)(2,1)S(1)}, bf16[512,768]{1,0:T(8,128)(2,1)S(1)}, u32[]{:S(2)}, u32[]{:S(2)}) collective-permute-start(bf16[512,768]{1,0:T(8,128)(2,1)S(1)} %copy-done.19), channel_id=1, source_target_pairs={{0,1},{1,0},{2,3},{3,2},{4,5},{5,4},{6,7},{7,6},{8,9},{9,8},{10,11... | collective-permute-start | bytes 2359304 | tf_op jit(solution)/shard_map/ppermute | solution.py:25
  45.9 4.3 %collective-permute-start.3 = (bf16[256,768]{1,0:T(8,128)(2,1)S(1)}, bf16[256,768]{1,0:T(8,128)(2,1)S(1)}, u32[]{:S(2)}, u32[]{:S(2)}) collective-permute-start(bf16[256,768]{1,0:T(8,128)(2,1)S(1)} %get-tuple-element.39), channel_id=1, source_target_pairs={{1,2},{2,1},{3,4},{4,3},{5,6},{6,5},{7,8},{8,7},{9,10},{10,9},{11,... | collective-permute-start | bytes 1179656 | tf_op jit(solution)/shard_map/ppermute | solution.py:25
  50.2 4.8 %collective-permute-done.2.refs_2_ = bf16[512,768]{1,0:T(8,128)(2,1)S(1)} collective-permute-done((bf16[512,768]{1,0:T(8,128)(2,1)S(1)}, bf16[512,768]{1,0:T(8,128)(2,1)S(1)}, u32[]{:S(2)}, u32[]{:S(2)}) %collective-permute-start.2) | collective-permute-done | bytes 786464 | tf_op jit(solution)/shard_map/ppermute | solution.py:25
  55.0 2.8 %text_near_head.1.refs_3_ = f32[1024,768]{1,0:T(8,128)S(1)} custom-call(f32[4]{0:T(128)S(1)} %pad_maximum_fusion.refs_0_, bf16[1024,768]{1,0:T(8,128)(2,1)S(1)} %copy-done.2, bf16[512,768]{1,0:T(8,128)(2,1)S(1)} %collective-permute-done.2.refs_2_, f32[1024,768]{1,0:T(8,128)S(1)} %text_own.1.refs_3_), custom_call_target="tpu_custom_call", output_to_operand_aliasing={{}: (3, {})} | custom-call | flops 786432 | bytes 786432 | tf_op jit(solution)/shard_map/text_near_head/pallas_call | solution.py:178
  57.8 4.2 %collective-permute-done.refs_2_ = bf16[1024,768]{1,0:T(8,128)(2,1)} collective-permute-done((bf16[1024,768]{1,0:T(8,128)(2,1)}, bf16[1024,768]{1,0:T(8,128)(2,1)}, u32[]{:S(2)}, u32[]{:S(2)}) %collective-permute-start) | collective-permute-done | bytes 1572896 | tf_op jit(solution)/shard_map/ppermute | solution.py:25
  62.0 7.6 %image_far.1 = f32[1024,768]{1,0:T(8,128)} custom-call(f32[4]{0:T(128)S(1)} %pad_maximum_fusion.refs_0_, bf16[1024,768]{1,0:T(8,128)(2,1)S(1)} %copy-done.5, bf16[1024,768]{1,0:T(8,128)(2,1)} %collective-permute-done.refs_2_, f32[1024,768]{1,0:T(8,128)S(1)} %image_near.1.refs_3_, bf16[1024,768]{1,0:T(8,128)(2,1)S(1)} %copy-done.7, f32[1024,1]{1,0:T(8,128)S(1)} %copy-done.12), custom_call_target="tpu_custom_call" | custom-call | flops 786432 | bytes 786432 | tf_op jit(solution)/shard_map/image_far/pallas_call | solution.py:178
  69.6 1.4 %collective-permute-done.5.refs_2_ = bf16[512,768]{1,0:T(8,128)(2,1)S(1)} collective-permute-done((bf16[512,768]{1,0:T(8,128)(2,1)S(1)}, bf16[512,768]{1,0:T(8,128)(2,1)S(1)}, u32[]{:S(2)}, u32[]{:S(2)}) %collective-permute-start.5) | collective-permute-done | bytes 786464 | tf_op jit(solution)/shard_map/ppermute | solution.py:25
  71.0 2.8 %text_near_tail.1.refs_3_ = f32[1024,768]{1,0:T(8,128)S(1)} custom-call(f32[4]{0:T(128)S(1)} %pad_maximum_fusion.refs_0_, bf16[1024,768]{1,0:T(8,128)(2,1)S(1)} %copy-done.2, bf16[512,768]{1,0:T(8,128)(2,1)S(1)} %collective-permute-done.5.refs_2_, f32[1024,768]{1,0:T(8,128)S(1)} %text_near_head.1.refs_3_), custom_call_target="tpu_custom_call", output_to_operand_aliasing={{}: (3, {})} | custom-call | flops 786432 | bytes 786432 | tf_op jit(solution)/shard_map/text_near_tail/pallas_call | solution.py:178
  74.5 3.6 %text_far_head.1.refs_3_ = f32[1024,768]{1,0:T(8,128)S(1)} custom-call(f32[4]{0:T(128)S(1)} %pad_maximum_fusion.refs_0_, bf16[1024,768]{1,0:T(8,128)(2,1)S(1)} %copy-done.2, bf16[768,768]{1,0:T(8,128)(2,1)S(1)} %collective-permute-done.4.refs_2_, f32[1024,768]{1,0:T(8,128)S(1)} %text_near_tail.1.refs_3_), custom_call_target="tpu_custom_call", output_to_operand_aliasing={{}: (3, {})} | custom-call | flops 786432 | bytes 786432 | tf_op jit(solution)/shard_map/text_far_head/pallas_call | solution.py:178
  78.8 3.4 %text_far_tail.1 = f32[1024,768]{1,0:T(8,128)} custom-call(f32[4]{0:T(128)S(1)} %pad_maximum_fusion.refs_0_, bf16[1024,768]{1,0:T(8,128)(2,1)S(1)} %copy-done.2, bf16[256,768]{1,0:T(8,128)(2,1)S(1)} %collective-permute-done.3.refs_2_, f32[1024,768]{1,0:T(8,128)S(1)} %text_far_head.1.refs_3_, bf16[1024,768]{1,0:T(8,128)(2,1)S(1)} %copy-done.9, ...), custom_call_target="tpu_custom_call" | custom-call | flops 786432 | bytes 786432 | tf_op jit(solution)/shard_map/text_far_tail/pallas_call | solution.py:178
  (43 shorter events, 3.2 us)
Async XLA Ops:
  0.6 15.5 %copy-start.15 = (s32[1,1024]{1,0:T(1,128)S(1)}, s32[1,1024]{1,0:T(1,128)}, u32[]{:S(2)}) copy-start(s32[1,1024]{1,0:T(1,128)} %refs_3_.1) | copy-start | bytes 12292
  0.6 37.6 %collective-permute-start.1 = (bf16[1024,768]{1,0:T(8,128)(2,1)}, bf16[1024,768]{1,0:T(8,128)(2,1)}, u32[]{:S(2)}, u32[]{:S(2)}) collective-permute-start(bf16[1024,768]{1,0:T(8,128)(2,1)} %refs_4_.3), channel_id=1, source_target_pairs={{0,1},{1,0},{2,3},{3,2},{4,5},{5,4},{6,7},{7,6},{8,9},{9,8},{10,11... | collective-permute-start | bytes 4718600 | tf_op jit(solution)/shard_map/ppermute | solution.py:25
  2.7 59.3 %collective-permute-start = (bf16[1024,768]{1,0:T(8,128)(2,1)}, bf16[1024,768]{1,0:T(8,128)(2,1)}, u32[]{:S(2)}, u32[]{:S(2)}) collective-permute-start(bf16[1024,768]{1,0:T(8,128)(2,1)} %refs_4_.3), channel_id=1, source_target_pairs={{1,2},{2,1},{3,4},{4,3},{5,6},{6,5},{7,8},{8,7},{9,10},{10,9},{11,... | collective-permute-start | bytes 4718600 | tf_op jit(solution)/shard_map/ppermute | solution.py:25
  10.4 1.4 %copy-start.6 = (bf16[1024,768]{1,0:T(8,128)(2,1)S(1)}, bf16[1024,768]{1,0:T(8,128)(2,1)}, u32[]{:S(2)}) copy-start(bf16[1024,768]{1,0:T(8,128)(2,1)} %refs_4_.2) | copy-start | bytes 4718596
  11.8 1.4 %copy-start.8 = (bf16[1024,768]{1,0:T(8,128)(2,1)S(1)}, bf16[1024,768]{1,0:T(8,128)(2,1)}, u32[]{:S(2)}) copy-start(bf16[1024,768]{1,0:T(8,128)(2,1)} %refs_4_.3) | copy-start | bytes 4718596
  16.0 4.2 %copy-start = (bf16[1024,768]{1,0:T(8,128)(2,1)}, bf16[1024,768]{1,0:T(8,128)(2,1)S(1)}, u32[]{:S(2)}) copy-start(bf16[1024,768]{1,0:T(8,128)(2,1)S(1)} %get-tuple-element.23.refs_1_.refs_2_) | copy-start | bytes 4718596
  16.0 4.2 %copy-start.3 = (bf16[1024,768]{1,0:T(8,128)(2,1)}, bf16[1024,768]{1,0:T(8,128)(2,1)S(1)}, u32[]{:S(2)}) copy-start(bf16[1024,768]{1,0:T(8,128)(2,1)S(1)} %get-tuple-element.26.refs_2_.refs_1_) | copy-start | bytes 4718596
  16.0 4.2 %copy-start.13 = (f32[1024,1]{1,0:T(8,128)}, f32[1024,1]{1,0:T(8,128)S(1)}, u32[]{:S(2)}) copy-start(f32[1024,1]{1,0:T(8,128)S(1)} %get-tuple-element.43.refs_5_) | copy-start | bytes 12292
  16.0 4.2 %copy-start.16 = (bf16[768,768]{1,0:T(8,128)(2,1)}, bf16[768,768]{1,0:T(8,128)(2,1)S(1)}, u32[]{:S(2)}) copy-start(bf16[768,768]{1,0:T(8,128)(2,1)S(1)} %get-tuple-element.40) | copy-start | bytes 3538948
  16.0 4.2 %copy-start.18 = (bf16[512,768]{1,0:T(8,128)(2,1)}, bf16[512,768]{1,0:T(8,128)(2,1)S(1)}, u32[]{:S(2)}) copy-start(bf16[512,768]{1,0:T(8,128)(2,1)S(1)} %get-tuple-element.41) | copy-start | bytes 2359300
  21.3 1.4 %copy-start.1 = (bf16[1024,768]{1,0:T(8,128)(2,1)S(1)}, bf16[1024,768]{1,0:T(8,128)(2,1)}, u32[]{:S(2)}) copy-start(bf16[1024,768]{1,0:T(8,128)(2,1)} %copy-done) | copy-start | bytes 4718596
  25.1 4.1 %copy-start.17 = (bf16[768,768]{1,0:T(8,128)(2,1)S(1)}, bf16[768,768]{1,0:T(8,128)(2,1)}, u32[]{:S(2)}) copy-start(bf16[768,768]{1,0:T(8,128)(2,1)} %copy-done.16) | copy-start | bytes 3538948
  25.1 5.0 %copy-start.21 = (bf16[512,768]{1,0:T(8,128)(2,1)S(1)}, bf16[512,768]{1,0:T(8,128)(2,1)}, u32[]{:S(2)}) copy-start(bf16[512,768]{1,0:T(8,128)(2,1)} %copy-done.20) | copy-start | bytes 2359300
  29.2 14.5 %copy-start.19 = (bf16[512,768]{1,0:T(8,128)(2,1)S(1)}, bf16[512,768]{1,0:T(8,128)(2,1)}, u32[]{:S(2)}) copy-start(bf16[512,768]{1,0:T(8,128)(2,1)} %copy-done.18) | copy-start | bytes 2359300
  29.2 25.8 %copy-start.2 = (bf16[1024,768]{1,0:T(8,128)(2,1)S(1)}, bf16[1024,768]{1,0:T(8,128)(2,1)}, u32[]{:S(2)}) copy-start(bf16[1024,768]{1,0:T(8,128)(2,1)} %copy-done) | copy-start | bytes 4718596
  29.2 45.3 %collective-permute-start.4 = (bf16[768,768]{1,0:T(8,128)(2,1)S(1)}, bf16[768,768]{1,0:T(8,128)(2,1)S(1)}, u32[]{:S(2)}, u32[]{:S(2)}) collective-permute-start(bf16[768,768]{1,0:T(8,128)(2,1)S(1)} %copy-done.17), channel_id=1, source_target_pairs={{1,2},{2,1},{3,4},{4,3},{5,6},{6,5},{7,8},{8,7},{9,10},{10,9},{11,... | collective-permute-start | bytes 3538952 | tf_op jit(solution)/shard_map/ppermute | solution.py:25
  30.2 24.9 %collective-permute-start.2 = (bf16[512,768]{1,0:T(8,128)(2,1)S(1)}, bf16[512,768]{1,0:T(8,128)(2,1)S(1)}, u32[]{:S(2)}, u32[]{:S(2)}) collective-permute-start(bf16[512,768]{1,0:T(8,128)(2,1)S(1)} %copy-done.21), channel_id=1, source_target_pairs={{0,1},{1,0},{2,3},{3,2},{4,5},{5,4},{6,7},{7,6},{8,9},{9,8},{10,11... | collective-permute-start | bytes 2359304 | tf_op jit(solution)/shard_map/ppermute | solution.py:25
  43.7 18.3 %copy-start.5 = (bf16[1024,768]{1,0:T(8,128)(2,1)S(1)}, bf16[1024,768]{1,0:T(8,128)(2,1)}, u32[]{:S(2)}) copy-start(bf16[1024,768]{1,0:T(8,128)(2,1)} %copy-done.3) | copy-start | bytes 4718596
  43.7 18.3 %copy-start.7 = (bf16[1024,768]{1,0:T(8,128)(2,1)S(1)}, bf16[1024,768]{1,0:T(8,128)(2,1)}, u32[]{:S(2)}) copy-start(bf16[1024,768]{1,0:T(8,128)(2,1)} %refs_4_.2) | copy-start | bytes 4718596
  43.8 18.3 %copy-start.12 = (f32[1024,1]{1,0:T(8,128)S(1)}, f32[1024,1]{1,0:T(8,128)}, u32[]{:S(2)}) copy-start(f32[1024,1]{1,0:T(8,128)} %copy-done.11) | copy-start | bytes 12292
  43.8 27.3 %collective-permute-start.5 = (bf16[512,768]{1,0:T(8,128)(2,1)S(1)}, bf16[512,768]{1,0:T(8,128)(2,1)S(1)}, u32[]{:S(2)}, u32[]{:S(2)}) collective-permute-start(bf16[512,768]{1,0:T(8,128)(2,1)S(1)} %copy-done.19), channel_id=1, source_target_pairs={{0,1},{1,0},{2,3},{3,2},{4,5},{5,4},{6,7},{7,6},{8,9},{9,8},{10,11... | collective-permute-start | bytes 2359304 | tf_op jit(solution)/shard_map/ppermute | solution.py:25
  45.9 32.9 %collective-permute-start.3 = (bf16[256,768]{1,0:T(8,128)(2,1)S(1)}, bf16[256,768]{1,0:T(8,128)(2,1)S(1)}, u32[]{:S(2)}, u32[]{:S(2)}) collective-permute-start(bf16[256,768]{1,0:T(8,128)(2,1)S(1)} %get-tuple-element.39), channel_id=1, source_target_pairs={{1,2},{2,1},{3,4},{4,3},{5,6},{6,5},{7,8},{8,7},{9,10},{10,9},{11,... | collective-permute-start | bytes 1179656 | tf_op jit(solution)/shard_map/ppermute | solution.py:25
  73.8 5.0 %copy-start.9 = (bf16[1024,768]{1,0:T(8,128)(2,1)S(1)}, bf16[1024,768]{1,0:T(8,128)(2,1)}, u32[]{:S(2)}) copy-start(bf16[1024,768]{1,0:T(8,128)(2,1)} %refs_4_.3) | copy-start | bytes 4718596
  73.8 4.9 %copy-start.14 = (f32[1024,1]{1,0:T(8,128)S(1)}, f32[1024,1]{1,0:T(8,128)}, u32[]{:S(2)}) copy-start(f32[1024,1]{1,0:T(8,128)} %copy-done.13) | copy-start | bytes 12292
  (4 other events, 4.2 us)

commit v5 on v4

--- a/solution.py
+++ b/solution.py
@@ -10,7 +10,7 @@
 AXES = ("grp", "dp")
 LOG2E = 1.4426950408889634
 VMEM_LIMIT = 24 * 2**20
-NEAR_LAST, FAR_LAST = 2, 4
+NEAR_LAST, FAR_LAST = 512, 256
 IN_VMEM = pl.BlockSpec(memory_space=pltpu.VMEM)
 ANYWHERE = pl.BlockSpec(memory_space=pl.ANY)
 IN_SMEM = pl.BlockSpec(memory_space=pltpu.SMEM)
@@ -33,7 +33,7 @@
 
 def prepare_kernel(image, text, *outs):
     image_out, image_norm, text_out, text_norm, *parts = outs
-    rows, step = image.shape[0], 256
+    rows, step = image.shape[0], 128
     for r in range(0, rows, step):
         at = slice(r, r + step)
         unit, image_norm[at, :] = unit_rows(image[at, :])
@@ -54,7 +54,7 @@
     unit = jax.ShapeDtypeStruct((rows, width), jnp.bfloat16)
     norm = jax.ShapeDtypeStruct((rows, 1), jnp.float32)
     parts = []
-    for last in (rows // NEAR_LAST, rows // FAR_LAST):
+    for last in (NEAR_LAST, FAR_LAST):
         parts.append(jax.ShapeDtypeStruct((rows - last, width), jnp.bfloat16))
         parts.append(jax.ShapeDtypeStruct((last, width), jnp.bfloat16))
     return pl.pallas_call(
@@ -70,13 +70,13 @@
     )(image, text)
 
 
-def side_kernel(*refs, label, raw_other, has_sum, final, late, step, chunk):
+def side_kernel(*refs, label, raw_other, has_sum, finish, written, late, step, chunk):
     refs = list(refs)
     scalars, own_ref, other_ref = refs[:3]
     refs = refs[3:]
     pair_ref = refs.pop(0) if label else None
     sum_ref = refs.pop(0) if has_sum else None
-    raw_ref, norm_ref = (refs.pop(0), refs.pop(0)) if final else (None, None)
+    raw_ref, norm_ref = (refs.pop(0), refs.pop(0)) if finish else (None, None)
     out_ref = refs.pop(0)
     rows, count = own_ref.shape[0], other_ref.shape[0]
     if raw_other:
@@ -86,7 +86,7 @@
             unit_ref[r : r + 256, :] = unit.astype(jnp.bfloat16)
     else:
         unit_ref = other_ref
-    if final:
+    if written:
         grad_ref, sem = refs[:2]
     if late:
         late_ref, late_sem = refs[2:]
@@ -131,27 +131,36 @@
         tiles = [grad_tile(r, i * chunk, part) for i, part in enumerate(now)]
         tile = tiles[0] if len(tiles) == 1 else jnp.concatenate(tiles, 1)
         total = jnp.dot(tile, unit_ref[...], preferred_element_type=jnp.float32)
-        if has_sum:
-            total = total + sum_ref[at, :]
         if late and r == 0:
             fetch.wait()
-        if final:
+        if finish == "more":
+            along = sum(
+                jnp.sum(piece.astype(jnp.float32) * part, -1, keepdims=True)
+                for piece, part in zip(tiles, now)
+            )
+            norm = norm_ref[at, :]
+            raw = raw_ref[at, :].astype(jnp.float32)
+            total = sum_ref[at, :] + norm * total - (norm * norm * along) * raw
+        elif has_sum:
+            total = total + sum_ref[at, :]
+        if finish == "whole":
             norm = norm_ref[at, :]
             unit = raw_ref[at, :].astype(jnp.float32) * norm
             total = norm * (total - unit * jnp.sum(unit * total, -1, keepdims=True))
+        if written:
             grad_ref[at, :] = total
             pltpu.make_async_copy(grad_ref.at[at], out_ref.at[at], sem.at[r // step]).start()
         else:
             out_ref[at, :] = total
-    if final:
+    if written:
         for r in range(0, rows, step):
             at = slice(r, r + step)
             pltpu.make_async_copy(grad_ref.at[at], out_ref.at[at], sem.at[r // step]).wait()
 
 
 def one_side(
-    scalars, own, other, pair=None, label=None, raw_other=False, so_far=None, final=None, late=False,
-    step=256, chunk=256, name="side",
+    scalars, own, other, pair=None, label=None, raw_other=False, so_far=None, finish=None, rows_of=(),
+    written=False, late=False, step=256, chunk=256, name="side",
 ):
     rows, width = own.shape
     count = other.shape[0]
@@ -160,28 +169,30 @@
         args.append(pair)
     if so_far is not None:
         args.append(so_far)
+    sum_at = len(args) - 1
+    specs = [IN_SMEM] + [IN_VMEM] * sum_at
+    if finish:
+        args += list(rows_of)
+        specs += [ANYWHERE if late else IN_VMEM, IN_VMEM]
     scratch = []
     if raw_other:
         scratch.append(pltpu.VMEM((count, width), jnp.bfloat16))
-    specs = [IN_SMEM] + [IN_VMEM] * (len(args) - 1)
-    if final is not None:
-        args += list(final)
-        specs += [ANYWHERE if late else IN_VMEM, IN_VMEM]
+    if written:
         scratch.append(pltpu.VMEM((rows, width), jnp.float32))
         scratch.append(pltpu.SemaphoreType.DMA((rows // step,)))
     if late:
         scratch += [pltpu.VMEM((rows, width), jnp.bfloat16), pltpu.SemaphoreType.DMA]
     kernel = functools.partial(
-        side_kernel, label=label, raw_other=raw_other, has_sum=so_far is not None,
-        final=final is not None, late=late, step=step, chunk=min(chunk, count),
+        side_kernel, label=label, raw_other=raw_other, has_sum=so_far is not None, finish=finish,
+        written=written, late=late, step=step, chunk=chunk,
     )
     return pl.pallas_call(
         kernel,
         in_specs=specs,
-        out_specs=IN_VMEM if final is None else ANYWHERE,
+        out_specs=ANYWHERE if written else IN_VMEM,
         out_shape=jax.ShapeDtypeStruct((rows, width), jnp.float32),
         scratch_shapes=scratch,
-        input_output_aliases={len(args) - 1: 0} if so_far is not None and final is None else {},
+        input_output_aliases={sum_at: 0} if so_far is not None and not written else {},
         compiler_params=pltpu.CompilerParams(vmem_limit_bytes=VMEM_LIMIT),
         cost_estimate=pl.CostEstimate(
             flops=rows * width, bytes_accessed=rows * width, transcendentals=0
@@ -223,15 +234,19 @@
     text_sum = one_side(scalars, text_unit, near_head, so_far=text_sum, name="text_near_head")
     image_sum, text_sum = lax.optimization_barrier((image_sum, text_sum))
     image_grad = one_side(
-        scalars, image_unit, text_far, raw_other=True, so_far=image_sum,
-        final=(photo_vectors_raw, image_norm), late=True, name="image_far",
+        scalars, image_unit, text_far, raw_other=True, so_far=image_sum, finish="whole",
+        rows_of=(photo_vectors_raw, image_norm), written=True, late=True, name="image_far",
     )
     image_grad, text_sum = lax.optimization_barrier((image_grad, text_sum))
+    own_text = (sentence_vectors_raw, text_norm)
     text_sum = one_side(scalars, text_unit, near_tail, so_far=text_sum, name="text_near_tail")
-    text_sum = one_side(scalars, text_unit, far_head, so_far=text_sum, name="text_far_head")
     text_grad = one_side(
-        scalars, text_unit, far_tail, so_far=text_sum, final=(sentence_vectors_raw, text_norm),
-        name="text_far_tail",
+        scalars, text_unit, far_head, so_far=text_sum, finish="whole", rows_of=own_text,
+        name="text_far_head",
+    )
+    text_grad = one_side(
+        scalars, text_unit, far_tail, so_far=text_grad, finish="more", rows_of=own_text,
+        written=True, name="text_far_tail",
     )
     return (image_grad, text_grad)
 

time: 82.7 us -> 82.4 us (level)
  transfers between devices with their start and end apart: 6 -> 6, of which waited for: 6 -> 6; matrix products, arithmetic and copies ran while one was open for 1% -> 1% of each run, Pallas kernels for 38% -> 39%
where the time goes in v5:
time: 82.4 us; the launch traced here: 82.1 us
  Pallas kernels  34.8 us (42%)
  waiting for transfers between devices  19.5 us (24%)
  starting transfers between devices  15.8 us (19%)
  local copies, waits for them, and re-layouts  9.45 us (11%)
  between operations  2.42 us (3%)
    pallas_call x8, Pallas kernels, one_side(): pl.pallas_call(kernel, in_specs=specs, out_specs=ANYWHERE if written else...  33.8 us
    ppermute x6, waiting for transfers between devices, swapped(): return lax.ppermute(x, AXES, pairs)  19.5 us
    ppermute x6, starting transfers between devices, swapped(): return lax.ppermute(x, AXES, pairs)  15.8 us
    unnamed x44, local copies, waits for them, and re-layouts  8.44 us
  transfers between devices with their start and end apart: 6, of which 6 were waited for; matrix products, arithmetic and copies ran while one was open for 1% of the time, Pallas kernels for 39%

profile of v5, /device:TPU:0, one launch (start us, length us, event | category | flops | bytes accessed | tf_op | source)
XLA Modules:
  0.0 82.1 jit_solution(14187771049632414338)
XLA Ops:
  0.6 2.1 %collective-permute-start.1 = (bf16[1024,768]{1,0:T(8,128)(2,1)}, bf16[1024,768]{1,0:T(8,128)(2,1)}, u32[]{:S(2)}, u32[]{:S(2)}) collective-permute-start(bf16[1024,768]{1,0:T(8,128)(2,1)} %refs_4_.5), channel_id=1, source_target_pairs={{0,1},{1,0},{2,3},{3,2},{4,5},{5,4},{6,7},{7,6},{8,9},{9,8},{10,11... | collective-permute-start | bytes 4718600 | tf_op jit(solution)/shard_map/ppermute | solution.py:25
  2.7 6.3 %collective-permute-start = (bf16[1024,768]{1,0:T(8,128)(2,1)}, bf16[1024,768]{1,0:T(8,128)(2,1)}, u32[]{:S(2)}, u32[]{:S(2)}) collective-permute-start(bf16[1024,768]{1,0:T(8,128)(2,1)} %refs_4_.5), channel_id=1, source_target_pairs={{1,2},{2,1},{3,4},{4,3},{5,6},{6,5},{7,8},{8,7},{9,10},{10,9},{11,... | collective-permute-start | bytes 4718600 | tf_op jit(solution)/shard_map/ppermute | solution.py:25
  10.4 1.4 %copy-done.6 = bf16[1024,768]{1,0:T(8,128)(2,1)S(1)} copy-done((bf16[1024,768]{1,0:T(8,128)(2,1)S(1)}, bf16[1024,768]{1,0:T(8,128)(2,1)}, u32[]{:S(2)}) %copy-start.6) | copy-done | bytes 1572888
  11.8 1.4 %copy-done.8 = bf16[1024,768]{1,0:T(8,128)(2,1)S(1)} copy-done((bf16[1024,768]{1,0:T(8,128)(2,1)S(1)}, bf16[1024,768]{1,0:T(8,128)(2,1)}, u32[]{:S(2)}) %copy-start.8) | copy-done | bytes 1572888
  13.2 1.1 %prepare.1 = (bf16[1024,768]{1,0:T(8,128)(2,1)S(1)}, f32[1024,1]{1,0:T(8,128)S(1)}, bf16[1024,768]{1,0:T(8,128)(2,1)S(1)}, f32[1024,1]{1,0:T(8,128)S(1)}, bf16[5...) custom-call(bf16[1024,768]{1,0:T(8,128)(2,1)S(1)} %copy-done.8, ...), custom_call_target="tpu_custom_call" | custom-call | flops 6291456 | bytes 6291456 | tf_op jit(solution)/shard_map/prepare/pallas_call | solution.py:60
  16.1 4.1 %text_own.1.refs_3_ = f32[1024,768]{1,0:T(8,128)S(1)} custom-call(f32[4]{0:T(128)S(1)} %pad_maximum_fusion.refs_0_, bf16[1024,768]{1,0:T(8,128)(2,1)S(1)} %get-tuple-element.23.refs_1_.refs_2_, bf16[1024,768]{1,0:T(8,128)(2,1)S(1)} %get-tuple-element.26.refs_2_.refs_1_, s32[1,1024]{1,0:T(1,128)S(1)} %copy-done.15), custom_call_target="tpu_custom_call" | custom-call | flops 786432 | bytes 786432 | tf_op jit(solution)/shard_map/text_own/pallas_call | solution.py:189
  20.2 1.0 %copy.11.refs_3_ = s32[1024,1]{1,0:T(8,128)} copy(s32[1024,1]{0,1:T(1,128)S(1)} %bitcast.1) | data formatting | bytes 8192 | tf_op jit(solution)/shard_map/reshape | solution.py:222
  21.3 1.4 %copy-done.1 = bf16[1024,768]{1,0:T(8,128)(2,1)S(1)} copy-done((bf16[1024,768]{1,0:T(8,128)(2,1)S(1)}, bf16[1024,768]{1,0:T(8,128)(2,1)}, u32[]{:S(2)}) %copy-start.1) | copy-done | bytes 1572888
  22.7 1.4 %copy-done.4 = bf16[1024,768]{1,0:T(8,128)(2,1)S(1)} copy-done((bf16[1024,768]{1,0:T(8,128)(2,1)S(1)}, bf16[1024,768]{1,0:T(8,128)(2,1)}, u32[]{:S(2)}) %copy-start.4) | copy-done | bytes 1572888
  24.1 1.0 %copy-done.10 = s32[1024,1]{1,0:T(8,128)S(1)} copy-done((s32[1024,1]{1,0:T(8,128)S(1)}, s32[1024,1]{1,0:T(8,128)}, u32[]{:S(2)}) %copy-start.10) | copy-done | bytes 4120
  25.1 4.1 %image_own.1.refs_3_ = f32[1024,768]{1,0:T(8,128)S(1)} custom-call(f32[4]{0:T(128)S(1)} %pad_maximum_fusion.refs_0_, bf16[1024,768]{1,0:T(8,128)(2,1)S(1)} %copy-done.4, bf16[1024,768]{1,0:T(8,128)(2,1)S(1)} %copy-done.1, s32[1024,1]{1,0:T(8,128)S(1)} %copy-done.10), custom_call_target="tpu_custom_call" | custom-call | flops 786432 | bytes 786432 | tf_op jit(solution)/shard_map/image_own/pallas_call | solution.py:189
  29.2 0.9 %collective-permute-start.4 = (bf16[768,768]{1,0:T(8,128)(2,1)S(1)}, bf16[768,768]{1,0:T(8,128)(2,1)S(1)}, u32[]{:S(2)}, u32[]{:S(2)}) collective-permute-start(bf16[768,768]{1,0:T(8,128)(2,1)S(1)} %copy-done.17), channel_id=1, source_target_pairs={{1,2},{2,1},{3,4},{4,3},{5,6},{6,5},{7,8},{8,7},{9,10},{10,9},{11,... | collective-permute-start | bytes 3538952 | tf_op jit(solution)/shard_map/ppermute | solution.py:25
  30.2 8.1 %collective-permute-done.1.refs_2_ = bf16[1024,768]{1,0:T(8,128)(2,1)} collective-permute-done((bf16[1024,768]{1,0:T(8,128)(2,1)}, bf16[1024,768]{1,0:T(8,128)(2,1)}, u32[]{:S(2)}, u32[]{:S(2)}) %collective-permute-start.1) | collective-permute-done | bytes 1572896 | tf_op jit(solution)/shard_map/ppermute | solution.py:25
  38.3 5.4 %image_near.1.refs_3_ = f32[1024,768]{1,0:T(8,128)S(1)} custom-call(f32[4]{0:T(128)S(1)} %pad_maximum_fusion.refs_0_, bf16[1024,768]{1,0:T(8,128)(2,1)S(1)} %copy-done.4, bf16[1024,768]{1,0:T(8,128)(2,1)} %collective-permute-done.1.refs_2_, f32[1024,768]{1,0:T(8,128)S(1)} %image_own.1.refs_3_), custom_call_target="tpu_custom_call", output_to_operand_aliasing={{}: (3, {})} | custom-call | flops 786432 | bytes 786432 | tf_op jit(solution)/shard_map/image_near/pallas_call | solution.py:189
  43.8 2.1 %collective-permute-start.5 = (bf16[512,768]{1,0:T(8,128)(2,1)S(1)}, bf16[512,768]{1,0:T(8,128)(2,1)S(1)}, u32[]{:S(2)}, u32[]{:S(2)}) collective-permute-start(bf16[512,768]{1,0:T(8,128)(2,1)S(1)} %copy-done.19), channel_id=1, source_target_pairs={{0,1},{1,0},{2,3},{3,2},{4,5},{5,4},{6,7},{7,6},{8,9},{9,8},{10,11... | collective-permute-start | bytes 2359304 | tf_op jit(solution)/shard_map/ppermute | solution.py:25
  45.9 4.3 %collective-permute-start.3 = (bf16[256,768]{1,0:T(8,128)(2,1)S(1)}, bf16[256,768]{1,0:T(8,128)(2,1)S(1)}, u32[]{:S(2)}, u32[]{:S(2)}) collective-permute-start(bf16[256,768]{1,0:T(8,128)(2,1)S(1)} %get-tuple-element.39), channel_id=1, source_target_pairs={{1,2},{2,1},{3,4},{4,3},{5,6},{6,5},{7,8},{8,7},{9,10},{10,9},{11,... | collective-permute-start | bytes 1179656 | tf_op jit(solution)/shard_map/ppermute | solution.py:25
  50.2 4.8 %collective-permute-done.2.refs_2_ = bf16[512,768]{1,0:T(8,128)(2,1)S(1)} collective-permute-done((bf16[512,768]{1,0:T(8,128)(2,1)S(1)}, bf16[512,768]{1,0:T(8,128)(2,1)S(1)}, u32[]{:S(2)}, u32[]{:S(2)}) %collective-permute-start.2) | collective-permute-done | bytes 786464 | tf_op jit(solution)/shard_map/ppermute | solution.py:25
  55.0 2.8 %text_near_head.1.refs_3_ = f32[1024,768]{1,0:T(8,128)S(1)} custom-call(f32[4]{0:T(128)S(1)} %pad_maximum_fusion.refs_0_, bf16[1024,768]{1,0:T(8,128)(2,1)S(1)} %copy-done.2, bf16[512,768]{1,0:T(8,128)(2,1)S(1)} %collective-permute-done.2.refs_2_, f32[1024,768]{1,0:T(8,128)S(1)} %text_own.1.refs_3_), custom_call_target="tpu_custom_call", output_to_operand_aliasing={{}: (3, {})} | custom-call | flops 786432 | bytes 786432 | tf_op jit(solution)/shard_map/text_near_head/pallas_call | solution.py:189
  57.8 4.2 %collective-permute-done.refs_2_ = bf16[1024,768]{1,0:T(8,128)(2,1)} collective-permute-done((bf16[1024,768]{1,0:T(8,128)(2,1)}, bf16[1024,768]{1,0:T(8,128)(2,1)}, u32[]{:S(2)}, u32[]{:S(2)}) %collective-permute-start) | collective-permute-done | bytes 1572896 | tf_op jit(solution)/shard_map/ppermute | solution.py:25
  62.0 7.7 %image_far.1 = f32[1024,768]{1,0:T(8,128)} custom-call(f32[4]{0:T(128)S(1)} %pad_maximum_fusion.refs_0_, bf16[1024,768]{1,0:T(8,128)(2,1)S(1)} %copy-done.5, bf16[1024,768]{1,0:T(8,128)(2,1)} %collective-permute-done.refs_2_, f32[1024,768]{1,0:T(8,128)S(1)} %image_near.1.refs_3_, bf16[1024,768]{1,0:T(8,128)(2,1)S(1)} %copy-done.9, f32[1024,1]{1,0:T(8,128)S(1)} %copy-done.14), custom_call_target="tpu_custom_call" | custom-call | flops 786432 | bytes 786432 | tf_op jit(solution)/shard_map/image_far/pallas_call | solution.py:189
  69.8 1.3 %collective-permute-done.5.refs_2_ = bf16[512,768]{1,0:T(8,128)(2,1)S(1)} collective-permute-done((bf16[512,768]{1,0:T(8,128)(2,1)S(1)}, bf16[512,768]{1,0:T(8,128)(2,1)S(1)}, u32[]{:S(2)}, u32[]{:S(2)}) %collective-permute-start.5) | collective-permute-done | bytes 786464 | tf_op jit(solution)/shard_map/ppermute | solution.py:25
  71.0 2.8 %text_near_tail.1.refs_3_ = f32[1024,768]{1,0:T(8,128)S(1)} custom-call(f32[4]{0:T(128)S(1)} %pad_maximum_fusion.refs_0_, bf16[1024,768]{1,0:T(8,128)(2,1)S(1)} %copy-done.2, bf16[512,768]{1,0:T(8,128)(2,1)S(1)} %collective-permute-done.5.refs_2_, f32[1024,768]{1,0:T(8,128)S(1)} %text_near_head.1.refs_3_), custom_call_target="tpu_custom_call", output_to_operand_aliasing={{}: (3, {})} | custom-call | flops 786432 | bytes 786432 | tf_op jit(solution)/shard_map/text_near_tail/pallas_call | solution.py:189
  74.6 3.8 %text_far_head.1.refs_3_ = f32[1024,768]{1,0:T(8,128)S(1)} custom-call(f32[4]{0:T(128)S(1)} %pad_maximum_fusion.refs_0_, bf16[1024,768]{1,0:T(8,128)(2,1)S(1)} %copy-done.2, bf16[768,768]{1,0:T(8,128)(2,1)S(1)} %collective-permute-done.4.refs_2_, f32[1024,768]{1,0:T(8,128)S(1)} %text_near_tail.1.refs_3_, ...), custom_call_target="tpu_custom_call", output_to_operand_aliasing={{}: (3, {})} | custom-call | flops 786432 | bytes 786432 | tf_op jit(solution)/shard_map/text_far_head/pallas_call | solution.py:189
  78.8 3.1 %text_far_tail.1 = f32[1024,768]{1,0:T(8,128)} custom-call(f32[4]{0:T(128)S(1)} %pad_maximum_fusion.refs_0_, bf16[1024,768]{1,0:T(8,128)(2,1)S(1)} %copy-done.2, bf16[256,768]{1,0:T(8,128)(2,1)S(1)} %collective-permute-done.3.refs_2_, f32[1024,768]{1,0:T(8,128)S(1)} %text_far_head.1.refs_3_, bf16[1024,768]{1,0:T(8,128)(2,1)S(1)} %copy-done.7, ...), custom_call_target="tpu_custom_call" | custom-call | flops 786432 | bytes 786432 | tf_op jit(solution)/shard_map/text_far_tail/pallas_call | solution.py:189
  (43 shorter events, 3.0 us)
Async XLA Ops:
  0.6 15.5 %copy-start.15 = (s32[1,1024]{1,0:T(1,128)S(1)}, s32[1,1024]{1,0:T(1,128)}, u32[]{:S(2)}) copy-start(s32[1,1024]{1,0:T(1,128)} %refs_3_.1) | copy-start | bytes 12292
  0.6 37.6 %collective-permute-start.1 = (bf16[1024,768]{1,0:T(8,128)(2,1)}, bf16[1024,768]{1,0:T(8,128)(2,1)}, u32[]{:S(2)}, u32[]{:S(2)}) collective-permute-start(bf16[1024,768]{1,0:T(8,128)(2,1)} %refs_4_.5), channel_id=1, source_target_pairs={{0,1},{1,0},{2,3},{3,2},{4,5},{5,4},{6,7},{7,6},{8,9},{9,8},{10,11... | collective-permute-start | bytes 4718600 | tf_op jit(solution)/shard_map/ppermute | solution.py:25
  2.7 59.3 %collective-permute-start = (bf16[1024,768]{1,0:T(8,128)(2,1)}, bf16[1024,768]{1,0:T(8,128)(2,1)}, u32[]{:S(2)}, u32[]{:S(2)}) collective-permute-start(bf16[1024,768]{1,0:T(8,128)(2,1)} %refs_4_.5), channel_id=1, source_target_pairs={{1,2},{2,1},{3,4},{4,3},{5,6},{6,5},{7,8},{8,7},{9,10},{10,9},{11,... | collective-permute-start | bytes 4718600 | tf_op jit(solution)/shard_map/ppermute | solution.py:25
  10.4 1.4 %copy-start.6 = (bf16[1024,768]{1,0:T(8,128)(2,1)S(1)}, bf16[1024,768]{1,0:T(8,128)(2,1)}, u32[]{:S(2)}) copy-start(bf16[1024,768]{1,0:T(8,128)(2,1)} %refs_4_.5) | copy-start | bytes 4718596
  16.0 4.2 %copy-start = (bf16[1024,768]{1,0:T(8,128)(2,1)}, bf16[1024,768]{1,0:T(8,128)(2,1)S(1)}, u32[]{:S(2)}) copy-start(bf16[1024,768]{1,0:T(8,128)(2,1)S(1)} %get-tuple-element.23.refs_1_.refs_2_) | copy-start | bytes 4718596
  16.0 4.2 %copy-start.3 = (bf16[1024,768]{1,0:T(8,128)(2,1)}, bf16[1024,768]{1,0:T(8,128)(2,1)S(1)}, u32[]{:S(2)}) copy-start(bf16[1024,768]{1,0:T(8,128)(2,1)S(1)} %get-tuple-element.26.refs_2_.refs_1_) | copy-start | bytes 4718596
  16.0 4.2 %copy-start.11 = (f32[1024,1]{1,0:T(8,128)}, f32[1024,1]{1,0:T(8,128)S(1)}, u32[]{:S(2)}) copy-start(f32[1024,1]{1,0:T(8,128)S(1)} %get-tuple-element.43.refs_5_) | copy-start | bytes 12292
  16.0 4.2 %copy-start.16 = (bf16[768,768]{1,0:T(8,128)(2,1)}, bf16[768,768]{1,0:T(8,128)(2,1)S(1)}, u32[]{:S(2)}) copy-start(bf16[768,768]{1,0:T(8,128)(2,1)S(1)} %get-tuple-element.40) | copy-start | bytes 3538948
  16.0 4.2 %copy-start.18 = (bf16[512,768]{1,0:T(8,128)(2,1)}, bf16[512,768]{1,0:T(8,128)(2,1)S(1)}, u32[]{:S(2)}) copy-start(bf16[512,768]{1,0:T(8,128)(2,1)S(1)} %get-tuple-element.41) | copy-start | bytes 2359300
  21.3 1.4 %copy-start.1 = (bf16[1024,768]{1,0:T(8,128)(2,1)S(1)}, bf16[1024,768]{1,0:T(8,128)(2,1)}, u32[]{:S(2)}) copy-start(bf16[1024,768]{1,0:T(8,128)(2,1)} %copy-done) | copy-start | bytes 4718596
  22.7 1.4 %copy-start.4 = (bf16[1024,768]{1,0:T(8,128)(2,1)S(1)}, bf16[1024,768]{1,0:T(8,128)(2,1)}, u32[]{:S(2)}) copy-start(bf16[1024,768]{1,0:T(8,128)(2,1)} %copy-done.3) | copy-start | bytes 4718596
  25.1 4.1 %copy-start.17 = (bf16[768,768]{1,0:T(8,128)(2,1)S(1)}, bf16[768,768]{1,0:T(8,128)(2,1)}, u32[]{:S(2)}) copy-start(bf16[768,768]{1,0:T(8,128)(2,1)} %copy-done.16) | copy-start | bytes 3538948
  25.1 5.1 %copy-start.21 = (bf16[512,768]{1,0:T(8,128)(2,1)S(1)}, bf16[512,768]{1,0:T(8,128)(2,1)}, u32[]{:S(2)}) copy-start(bf16[512,768]{1,0:T(8,128)(2,1)} %copy-done.20) | copy-start | bytes 2359300
  29.2 14.5 %copy-start.19 = (bf16[512,768]{1,0:T(8,128)(2,1)S(1)}, bf16[512,768]{1,0:T(8,128)(2,1)}, u32[]{:S(2)}) copy-start(bf16[512,768]{1,0:T(8,128)(2,1)} %copy-done.18) | copy-start | bytes 2359300
  29.2 25.8 %copy-start.2 = (bf16[1024,768]{1,0:T(8,128)(2,1)S(1)}, bf16[1024,768]{1,0:T(8,128)(2,1)}, u32[]{:S(2)}) copy-start(bf16[1024,768]{1,0:T(8,128)(2,1)} %copy-done) | copy-start | bytes 4718596
  29.2 45.3 %collective-permute-start.4 = (bf16[768,768]{1,0:T(8,128)(2,1)S(1)}, bf16[768,768]{1,0:T(8,128)(2,1)S(1)}, u32[]{:S(2)}, u32[]{:S(2)}) collective-permute-start(bf16[768,768]{1,0:T(8,128)(2,1)S(1)} %copy-done.17), channel_id=1, source_target_pairs={{1,2},{2,1},{3,4},{4,3},{5,6},{6,5},{7,8},{8,7},{9,10},{10,9},{11,... | collective-permute-start | bytes 3538952 | tf_op jit(solution)/shard_map/ppermute | solution.py:25
  30.2 24.9 %collective-permute-start.2 = (bf16[512,768]{1,0:T(8,128)(2,1)S(1)}, bf16[512,768]{1,0:T(8,128)(2,1)S(1)}, u32[]{:S(2)}, u32[]{:S(2)}) collective-permute-start(bf16[512,768]{1,0:T(8,128)(2,1)S(1)} %copy-done.21), channel_id=1, source_target_pairs={{0,1},{1,0},{2,3},{3,2},{4,5},{5,4},{6,7},{7,6},{8,9},{9,8},{10,11... | collective-permute-start | bytes 2359304 | tf_op jit(solution)/shard_map/ppermute | solution.py:25
  43.7 18.3 %copy-start.5 = (bf16[1024,768]{1,0:T(8,128)(2,1)S(1)}, bf16[1024,768]{1,0:T(8,128)(2,1)}, u32[]{:S(2)}) copy-start(bf16[1024,768]{1,0:T(8,128)(2,1)} %copy-done.3) | copy-start | bytes 4718596
  43.7 18.3 %copy-start.9 = (bf16[1024,768]{1,0:T(8,128)(2,1)S(1)}, bf16[1024,768]{1,0:T(8,128)(2,1)}, u32[]{:S(2)}) copy-start(bf16[1024,768]{1,0:T(8,128)(2,1)} %refs_4_.3) | copy-start | bytes 4718596
  43.8 18.3 %copy-start.14 = (f32[1024,1]{1,0:T(8,128)S(1)}, f32[1024,1]{1,0:T(8,128)}, u32[]{:S(2)}) copy-start(f32[1024,1]{1,0:T(8,128)} %copy-done.13) | copy-start | bytes 12292
  43.8 27.3 %collective-permute-start.5 = (bf16[512,768]{1,0:T(8,128)(2,1)S(1)}, bf16[512,768]{1,0:T(8,128)(2,1)S(1)}, u32[]{:S(2)}, u32[]{:S(2)}) collective-permute-start(bf16[512,768]{1,0:T(8,128)(2,1)S(1)} %copy-done.19), channel_id=1, source_target_pairs={{0,1},{1,0},{2,3},{3,2},{4,5},{5,4},{6,7},{7,6},{8,9},{9,8},{10,11... | collective-permute-start | bytes 2359304 | tf_op jit(solution)/shard_map/ppermute | solution.py:25
  45.9 32.9 %collective-permute-start.3 = (bf16[256,768]{1,0:T(8,128)(2,1)S(1)}, bf16[256,768]{1,0:T(8,128)(2,1)S(1)}, u32[]{:S(2)}, u32[]{:S(2)}) collective-permute-start(bf16[256,768]{1,0:T(8,128)(2,1)S(1)} %get-tuple-element.39), channel_id=1, source_target_pairs={{1,2},{2,1},{3,4},{4,3},{5,6},{6,5},{7,8},{8,7},{9,10},{10,9},{11,... | collective-permute-start | bytes 1179656 | tf_op jit(solution)/shard_map/ppermute | solution.py:25
  69.7 4.8 %copy-start.7 = (bf16[1024,768]{1,0:T(8,128)(2,1)S(1)}, bf16[1024,768]{1,0:T(8,128)(2,1)}, u32[]{:S(2)}) copy-start(bf16[1024,768]{1,0:T(8,128)(2,1)} %refs_4_.5) | copy-start | bytes 4718596
  69.8 4.8 %copy-start.12 = (f32[1024,1]{1,0:T(8,128)S(1)}, f32[1024,1]{1,0:T(8,128)}, u32[]{:S(2)}) copy-start(f32[1024,1]{1,0:T(8,128)} %copy-done.11) | copy-start | bytes 12292
  (4 other events, 4.2 us)

commit v6 on v5

--- a/solution.py
+++ b/solution.py
@@ -10,7 +10,7 @@
 AXES = ("grp", "dp")
 LOG2E = 1.4426950408889634
 VMEM_LIMIT = 24 * 2**20
-NEAR_LAST, FAR_LAST = 512, 256
+NEAR_LAST, FAR_LAST = 384, 256
 IN_VMEM = pl.BlockSpec(memory_space=pltpu.VMEM)
 ANYWHERE = pl.BlockSpec(memory_space=pl.ANY)
 IN_SMEM = pl.BlockSpec(memory_space=pltpu.SMEM)
@@ -70,13 +70,15 @@
     )(image, text)
 
 
-def side_kernel(*refs, label, raw_other, has_sum, finish, written, late, step, chunk):
+def side_kernel(*refs, label, raw_other, has_sum, finish, written, late, beside, step, chunk):
     refs = list(refs)
     scalars, own_ref, other_ref = refs[:3]
     refs = refs[3:]
     pair_ref = refs.pop(0) if label else None
     sum_ref = refs.pop(0) if has_sum else None
     raw_ref, norm_ref = (refs.pop(0), refs.pop(0)) if finish else (None, None)
+    if beside:
+        del refs[:2]
     out_ref = refs.pop(0)
     rows, count = own_ref.shape[0], other_ref.shape[0]
     if raw_other:
@@ -160,10 +162,11 @@
 
 def one_side(
     scalars, own, other, pair=None, label=None, raw_other=False, so_far=None, finish=None, rows_of=(),
-    written=False, late=False, step=256, chunk=256, name="side",
+    written=False, late=False, beside=None, step=256, chunk=256, name="side",
 ):
     rows, width = own.shape
     count = other.shape[0]
+    chunk = chunk if count % chunk == 0 else count // 2
     args = [scalars, own, other]
     if label:
         args.append(pair)
@@ -182,17 +185,25 @@
         scratch.append(pltpu.SemaphoreType.DMA((rows // step,)))
     if late:
         scratch += [pltpu.VMEM((rows, width), jnp.bfloat16), pltpu.SemaphoreType.DMA]
+    result = jax.ShapeDtypeStruct((rows, width), jnp.float32)
+    place = ANYWHERE if written else IN_VMEM
+    aliases = {sum_at: 0} if so_far is not None and not written else {}
+    if beside is not None:
+        args.append(beside)
+        specs.append(ANYWHERE)
+        result, place = [result, result], [ANYWHERE, place]
+        aliases = {len(args) - 1: 0}
     kernel = functools.partial(
         side_kernel, label=label, raw_other=raw_other, has_sum=so_far is not None, finish=finish,
-        written=written, late=late, step=step, chunk=chunk,
+        written=written, late=late, beside=beside is not None, step=step, chunk=chunk,
     )
     return pl.pallas_call(
         kernel,
         in_specs=specs,
-        out_specs=ANYWHERE if written else IN_VMEM,
-        out_shape=jax.ShapeDtypeStruct((rows, width), jnp.float32),
+        out_specs=place,
+        out_shape=result,
         scratch_shapes=scratch,
-        input_output_aliases={sum_at: 0} if so_far is not None and not written else {},
+        input_output_aliases=aliases,
         compiler_params=pltpu.CompilerParams(vmem_limit_bytes=VMEM_LIMIT),
         cost_estimate=pl.CostEstimate(
             flops=rows * width, bytes_accessed=rows * width, transcendentals=0
@@ -244,9 +255,9 @@
         scalars, text_unit, far_head, so_far=text_sum, finish="whole", rows_of=own_text,
         name="text_far_head",
     )
-    text_grad = one_side(
+    image_grad, text_grad = one_side(
         scalars, text_unit, far_tail, so_far=text_grad, finish="more", rows_of=own_text,
-        written=True, name="text_far_tail",
+        written=True, beside=image_grad, name="text_far_tail",
     )
     return (image_grad, text_grad)
 

time: 82.4 us -> 82.4 us (level)
  Pallas kernels: 34.8 us -> 35.7 us
    pallas_call x8, Pallas kernels: 33.8 us -> 34.7 us  [one_side(): pl.pallas_call(kernel, in_specs=specs, out_specs=place, out_shape=result,...]
    ppermute x6, waiting for transfers between devices: 19.5 us -> 18.7 us  [swapped(): return lax.ppermute(x, AXES, pairs)]
  transfers between devices with their start and end apart: 6 -> 6, of which waited for: 6 -> 5; matrix products, arithmetic and copies ran while one was open for 1% -> 1% of each run, Pallas kernels for 39% -> 40%
where the time goes in v6:
time: 82.4 us; the launch traced here: 82.1 us
  Pallas kernels  35.7 us (43%)
  waiting for transfers between devices  18.7 us (23%)
  starting transfers between devices  15.8 us (19%)
  local copies, waits for them, and re-layouts  9.36 us (11%)
  between operations  2.45 us (3%)
    pallas_call x8, Pallas kernels, one_side(): pl.pallas_call(kernel, in_specs=specs, out_specs=place, out_shape=result,...  34.7 us
    ppermute x6, waiting for transfers between devices, swapped(): return lax.ppermute(x, AXES, pairs)  18.7 us
    ppermute x6, starting transfers between devices, swapped(): return lax.ppermute(x, AXES, pairs)  15.8 us
    unnamed x44, local copies, waits for them, and re-layouts  8.35 us
  transfers between devices with their start and end apart: 6, of which 5 were waited for; matrix products, arithmetic and copies ran while one was open for 1% of the time, Pallas kernels for 40%

profile of v6, /device:TPU:0, one launch (start us, length us, event | category | flops | bytes accessed | tf_op | source)
XLA Modules:
  0.0 82.1 jit_solution(5729170882829967242)
XLA Ops:
  0.6 2.1 %collective-permute-start = (bf16[1024,768]{1,0:T(8,128)(2,1)}, bf16[1024,768]{1,0:T(8,128)(2,1)}, u32[]{:S(2)}, u32[]{:S(2)}) collective-permute-start(bf16[1024,768]{1,0:T(8,128)(2,1)} %refs_4_.5), channel_id=1, source_target_pairs={{0,1},{1,0},{2,3},{3,2},{4,5},{5,4},{6,7},{7,6},{8,9},{9,8},{10,11... | collective-permute-start | bytes 4718600 | tf_op jit(solution)/shard_map/ppermute | solution.py:25
  2.7 6.3 %collective-permute-start.4 = (bf16[1024,768]{1,0:T(8,128)(2,1)}, bf16[1024,768]{1,0:T(8,128)(2,1)}, u32[]{:S(2)}, u32[]{:S(2)}) collective-permute-start(bf16[1024,768]{1,0:T(8,128)(2,1)} %refs_4_.5), channel_id=1, source_target_pairs={{1,2},{2,1},{3,4},{4,3},{5,6},{6,5},{7,8},{8,7},{9,10},{10,9},{11,... | collective-permute-start | bytes 4718600 | tf_op jit(solution)/shard_map/ppermute | solution.py:25
  10.4 1.4 %copy-done.6 = bf16[1024,768]{1,0:T(8,128)(2,1)S(1)} copy-done((bf16[1024,768]{1,0:T(8,128)(2,1)S(1)}, bf16[1024,768]{1,0:T(8,128)(2,1)}, u32[]{:S(2)}) %copy-start.6) | copy-done | bytes 1572888
  11.8 1.4 %copy-done.8 = bf16[1024,768]{1,0:T(8,128)(2,1)S(1)} copy-done((bf16[1024,768]{1,0:T(8,128)(2,1)S(1)}, bf16[1024,768]{1,0:T(8,128)(2,1)}, u32[]{:S(2)}) %copy-start.8) | copy-done | bytes 1572888
  13.2 1.1 %prepare.1 = (bf16[1024,768]{1,0:T(8,128)(2,1)S(1)}, f32[1024,1]{1,0:T(8,128)S(1)}, bf16[1024,768]{1,0:T(8,128)(2,1)S(1)}, f32[1024,1]{1,0:T(8,128)S(1)}, bf16[6...) custom-call(bf16[1024,768]{1,0:T(8,128)(2,1)S(1)} %copy-done.8, ...), custom_call_target="tpu_custom_call" | custom-call | flops 6291456 | bytes 6291456 | tf_op jit(solution)/shard_map/prepare/pallas_call | solution.py:60
  15.1 0.8 %copy-done.20 = bf16[384,768]{1,0:T(8,128)(2,1)} copy-done((bf16[384,768]{1,0:T(8,128)(2,1)}, bf16[384,768]{1,0:T(8,128)(2,1)S(1)}, u32[]{:S(2)}) %copy-start.20) | copy-done | bytes 589848
  16.1 4.1 %text_own.1.refs_3_ = f32[1024,768]{1,0:T(8,128)S(1)} custom-call(f32[4]{0:T(128)S(1)} %pad_maximum_fusion.refs_0_, bf16[1024,768]{1,0:T(8,128)(2,1)S(1)} %get-tuple-element.23.refs_1_.refs_2_, bf16[1024,768]{1,0:T(8,128)(2,1)S(1)} %get-tuple-element.26.refs_2_.refs_1_, s32[1,1024]{1,0:T(1,128)S(1)} %copy-done.15), custom_call_target="tpu_custom_call" | custom-call | flops 786432 | bytes 786432 | tf_op jit(solution)/shard_map/text_own/pallas_call | solution.py:200
  20.2 1.0 %copy.12.refs_3_ = s32[1024,1]{1,0:T(8,128)} copy(s32[1024,1]{0,1:T(1,128)S(1)} %bitcast.1) | data formatting | bytes 8192 | tf_op jit(solution)/shard_map/reshape | solution.py:233
  21.2 1.4 %copy-done.1 = bf16[1024,768]{1,0:T(8,128)(2,1)S(1)} copy-done((bf16[1024,768]{1,0:T(8,128)(2,1)S(1)}, bf16[1024,768]{1,0:T(8,128)(2,1)}, u32[]{:S(2)}) %copy-start.1) | copy-done | bytes 1572888
  22.6 1.4 %copy-done.4 = bf16[1024,768]{1,0:T(8,128)(2,1)S(1)} copy-done((bf16[1024,768]{1,0:T(8,128)(2,1)S(1)}, bf16[1024,768]{1,0:T(8,128)(2,1)}, u32[]{:S(2)}) %copy-start.4) | copy-done | bytes 1572888
  24.0 1.0 %copy-done.10 = s32[1024,1]{1,0:T(8,128)S(1)} copy-done((s32[1024,1]{1,0:T(8,128)S(1)}, s32[1024,1]{1,0:T(8,128)}, u32[]{:S(2)}) %copy-start.10) | copy-done | bytes 4120
  25.0 4.1 %image_own.1.refs_3_ = f32[1024,768]{1,0:T(8,128)S(1)} custom-call(f32[4]{0:T(128)S(1)} %pad_maximum_fusion.refs_0_, bf16[1024,768]{1,0:T(8,128)(2,1)S(1)} %copy-done.4, bf16[1024,768]{1,0:T(8,128)(2,1)S(1)} %copy-done.1, s32[1024,1]{1,0:T(8,128)S(1)} %copy-done.10), custom_call_target="tpu_custom_call" | custom-call | flops 786432 | bytes 786432 | tf_op jit(solution)/shard_map/image_own/pallas_call | solution.py:200
  29.1 0.9 %collective-permute-start.2 = (bf16[768,768]{1,0:T(8,128)(2,1)S(1)}, bf16[768,768]{1,0:T(8,128)(2,1)S(1)}, u32[]{:S(2)}, u32[]{:S(2)}) collective-permute-start(bf16[768,768]{1,0:T(8,128)(2,1)S(1)} %copy-done.17), channel_id=1, source_target_pairs={{1,2},{2,1},{3,4},{4,3},{5,6},{6,5},{7,8},{8,7},{9,10},{10,9},{11,... | collective-permute-start | bytes 3538952 | tf_op jit(solution)/shard_map/ppermute | solution.py:25
  30.1 8.2 %collective-permute-done.refs_2_ = bf16[1024,768]{1,0:T(8,128)(2,1)} collective-permute-done((bf16[1024,768]{1,0:T(8,128)(2,1)}, bf16[1024,768]{1,0:T(8,128)(2,1)}, u32[]{:S(2)}, u32[]{:S(2)}) %collective-permute-start) | collective-permute-done | bytes 1572896 | tf_op jit(solution)/shard_map/ppermute | solution.py:25
  38.3 5.4 %image_near.1.refs_3_ = f32[1024,768]{1,0:T(8,128)S(1)} custom-call(f32[4]{0:T(128)S(1)} %pad_maximum_fusion.refs_0_, bf16[1024,768]{1,0:T(8,128)(2,1)S(1)} %copy-done.4, bf16[1024,768]{1,0:T(8,128)(2,1)} %collective-permute-done.refs_2_, f32[1024,768]{1,0:T(8,128)S(1)} %image_own.1.refs_3_), custom_call_target="tpu_custom_call", output_to_operand_aliasing={{}: (3, {})} | custom-call | flops 786432 | bytes 786432 | tf_op jit(solution)/shard_map/image_near/pallas_call | solution.py:200
  43.8 2.1 %collective-permute-start.3 = (bf16[384,768]{1,0:T(8,128)(2,1)S(1)}, bf16[384,768]{1,0:T(8,128)(2,1)S(1)}, u32[]{:S(2)}, u32[]{:S(2)}) collective-permute-start(bf16[384,768]{1,0:T(8,128)(2,1)S(1)} %copy-done.21), channel_id=1, source_target_pairs={{0,1},{1,0},{2,3},{3,2},{4,5},{5,4},{6,7},{7,6},{8,9},{9,8},{10,11... | collective-permute-start | bytes 1769480 | tf_op jit(solution)/shard_map/ppermute | solution.py:25
  45.9 4.3 %collective-permute-start.1 = (bf16[256,768]{1,0:T(8,128)(2,1)S(1)}, bf16[256,768]{1,0:T(8,128)(2,1)S(1)}, u32[]{:S(2)}, u32[]{:S(2)}) collective-permute-start(bf16[256,768]{1,0:T(8,128)(2,1)S(1)} %get-tuple-element.32), channel_id=1, source_target_pairs={{1,2},{2,1},{3,4},{4,3},{5,6},{6,5},{7,8},{8,7},{9,10},{10,9},{11,... | collective-permute-start | bytes 1179656 | tf_op jit(solution)/shard_map/ppermute | solution.py:25
  50.2 9.0 %collective-permute-done.5.refs_2_ = bf16[640,768]{1,0:T(8,128)(2,1)S(1)} collective-permute-done((bf16[640,768]{1,0:T(8,128)(2,1)S(1)}, bf16[640,768]{1,0:T(8,128)(2,1)S(1)}, u32[]{:S(2)}, u32[]{:S(2)}) %collective-permute-start.5) | collective-permute-done | bytes 983072 | tf_op jit(solution)/shard_map/ppermute | solution.py:25
  59.2 3.8 %text_near_head.1.refs_3_ = f32[1024,768]{1,0:T(8,128)S(1)} custom-call(f32[4]{0:T(128)S(1)} %pad_maximum_fusion.refs_0_, bf16[1024,768]{1,0:T(8,128)(2,1)S(1)} %copy-done.2, bf16[640,768]{1,0:T(8,128)(2,1)S(1)} %collective-permute-done.5.refs_2_, f32[1024,768]{1,0:T(8,128)S(1)} %text_own.1.refs_3_), custom_call_target="tpu_custom_call", output_to_operand_aliasing={{}: (3, {})} | custom-call | flops 786432 | bytes 786432 | tf_op jit(solution)/shard_map/text_near_head/pallas_call | solution.py:200
  63.1 7.7 %image_far.1.refs_6_ = f32[1024,768]{1,0:T(8,128)} custom-call(f32[4]{0:T(128)S(1)} %pad_maximum_fusion.refs_0_, bf16[1024,768]{1,0:T(8,128)(2,1)S(1)} %copy-done.5, bf16[1024,768]{1,0:T(8,128)(2,1)} %collective-permute-done.4.refs_2_, f32[1024,768]{1,0:T(8,128)S(1)} %image_near.1.refs_3_, bf16[1024,768]{1,0:T(8,128)(2,1)S(1)} %copy-done.9, ...), custom_call_target="tpu_custom_call" | custom-call | flops 786432 | bytes 786432 | tf_op jit(solution)/shard_map/image_far/pallas_call | solution.py:200
  71.0 2.7 %text_near_tail.1.refs_3_ = f32[1024,768]{1,0:T(8,128)S(1)} custom-call(f32[4]{0:T(128)S(1)} %pad_maximum_fusion.refs_0_, bf16[1024,768]{1,0:T(8,128)(2,1)S(1)} %copy-done.2, bf16[384,768]{1,0:T(8,128)(2,1)S(1)} %collective-permute-done.3.refs_2_, f32[1024,768]{1,0:T(8,128)S(1)} %text_near_head.1.refs_3_), custom_call_target="tpu_custom_call", output_to_operand_aliasing={{}: (3, {})} | custom-call | flops 786432 | bytes 786432 | tf_op jit(solution)/shard_map/text_near_tail/pallas_call | solution.py:200
  73.7 0.8 %collective-permute-done.2.refs_2_ = bf16[768,768]{1,0:T(8,128)(2,1)S(1)} collective-permute-done((bf16[768,768]{1,0:T(8,128)(2,1)S(1)}, bf16[768,768]{1,0:T(8,128)(2,1)S(1)}, u32[]{:S(2)}, u32[]{:S(2)}) %collective-permute-start.2) | collective-permute-done | bytes 1179680 | tf_op jit(solution)/shard_map/ppermute | solution.py:25
  74.6 3.8 %text_far_head.1.refs_3_ = f32[1024,768]{1,0:T(8,128)S(1)} custom-call(f32[4]{0:T(128)S(1)} %pad_maximum_fusion.refs_0_, bf16[1024,768]{1,0:T(8,128)(2,1)S(1)} %copy-done.2, bf16[768,768]{1,0:T(8,128)(2,1)S(1)} %collective-permute-done.2.refs_2_, f32[1024,768]{1,0:T(8,128)S(1)} %text_near_tail.1.refs_3_, ...), custom_call_target="tpu_custom_call", output_to_operand_aliasing={{}: (3, {})} | custom-call | flops 786432 | bytes 786432 | tf_op jit(solution)/shard_map/text_far_head/pallas_call | solution.py:200
  78.8 3.1 %text_far_tail.1 = (f32[1024,768]{1,0:T(8,128)}, f32[1024,768]{1,0:T(8,128)}) custom-call(f32[4]{0:T(128)S(1)} %pad_maximum_fusion.refs_0_, bf16[1024,768]{1,0:T(8,128)(2,1)S(1)} %copy-done.2, bf16[256,768]{1,0:T(8,128)(2,1)S(1)} %collective-permute-done.1.refs_2_, f32[1024,768]{1,0:T(8,128)S(1)} %text_far_head.1.refs_3_, ...), custom_call_target="tpu_custom_call", output_to_operand_aliasing={{0}: (6, {})} | custom-call | flops 786432 | bytes 786432 | tf_op jit(solution)/shard_map/text_far_tail/pallas_call | solution.py:200
  (43 shorter events, 1.5 us)
Async XLA Ops:
  0.6 15.4 %copy-start.15 = (s32[1,1024]{1,0:T(1,128)S(1)}, s32[1,1024]{1,0:T(1,128)}, u32[]{:S(2)}) copy-start(s32[1,1024]{1,0:T(1,128)} %refs_3_.1) | copy-start | bytes 12292
  0.6 37.6 %collective-permute-start = (bf16[1024,768]{1,0:T(8,128)(2,1)}, bf16[1024,768]{1,0:T(8,128)(2,1)}, u32[]{:S(2)}, u32[]{:S(2)}) collective-permute-start(bf16[1024,768]{1,0:T(8,128)(2,1)} %refs_4_.5), channel_id=1, source_target_pairs={{0,1},{1,0},{2,3},{3,2},{4,5},{5,4},{6,7},{7,6},{8,9},{9,8},{10,11... | collective-permute-start | bytes 4718600 | tf_op jit(solution)/shard_map/ppermute | solution.py:25
  2.7 60.3 %collective-permute-start.4 = (bf16[1024,768]{1,0:T(8,128)(2,1)}, bf16[1024,768]{1,0:T(8,128)(2,1)}, u32[]{:S(2)}, u32[]{:S(2)}) collective-permute-start(bf16[1024,768]{1,0:T(8,128)(2,1)} %refs_4_.5), channel_id=1, source_target_pairs={{1,2},{2,1},{3,4},{4,3},{5,6},{6,5},{7,8},{8,7},{9,10},{10,9},{11,... | collective-permute-start | bytes 4718600 | tf_op jit(solution)/shard_map/ppermute | solution.py:25
  10.4 1.4 %copy-start.6 = (bf16[1024,768]{1,0:T(8,128)(2,1)S(1)}, bf16[1024,768]{1,0:T(8,128)(2,1)}, u32[]{:S(2)}) copy-start(bf16[1024,768]{1,0:T(8,128)(2,1)} %refs_4_.5) | copy-start | bytes 4718596
  11.8 1.4 %copy-start.8 = (bf16[1024,768]{1,0:T(8,128)(2,1)S(1)}, bf16[1024,768]{1,0:T(8,128)(2,1)}, u32[]{:S(2)}) copy-start(bf16[1024,768]{1,0:T(8,128)(2,1)} %refs_4_.3) | copy-start | bytes 4718596
  15.9 4.2 %copy-start = (bf16[1024,768]{1,0:T(8,128)(2,1)}, bf16[1024,768]{1,0:T(8,128)(2,1)S(1)}, u32[]{:S(2)}) copy-start(bf16[1024,768]{1,0:T(8,128)(2,1)S(1)} %get-tuple-element.23.refs_1_.refs_2_) | copy-start | bytes 4718596
  16.0 4.2 %copy-start.3 = (bf16[1024,768]{1,0:T(8,128)(2,1)}, bf16[1024,768]{1,0:T(8,128)(2,1)S(1)}, u32[]{:S(2)}) copy-start(bf16[1024,768]{1,0:T(8,128)(2,1)S(1)} %get-tuple-element.26.refs_2_.refs_1_) | copy-start | bytes 4718596
  16.0 4.2 %copy-start.11 = (f32[1024,1]{1,0:T(8,128)}, f32[1024,1]{1,0:T(8,128)S(1)}, u32[]{:S(2)}) copy-start(f32[1024,1]{1,0:T(8,128)S(1)} %get-tuple-element.42.refs_5_) | copy-start | bytes 12292
  16.0 4.2 %copy-start.16 = (bf16[768,768]{1,0:T(8,128)(2,1)}, bf16[768,768]{1,0:T(8,128)(2,1)S(1)}, u32[]{:S(2)}) copy-start(bf16[768,768]{1,0:T(8,128)(2,1)S(1)} %get-tuple-element.33) | copy-start | bytes 3538948
  16.0 4.2 %copy-start.18 = (bf16[640,768]{1,0:T(8,128)(2,1)}, bf16[640,768]{1,0:T(8,128)(2,1)S(1)}, u32[]{:S(2)}) copy-start(bf16[640,768]{1,0:T(8,128)(2,1)S(1)} %get-tuple-element.36) | copy-start | bytes 2949124
  21.2 1.4 %copy-start.1 = (bf16[1024,768]{1,0:T(8,128)(2,1)S(1)}, bf16[1024,768]{1,0:T(8,128)(2,1)}, u32[]{:S(2)}) copy-start(bf16[1024,768]{1,0:T(8,128)(2,1)} %copy-done) | copy-start | bytes 4718596
  25.0 4.1 %copy-start.17 = (bf16[768,768]{1,0:T(8,128)(2,1)S(1)}, bf16[768,768]{1,0:T(8,128)(2,1)}, u32[]{:S(2)}) copy-start(bf16[768,768]{1,0:T(8,128)(2,1)} %copy-done.16) | copy-start | bytes 3538948
  25.0 5.0 %copy-start.19 = (bf16[640,768]{1,0:T(8,128)(2,1)S(1)}, bf16[640,768]{1,0:T(8,128)(2,1)}, u32[]{:S(2)}) copy-start(bf16[640,768]{1,0:T(8,128)(2,1)} %copy-done.18) | copy-start | bytes 2949124
  29.1 14.6 %copy-start.21 = (bf16[384,768]{1,0:T(8,128)(2,1)S(1)}, bf16[384,768]{1,0:T(8,128)(2,1)}, u32[]{:S(2)}) copy-start(bf16[384,768]{1,0:T(8,128)(2,1)} %copy-done.20) | copy-start | bytes 1769476
  29.1 30.1 %copy-start.2 = (bf16[1024,768]{1,0:T(8,128)(2,1)S(1)}, bf16[1024,768]{1,0:T(8,128)(2,1)}, u32[]{:S(2)}) copy-start(bf16[1024,768]{1,0:T(8,128)(2,1)} %copy-done) | copy-start | bytes 4718596
  29.1 45.4 %collective-permute-start.2 = (bf16[768,768]{1,0:T(8,128)(2,1)S(1)}, bf16[768,768]{1,0:T(8,128)(2,1)S(1)}, u32[]{:S(2)}, u32[]{:S(2)}) collective-permute-start(bf16[768,768]{1,0:T(8,128)(2,1)S(1)} %copy-done.17), channel_id=1, source_target_pairs={{1,2},{2,1},{3,4},{4,3},{5,6},{6,5},{7,8},{8,7},{9,10},{10,9},{11,... | collective-permute-start | bytes 3538952 | tf_op jit(solution)/shard_map/ppermute | solution.py:25
  30.1 29.2 %collective-permute-start.5 = (bf16[640,768]{1,0:T(8,128)(2,1)S(1)}, bf16[640,768]{1,0:T(8,128)(2,1)S(1)}, u32[]{:S(2)}, u32[]{:S(2)}) collective-permute-start(bf16[640,768]{1,0:T(8,128)(2,1)S(1)} %copy-done.19), channel_id=1, source_target_pairs={{0,1},{1,0},{2,3},{3,2},{4,5},{5,4},{6,7},{7,6},{8,9},{9,8},{10,11... | collective-permute-start | bytes 2949128 | tf_op jit(solution)/shard_map/ppermute | solution.py:25
  43.7 19.3 %copy-start.5 = (bf16[1024,768]{1,0:T(8,128)(2,1)S(1)}, bf16[1024,768]{1,0:T(8,128)(2,1)}, u32[]{:S(2)}) copy-start(bf16[1024,768]{1,0:T(8,128)(2,1)} %copy-done.3) | copy-start | bytes 4718596
  43.7 19.3 %copy-start.9 = (bf16[1024,768]{1,0:T(8,128)(2,1)S(1)}, bf16[1024,768]{1,0:T(8,128)(2,1)}, u32[]{:S(2)}) copy-start(bf16[1024,768]{1,0:T(8,128)(2,1)} %refs_4_.3) | copy-start | bytes 4718596
  43.8 19.3 %copy-start.14 = (f32[1024,1]{1,0:T(8,128)S(1)}, f32[1024,1]{1,0:T(8,128)}, u32[]{:S(2)}) copy-start(f32[1024,1]{1,0:T(8,128)} %copy-done.13) | copy-start | bytes 12292
  43.8 27.3 %collective-permute-start.3 = (bf16[384,768]{1,0:T(8,128)(2,1)S(1)}, bf16[384,768]{1,0:T(8,128)(2,1)S(1)}, u32[]{:S(2)}, u32[]{:S(2)}) collective-permute-start(bf16[384,768]{1,0:T(8,128)(2,1)S(1)} %copy-done.21), channel_id=1, source_target_pairs={{0,1},{1,0},{2,3},{3,2},{4,5},{5,4},{6,7},{7,6},{8,9},{9,8},{10,11... | collective-permute-start | bytes 1769480 | tf_op jit(solution)/shard_map/ppermute | solution.py:25
  45.9 32.9 %collective-permute-start.1 = (bf16[256,768]{1,0:T(8,128)(2,1)S(1)}, bf16[256,768]{1,0:T(8,128)(2,1)S(1)}, u32[]{:S(2)}, u32[]{:S(2)}) collective-permute-start(bf16[256,768]{1,0:T(8,128)(2,1)S(1)} %get-tuple-element.32), channel_id=1, source_target_pairs={{1,2},{2,1},{3,4},{4,3},{5,6},{6,5},{7,8},{8,7},{9,10},{10,9},{11,... | collective-permute-start | bytes 1179656 | tf_op jit(solution)/shard_map/ppermute | solution.py:25
  70.8 3.8 %copy-start.7 = (bf16[1024,768]{1,0:T(8,128)(2,1)S(1)}, bf16[1024,768]{1,0:T(8,128)(2,1)}, u32[]{:S(2)}) copy-start(bf16[1024,768]{1,0:T(8,128)(2,1)} %refs_4_.5) | copy-start | bytes 4718596
  70.8 3.8 %copy-start.12 = (f32[1024,1]{1,0:T(8,128)S(1)}, f32[1024,1]{1,0:T(8,128)}, u32[]{:S(2)}) copy-start(f32[1024,1]{1,0:T(8,128)} %copy-done.11) | copy-start | bytes 12292
  (4 other events, 4.1 us)

commit v7 on v6

--- a/solution.py
+++ b/solution.py
@@ -70,7 +70,7 @@
     )(image, text)
 
 
-def side_kernel(*refs, label, raw_other, has_sum, finish, written, late, beside, step, chunk):
+def side_kernel(*refs, label, raw_other, has_sum, finish, written, beside, step, chunk):
     refs = list(refs)
     scalars, own_ref, other_ref = refs[:3]
     refs = refs[3:]
@@ -89,12 +89,7 @@
     else:
         unit_ref = other_ref
     if written:
-        grad_ref, sem = refs[:2]
-    if late:
-        late_ref, late_sem = refs[2:]
-        fetch = pltpu.make_async_copy(raw_ref, late_ref, late_sem)
-        fetch.start()
-        raw_ref = late_ref
+        grad_ref, sem = refs
     slope, shift, floor, log_floor = (scalars[i] for i in range(4))
 
     def scores(r):
@@ -133,8 +128,6 @@
         tiles = [grad_tile(r, i * chunk, part) for i, part in enumerate(now)]
         tile = tiles[0] if len(tiles) == 1 else jnp.concatenate(tiles, 1)
         total = jnp.dot(tile, unit_ref[...], preferred_element_type=jnp.float32)
-        if late and r == 0:
-            fetch.wait()
         if finish == "more":
             along = sum(
                 jnp.sum(piece.astype(jnp.float32) * part, -1, keepdims=True)
@@ -162,11 +155,11 @@
 
 def one_side(
     scalars, own, other, pair=None, label=None, raw_other=False, so_far=None, finish=None, rows_of=(),
-    written=False, late=False, beside=None, step=256, chunk=256, name="side",
+    written=False, beside=None, step=256, chunk=256, name="side",
 ):
     rows, width = own.shape
     count = other.shape[0]
-    chunk = chunk if count % chunk == 0 else count // 2
+    chunk = chunk if count % chunk == 0 else count
     args = [scalars, own, other]
     if label:
         args.append(pair)
@@ -176,15 +169,13 @@
     specs = [IN_SMEM] + [IN_VMEM] * sum_at
     if finish:
         args += list(rows_of)
-        specs += [ANYWHERE if late else IN_VMEM, IN_VMEM]
+        specs += [IN_VMEM, IN_VMEM]
     scratch = []
     if raw_other:
         scratch.append(pltpu.VMEM((count, width), jnp.bfloat16))
     if written:
         scratch.append(pltpu.VMEM((rows, width), jnp.float32))
         scratch.append(pltpu.SemaphoreType.DMA((rows // step,)))
-    if late:
-        scratch += [pltpu.VMEM((rows, width), jnp.bfloat16), pltpu.SemaphoreType.DMA]
     result = jax.ShapeDtypeStruct((rows, width), jnp.float32)
     place = ANYWHERE if written else IN_VMEM
     aliases = {sum_at: 0} if so_far is not None and not written else {}
@@ -195,7 +186,7 @@
         aliases = {len(args) - 1: 0}
     kernel = functools.partial(
         side_kernel, label=label, raw_other=raw_other, has_sum=so_far is not None, finish=finish,
-        written=written, late=late, beside=beside is not None, step=step, chunk=chunk,
+        written=written, beside=beside is not None, step=step, chunk=chunk,
     )
     return pl.pallas_call(
         kernel,
@@ -246,7 +237,7 @@
     image_sum, text_sum = lax.optimization_barrier((image_sum, text_sum))
     image_grad = one_side(
         scalars, image_unit, text_far, raw_other=True, so_far=image_sum, finish="whole",
-        rows_of=(photo_vectors_raw, image_norm), written=True, late=True, name="image_far",
+        rows_of=(photo_vectors_raw, image_norm), written=True, name="image_far",
     )
     image_grad, text_sum = lax.optimization_barrier((image_grad, text_sum))
     own_text = (sentence_vectors_raw, text_norm)

time: 82.4 us -> 82.4 us (level)
  Pallas kernels: 35.7 us -> 34.2 us
  waiting for transfers between devices: 18.7 us -> 20.2 us
    ppermute x6, waiting for transfers between devices: 18.7 us -> 20.2 us  [swapped(): return lax.ppermute(x, AXES, pairs)]
    pallas_call x8, Pallas kernels: 34.7 us -> 33.2 us  [one_side(): pl.pallas_call(kernel, in_specs=specs, out_specs=place, out_shape=result,...]
  transfers between devices with their start and end apart: 6 -> 6, of which waited for: 5 -> 5; matrix products, arithmetic and copies ran while one was open for 1% -> 1% of each run, Pallas kernels for 40% -> 38%
where the time goes in v7:
time: 82.4 us; the launch traced here: 82 us
  Pallas kernels  34.2 us (42%)
  waiting for transfers between devices  20.2 us (25%)
  starting transfers between devices  15.8 us (19%)
  local copies, waits for them, and re-layouts  9.36 us (11%)
  between operations  2.43 us (3%)
    pallas_call x8, Pallas kernels, one_side(): pl.pallas_call(kernel, in_specs=specs, out_specs=place, out_shape=result,...  33.2 us
    ppermute x6, waiting for transfers between devices, swapped(): return lax.ppermute(x, AXES, pairs)  20.2 us
    ppermute x6, starting transfers between devices, swapped(): return lax.ppermute(x, AXES, pairs)  15.8 us
    unnamed x44, local copies, waits for them, and re-layouts  8.35 us
  transfers between devices with their start and end apart: 6, of which 5 were waited for; matrix products, arithmetic and copies ran while one was open for 1% of the time, Pallas kernels for 38%

profile of v7, /device:TPU:0, one launch (start us, length us, event | category | flops | bytes accessed | tf_op | source)
XLA Modules:
  0.0 82.0 jit_solution(2111439178083029350)
XLA Ops:
  0.6 2.1 %collective-permute-start = (bf16[1024,768]{1,0:T(8,128)(2,1)}, bf16[1024,768]{1,0:T(8,128)(2,1)}, u32[]{:S(2)}, u32[]{:S(2)}) collective-permute-start(bf16[1024,768]{1,0:T(8,128)(2,1)} %refs_4_.5), channel_id=1, source_target_pairs={{0,1},{1,0},{2,3},{3,2},{4,5},{5,4},{6,7},{7,6},{8,9},{9,8},{10,11... | collective-permute-start | bytes 4718600 | tf_op jit(solution)/shard_map/ppermute | solution.py:25
  2.7 6.3 %collective-permute-start.4 = (bf16[1024,768]{1,0:T(8,128)(2,1)}, bf16[1024,768]{1,0:T(8,128)(2,1)}, u32[]{:S(2)}, u32[]{:S(2)}) collective-permute-start(bf16[1024,768]{1,0:T(8,128)(2,1)} %refs_4_.5), channel_id=1, source_target_pairs={{1,2},{2,1},{3,4},{4,3},{5,6},{6,5},{7,8},{8,7},{9,10},{10,9},{11,... | collective-permute-start | bytes 4718600 | tf_op jit(solution)/shard_map/ppermute | solution.py:25
  10.4 1.4 %copy-done.6 = bf16[1024,768]{1,0:T(8,128)(2,1)S(1)} copy-done((bf16[1024,768]{1,0:T(8,128)(2,1)S(1)}, bf16[1024,768]{1,0:T(8,128)(2,1)}, u32[]{:S(2)}) %copy-start.6) | copy-done | bytes 1572888
  11.8 1.4 %copy-done.8 = bf16[1024,768]{1,0:T(8,128)(2,1)S(1)} copy-done((bf16[1024,768]{1,0:T(8,128)(2,1)S(1)}, bf16[1024,768]{1,0:T(8,128)(2,1)}, u32[]{:S(2)}) %copy-start.8) | copy-done | bytes 1572888
  13.2 1.1 %prepare.1 = (bf16[1024,768]{1,0:T(8,128)(2,1)S(1)}, f32[1024,1]{1,0:T(8,128)S(1)}, bf16[1024,768]{1,0:T(8,128)(2,1)S(1)}, f32[1024,1]{1,0:T(8,128)S(1)}, bf16[6...) custom-call(bf16[1024,768]{1,0:T(8,128)(2,1)S(1)} %copy-done.8, ...), custom_call_target="tpu_custom_call" | custom-call | flops 6291456 | bytes 6291456 | tf_op jit(solution)/shard_map/prepare/pallas_call | solution.py:60
  16.1 4.1 %text_own.1.refs_3_ = f32[1024,768]{1,0:T(8,128)S(1)} custom-call(f32[4]{0:T(128)S(1)} %pad_maximum_fusion.refs_0_, bf16[1024,768]{1,0:T(8,128)(2,1)S(1)} %get-tuple-element.23.refs_1_.refs_2_, bf16[1024,768]{1,0:T(8,128)(2,1)S(1)} %get-tuple-element.26.refs_2_.refs_1_, s32[1,1024]{1,0:T(1,128)S(1)} %copy-done.15), custom_call_target="tpu_custom_call" | custom-call | flops 786432 | bytes 786432 | tf_op jit(solution)/shard_map/text_own/pallas_call | solution.py:191
  20.2 1.0 %copy.12.refs_3_ = s32[1024,1]{1,0:T(8,128)} copy(s32[1024,1]{0,1:T(1,128)S(1)} %bitcast.1) | data formatting | bytes 8192 | tf_op jit(solution)/shard_map/reshape | solution.py:224
  21.2 1.4 %copy-done.1 = bf16[1024,768]{1,0:T(8,128)(2,1)S(1)} copy-done((bf16[1024,768]{1,0:T(8,128)(2,1)S(1)}, bf16[1024,768]{1,0:T(8,128)(2,1)}, u32[]{:S(2)}) %copy-start.1) | copy-done | bytes 1572888
  22.6 1.4 %copy-done.4 = bf16[1024,768]{1,0:T(8,128)(2,1)S(1)} copy-done((bf16[1024,768]{1,0:T(8,128)(2,1)S(1)}, bf16[1024,768]{1,0:T(8,128)(2,1)}, u32[]{:S(2)}) %copy-start.4) | copy-done | bytes 1572888
  24.0 1.0 %copy-done.10 = s32[1024,1]{1,0:T(8,128)S(1)} copy-done((s32[1024,1]{1,0:T(8,128)S(1)}, s32[1024,1]{1,0:T(8,128)}, u32[]{:S(2)}) %copy-start.10) | copy-done | bytes 4120
  25.0 4.1 %image_own.1.refs_3_ = f32[1024,768]{1,0:T(8,128)S(1)} custom-call(f32[4]{0:T(128)S(1)} %pad_maximum_fusion.refs_0_, bf16[1024,768]{1,0:T(8,128)(2,1)S(1)} %copy-done.4, bf16[1024,768]{1,0:T(8,128)(2,1)S(1)} %copy-done.1, s32[1024,1]{1,0:T(8,128)S(1)} %copy-done.10), custom_call_target="tpu_custom_call" | custom-call | flops 786432 | bytes 786432 | tf_op jit(solution)/shard_map/image_own/pallas_call | solution.py:191
  29.1 0.9 %collective-permute-start.2 = (bf16[768,768]{1,0:T(8,128)(2,1)S(1)}, bf16[768,768]{1,0:T(8,128)(2,1)S(1)}, u32[]{:S(2)}, u32[]{:S(2)}) collective-permute-start(bf16[768,768]{1,0:T(8,128)(2,1)S(1)} %copy-done.17), channel_id=1, source_target_pairs={{1,2},{2,1},{3,4},{4,3},{5,6},{6,5},{7,8},{8,7},{9,10},{10,9},{11,... | collective-permute-start | bytes 3538952 | tf_op jit(solution)/shard_map/ppermute | solution.py:25
  30.1 8.2 %collective-permute-done.refs_2_ = bf16[1024,768]{1,0:T(8,128)(2,1)} collective-permute-done((bf16[1024,768]{1,0:T(8,128)(2,1)}, bf16[1024,768]{1,0:T(8,128)(2,1)}, u32[]{:S(2)}, u32[]{:S(2)}) %collective-permute-start) | collective-permute-done | bytes 1572896 | tf_op jit(solution)/shard_map/ppermute | solution.py:25
  38.3 5.4 %image_near.1.refs_3_ = f32[1024,768]{1,0:T(8,128)S(1)} custom-call(f32[4]{0:T(128)S(1)} %pad_maximum_fusion.refs_0_, bf16[1024,768]{1,0:T(8,128)(2,1)S(1)} %copy-done.4, bf16[1024,768]{1,0:T(8,128)(2,1)} %collective-permute-done.refs_2_, f32[1024,768]{1,0:T(8,128)S(1)} %image_own.1.refs_3_), custom_call_target="tpu_custom_call", output_to_operand_aliasing={{}: (3, {})} | custom-call | flops 786432 | bytes 786432 | tf_op jit(solution)/shard_map/image_near/pallas_call | solution.py:191
  43.8 2.1 %collective-permute-start.3 = (bf16[384,768]{1,0:T(8,128)(2,1)S(1)}, bf16[384,768]{1,0:T(8,128)(2,1)S(1)}, u32[]{:S(2)}, u32[]{:S(2)}) collective-permute-start(bf16[384,768]{1,0:T(8,128)(2,1)S(1)} %copy-done.21), channel_id=1, source_target_pairs={{0,1},{1,0},{2,3},{3,2},{4,5},{5,4},{6,7},{7,6},{8,9},{9,8},{10,11... | collective-permute-start | bytes 1769480 | tf_op jit(solution)/shard_map/ppermute | solution.py:25
  45.9 4.3 %collective-permute-start.1 = (bf16[256,768]{1,0:T(8,128)(2,1)S(1)}, bf16[256,768]{1,0:T(8,128)(2,1)S(1)}, u32[]{:S(2)}, u32[]{:S(2)}) collective-permute-start(bf16[256,768]{1,0:T(8,128)(2,1)S(1)} %get-tuple-element.32), channel_id=1, source_target_pairs={{1,2},{2,1},{3,4},{4,3},{5,6},{6,5},{7,8},{8,7},{9,10},{10,9},{11,... | collective-permute-start | bytes 1179656 | tf_op jit(solution)/shard_map/ppermute | solution.py:25
  50.2 9.0 %collective-permute-done.5.refs_2_ = bf16[640,768]{1,0:T(8,128)(2,1)S(1)} collective-permute-done((bf16[640,768]{1,0:T(8,128)(2,1)S(1)}, bf16[640,768]{1,0:T(8,128)(2,1)S(1)}, u32[]{:S(2)}, u32[]{:S(2)}) %collective-permute-start.5) | collective-permute-done | bytes 983072 | tf_op jit(solution)/shard_map/ppermute | solution.py:25
  59.2 3.4 %text_near_head.1.refs_3_ = f32[1024,768]{1,0:T(8,128)S(1)} custom-call(f32[4]{0:T(128)S(1)} %pad_maximum_fusion.refs_0_, bf16[1024,768]{1,0:T(8,128)(2,1)S(1)} %copy-done.2, bf16[640,768]{1,0:T(8,128)(2,1)S(1)} %collective-permute-done.5.refs_2_, f32[1024,768]{1,0:T(8,128)S(1)} %text_own.1.refs_3_), custom_call_target="tpu_custom_call", output_to_operand_aliasing={{}: (3, {})} | custom-call | flops 786432 | bytes 786432 | tf_op jit(solution)/shard_map/text_near_head/pallas_call | solution.py:191
  62.7 6.6 %image_far.1.refs_6_ = f32[1024,768]{1,0:T(8,128)} custom-call(f32[4]{0:T(128)S(1)} %pad_maximum_fusion.refs_0_, bf16[1024,768]{1,0:T(8,128)(2,1)S(1)} %copy-done.5, bf16[1024,768]{1,0:T(8,128)(2,1)} %collective-permute-done.4.refs_2_, f32[1024,768]{1,0:T(8,128)S(1)} %image_near.1.refs_3_, bf16[1024,768]{1,0:T(8,128)(2,1)S(1)} %copy-done.9, ...), custom_call_target="tpu_custom_call" | custom-call | flops 786432 | bytes 786432 | tf_op jit(solution)/shard_map/image_far/pallas_call | solution.py:191
  69.4 1.6 %collective-permute-done.3.refs_2_ = bf16[384,768]{1,0:T(8,128)(2,1)S(1)} collective-permute-done((bf16[384,768]{1,0:T(8,128)(2,1)S(1)}, bf16[384,768]{1,0:T(8,128)(2,1)S(1)}, u32[]{:S(2)}, u32[]{:S(2)}) %collective-permute-start.3) | collective-permute-done | bytes 589856 | tf_op jit(solution)/shard_map/ppermute | solution.py:25
  71.0 2.6 %text_near_tail.1.refs_3_ = f32[1024,768]{1,0:T(8,128)S(1)} custom-call(f32[4]{0:T(128)S(1)} %pad_maximum_fusion.refs_0_, bf16[1024,768]{1,0:T(8,128)(2,1)S(1)} %copy-done.2, bf16[384,768]{1,0:T(8,128)(2,1)S(1)} %collective-permute-done.3.refs_2_, f32[1024,768]{1,0:T(8,128)S(1)} %text_near_head.1.refs_3_), custom_call_target="tpu_custom_call", output_to_operand_aliasing={{}: (3, {})} | custom-call | flops 786432 | bytes 786432 | tf_op jit(solution)/shard_map/text_near_tail/pallas_call | solution.py:191
  73.6 0.9 %collective-permute-done.2.refs_2_ = bf16[768,768]{1,0:T(8,128)(2,1)S(1)} collective-permute-done((bf16[768,768]{1,0:T(8,128)(2,1)S(1)}, bf16[768,768]{1,0:T(8,128)(2,1)S(1)}, u32[]{:S(2)}, u32[]{:S(2)}) %collective-permute-start.2) | collective-permute-done | bytes 1179680 | tf_op jit(solution)/shard_map/ppermute | solution.py:25
  74.6 3.8 %text_far_head.1.refs_3_ = f32[1024,768]{1,0:T(8,128)S(1)} custom-call(f32[4]{0:T(128)S(1)} %pad_maximum_fusion.refs_0_, bf16[1024,768]{1,0:T(8,128)(2,1)S(1)} %copy-done.2, bf16[768,768]{1,0:T(8,128)(2,1)S(1)} %collective-permute-done.2.refs_2_, f32[1024,768]{1,0:T(8,128)S(1)} %text_near_tail.1.refs_3_, ...), custom_call_target="tpu_custom_call", output_to_operand_aliasing={{}: (3, {})} | custom-call | flops 786432 | bytes 786432 | tf_op jit(solution)/shard_map/text_far_head/pallas_call | solution.py:191
  78.8 3.1 %text_far_tail.1 = (f32[1024,768]{1,0:T(8,128)}, f32[1024,768]{1,0:T(8,128)}) custom-call(f32[4]{0:T(128)S(1)} %pad_maximum_fusion.refs_0_, bf16[1024,768]{1,0:T(8,128)(2,1)S(1)} %copy-done.2, bf16[256,768]{1,0:T(8,128)(2,1)S(1)} %collective-permute-done.1.refs_2_, f32[1024,768]{1,0:T(8,128)S(1)} %text_far_head.1.refs_3_, ...), custom_call_target="tpu_custom_call", output_to_operand_aliasing={{0}: (6, {})} | custom-call | flops 786432 | bytes 786432 | tf_op jit(solution)/shard_map/text_far_tail/pallas_call | solution.py:191
  (43 shorter events, 2.1 us)
Async XLA Ops:
  0.6 15.4 %copy-start.15 = (s32[1,1024]{1,0:T(1,128)S(1)}, s32[1,1024]{1,0:T(1,128)}, u32[]{:S(2)}) copy-start(s32[1,1024]{1,0:T(1,128)} %refs_3_.1) | copy-start | bytes 12292
  0.6 37.6 %collective-permute-start = (bf16[1024,768]{1,0:T(8,128)(2,1)}, bf16[1024,768]{1,0:T(8,128)(2,1)}, u32[]{:S(2)}, u32[]{:S(2)}) collective-permute-start(bf16[1024,768]{1,0:T(8,128)(2,1)} %refs_4_.5), channel_id=1, source_target_pairs={{0,1},{1,0},{2,3},{3,2},{4,5},{5,4},{6,7},{7,6},{8,9},{9,8},{10,11... | collective-permute-start | bytes 4718600 | tf_op jit(solution)/shard_map/ppermute | solution.py:25
  2.7 60.0 %collective-permute-start.4 = (bf16[1024,768]{1,0:T(8,128)(2,1)}, bf16[1024,768]{1,0:T(8,128)(2,1)}, u32[]{:S(2)}, u32[]{:S(2)}) collective-permute-start(bf16[1024,768]{1,0:T(8,128)(2,1)} %refs_4_.5), channel_id=1, source_target_pairs={{1,2},{2,1},{3,4},{4,3},{5,6},{6,5},{7,8},{8,7},{9,10},{10,9},{11,... | collective-permute-start | bytes 4718600 | tf_op jit(solution)/shard_map/ppermute | solution.py:25
  10.4 1.4 %copy-start.6 = (bf16[1024,768]{1,0:T(8,128)(2,1)S(1)}, bf16[1024,768]{1,0:T(8,128)(2,1)}, u32[]{:S(2)}) copy-start(bf16[1024,768]{1,0:T(8,128)(2,1)} %refs_4_.5) | copy-start | bytes 4718596
  11.8 1.4 %copy-start.8 = (bf16[1024,768]{1,0:T(8,128)(2,1)S(1)}, bf16[1024,768]{1,0:T(8,128)(2,1)}, u32[]{:S(2)}) copy-start(bf16[1024,768]{1,0:T(8,128)(2,1)} %refs_4_.3) | copy-start | bytes 4718596
  15.9 4.2 %copy-start = (bf16[1024,768]{1,0:T(8,128)(2,1)}, bf16[1024,768]{1,0:T(8,128)(2,1)S(1)}, u32[]{:S(2)}) copy-start(bf16[1024,768]{1,0:T(8,128)(2,1)S(1)} %get-tuple-element.23.refs_1_.refs_2_) | copy-start | bytes 4718596
  16.0 4.2 %copy-start.3 = (bf16[1024,768]{1,0:T(8,128)(2,1)}, bf16[1024,768]{1,0:T(8,128)(2,1)S(1)}, u32[]{:S(2)}) copy-start(bf16[1024,768]{1,0:T(8,128)(2,1)S(1)} %get-tuple-element.26.refs_2_.refs_1_) | copy-start | bytes 4718596
  16.0 4.2 %copy-start.11 = (f32[1024,1]{1,0:T(8,128)}, f32[1024,1]{1,0:T(8,128)S(1)}, u32[]{:S(2)}) copy-start(f32[1024,1]{1,0:T(8,128)S(1)} %get-tuple-element.42.refs_5_) | copy-start | bytes 12292
  16.0 4.2 %copy-start.16 = (bf16[768,768]{1,0:T(8,128)(2,1)}, bf16[768,768]{1,0:T(8,128)(2,1)S(1)}, u32[]{:S(2)}) copy-start(bf16[768,768]{1,0:T(8,128)(2,1)S(1)} %get-tuple-element.33) | copy-start | bytes 3538948
  16.0 4.2 %copy-start.18 = (bf16[640,768]{1,0:T(8,128)(2,1)}, bf16[640,768]{1,0:T(8,128)(2,1)S(1)}, u32[]{:S(2)}) copy-start(bf16[640,768]{1,0:T(8,128)(2,1)S(1)} %get-tuple-element.36) | copy-start | bytes 2949124
  21.2 1.4 %copy-start.1 = (bf16[1024,768]{1,0:T(8,128)(2,1)S(1)}, bf16[1024,768]{1,0:T(8,128)(2,1)}, u32[]{:S(2)}) copy-start(bf16[1024,768]{1,0:T(8,128)(2,1)} %copy-done) | copy-start | bytes 4718596
  25.0 4.1 %copy-start.17 = (bf16[768,768]{1,0:T(8,128)(2,1)S(1)}, bf16[768,768]{1,0:T(8,128)(2,1)}, u32[]{:S(2)}) copy-start(bf16[768,768]{1,0:T(8,128)(2,1)} %copy-done.16) | copy-start | bytes 3538948
  25.0 5.0 %copy-start.19 = (bf16[640,768]{1,0:T(8,128)(2,1)S(1)}, bf16[640,768]{1,0:T(8,128)(2,1)}, u32[]{:S(2)}) copy-start(bf16[640,768]{1,0:T(8,128)(2,1)} %copy-done.18) | copy-start | bytes 2949124
  29.1 14.6 %copy-start.21 = (bf16[384,768]{1,0:T(8,128)(2,1)S(1)}, bf16[384,768]{1,0:T(8,128)(2,1)}, u32[]{:S(2)}) copy-start(bf16[384,768]{1,0:T(8,128)(2,1)} %copy-done.20) | copy-start | bytes 1769476
  29.1 30.1 %copy-start.2 = (bf16[1024,768]{1,0:T(8,128)(2,1)S(1)}, bf16[1024,768]{1,0:T(8,128)(2,1)}, u32[]{:S(2)}) copy-start(bf16[1024,768]{1,0:T(8,128)(2,1)} %copy-done) | copy-start | bytes 4718596
  29.1 45.4 %collective-permute-start.2 = (bf16[768,768]{1,0:T(8,128)(2,1)S(1)}, bf16[768,768]{1,0:T(8,128)(2,1)S(1)}, u32[]{:S(2)}, u32[]{:S(2)}) collective-permute-start(bf16[768,768]{1,0:T(8,128)(2,1)S(1)} %copy-done.17), channel_id=1, source_target_pairs={{1,2},{2,1},{3,4},{4,3},{5,6},{6,5},{7,8},{8,7},{9,10},{10,9},{11,... | collective-permute-start | bytes 3538952 | tf_op jit(solution)/shard_map/ppermute | solution.py:25
  30.1 29.2 %collective-permute-start.5 = (bf16[640,768]{1,0:T(8,128)(2,1)S(1)}, bf16[640,768]{1,0:T(8,128)(2,1)S(1)}, u32[]{:S(2)}, u32[]{:S(2)}) collective-permute-start(bf16[640,768]{1,0:T(8,128)(2,1)S(1)} %copy-done.19), channel_id=1, source_target_pairs={{0,1},{1,0},{2,3},{3,2},{4,5},{5,4},{6,7},{7,6},{8,9},{9,8},{10,11... | collective-permute-start | bytes 2949128 | tf_op jit(solution)/shard_map/ppermute | solution.py:25
  43.7 19.0 %copy-start.5 = (bf16[1024,768]{1,0:T(8,128)(2,1)S(1)}, bf16[1024,768]{1,0:T(8,128)(2,1)}, u32[]{:S(2)}) copy-start(bf16[1024,768]{1,0:T(8,128)(2,1)} %copy-done.3) | copy-start | bytes 4718596
  43.7 19.0 %copy-start.9 = (bf16[1024,768]{1,0:T(8,128)(2,1)S(1)}, bf16[1024,768]{1,0:T(8,128)(2,1)}, u32[]{:S(2)}) copy-start(bf16[1024,768]{1,0:T(8,128)(2,1)} %refs_4_.3) | copy-start | bytes 4718596
  43.8 19.0 %copy-start.14 = (f32[1024,1]{1,0:T(8,128)S(1)}, f32[1024,1]{1,0:T(8,128)}, u32[]{:S(2)}) copy-start(f32[1024,1]{1,0:T(8,128)} %copy-done.13) | copy-start | bytes 12292
  43.8 27.3 %collective-permute-start.3 = (bf16[384,768]{1,0:T(8,128)(2,1)S(1)}, bf16[384,768]{1,0:T(8,128)(2,1)S(1)}, u32[]{:S(2)}, u32[]{:S(2)}) collective-permute-start(bf16[384,768]{1,0:T(8,128)(2,1)S(1)} %copy-done.21), channel_id=1, source_target_pairs={{0,1},{1,0},{2,3},{3,2},{4,5},{5,4},{6,7},{7,6},{8,9},{9,8},{10,11... | collective-permute-start | bytes 1769480 | tf_op jit(solution)/shard_map/ppermute | solution.py:25
  45.9 32.9 %collective-permute-start.1 = (bf16[256,768]{1,0:T(8,128)(2,1)S(1)}, bf16[256,768]{1,0:T(8,128)(2,1)S(1)}, u32[]{:S(2)}, u32[]{:S(2)}) collective-permute-start(bf16[256,768]{1,0:T(8,128)(2,1)S(1)} %get-tuple-element.32), channel_id=1, source_target_pairs={{1,2},{2,1},{3,4},{4,3},{5,6},{6,5},{7,8},{8,7},{9,10},{10,9},{11,... | collective-permute-start | bytes 1179656 | tf_op jit(solution)/shard_map/ppermute | solution.py:25
  69.4 5.2 %copy-start.7 = (bf16[1024,768]{1,0:T(8,128)(2,1)S(1)}, bf16[1024,768]{1,0:T(8,128)(2,1)}, u32[]{:S(2)}) copy-start(bf16[1024,768]{1,0:T(8,128)(2,1)} %refs_4_.5) | copy-start | bytes 4718596
  69.4 5.2 %copy-start.12 = (f32[1024,1]{1,0:T(8,128)S(1)}, f32[1024,1]{1,0:T(8,128)}, u32[]{:S(2)}) copy-start(f32[1024,1]{1,0:T(8,128)} %copy-done.11) | copy-start | bytes 12292
  (4 other events, 4.1 us)
